TPU v7x, 32 devices: a whole 2x2x4 slice. The times are simulated.
32 devices in a mesh: seq: 8 (over z, x), rep: 4 (over y, core).
Axes of the slice: x: 2, y: 2, z: 4, core: 2. Of those that a mesh axis runs over, the one named last changes fastest.
Arguments:
- tokens: bfloat16 [4, 2048, 768], P('rep', 'seq'), may hold values from -6 to 6
- segments: int32 [4, 2048], P('rep', 'seq'), may hold values from 0 to 7, never falling along the last dimension, each value on 1 to 512 neighbouring positions
- orders: int32 [4, 12, 2048], P('rep'), may hold values from 0 to 2047, as said below
- owners: int32 [4, 12, 16], P('rep'), may hold values from 0 to 7, as said below
- query_weight: bfloat16 [768, 768], replicated, may hold values from -0.21875 to 0.21875
- query_bias: bfloat16 [768], replicated, may hold values from -3 to 3
- key_weight: bfloat16 [768, 768], replicated, may hold values from -0.21875 to 0.21875
- value_weight: bfloat16 [768, 768], replicated, may hold values from -0.21875 to 0.21875
- value_bias: bfloat16 [768], replicated, may hold values from -3 to 3
- out_weight: bfloat16 [768, 768], replicated, may hold values from -0.875 to 0.875
- out_bias: bfloat16 [768], replicated, may hold values from -3 to 3
- first_gain: bfloat16 [768], replicated, may hold values from 0.5 to 1.5
- first_shift: bfloat16 [768], replicated, may hold values from -3 to 3
- inner_weight: bfloat16 [768, 3072], replicated, may hold values from -0.21875 to 0.21875
- inner_bias: bfloat16 [3072], replicated, may hold values from -3 to 3
- outer_weight: bfloat16 [3072, 768], replicated, may hold values from -0.109375 to 0.109375
- outer_bias: bfloat16 [768], replicated, may hold values from -3 to 3
- second_gain: bfloat16 [768], replicated, may hold values from 0.5 to 1.5
- second_shift: bfloat16 [768], replicated, may hold values from -3 to 3
- cotangent: bfloat16 [4, 2048, 768], P('rep', 'seq'), may hold values from -6 to 6
Outputs:
- output: bfloat16 [4, 2048, 768], P('rep', 'seq')
- gradient_tokens: bfloat16 [4, 2048, 768], P('rep', 'seq')
- gradient_query_weight: float32 [768, 768], P('seq')
- gradient_query_bias: float32 [768], P('seq')
- gradient_key_weight: float32 [768, 768], P('seq')
- gradient_value_weight: float32 [768, 768], P('seq')
- gradient_value_bias: float32 [768], P('seq')
- gradient_out_weight: float32 [768, 768], P('seq')
- gradient_out_bias: float32 [768], P('seq')
- gradient_first_gain: float32 [768], P('seq')
- gradient_first_shift: float32 [768], P('seq')
- gradient_inner_weight: float32 [768, 3072], P('seq')
- gradient_inner_bias: float32 [3072], P('seq')
- gradient_outer_weight: float32 [3072, 768], P('seq')
- gradient_outer_bias: float32 [768], P('seq')
- gradient_second_gain: float32 [768], P('seq')
- gradient_second_shift: float32 [768], P('seq')
- cluster_stats: float32 [2, 12, 8], replicated
Inputs may be any that keep to these rules, and one draw needn't show every extreme that they name: `orders`: for each group and head, a permutation of the group's 2048 positions. For every head, the 256 tokens in the clusters that owners gives to one device hold exactly 32 tokens of each device's block of 256 tokens. `owners`: for each group and head, every device owns exactly 2 of the 16 clusters.
All inputs are finite; a program needn't handle non-finite values.
Results may differ from a plain program's by a relative error of at most 0.015.
Values may be sent and summed in bfloat16 or wider, within the bound.
A program may use at most 192 MiB of HBM per device.

v0:
```python
import jax
import jax.numpy as jnp
from jax import lax
from jax.sharding import PartitionSpec as P

EPSILON = 1e-12
NEGATIVE = -1e30


def norm_forward(hidden, gain_vector, shift_vector):
    centre = hidden - jnp.mean(hidden, axis=-1, keepdims=True)
    root_inverse = lax.rsqrt(jnp.mean(centre * centre, axis=-1, keepdims=True) + EPSILON)
    normed = centre * root_inverse
    return (
        normed * gain_vector.astype(jnp.float32) + shift_vector.astype(jnp.float32),
        normed,
        root_inverse,
    )


def norm_backward(upstream, normed, root_inverse, gain_vector):
    scaled = upstream * gain_vector.astype(jnp.float32)
    return root_inverse * (
        scaled
        - jnp.mean(scaled, axis=-1, keepdims=True)
        - normed * jnp.mean(scaled * normed, axis=-1, keepdims=True)
    )


def exact_gelu(inner_sum):
    return jax.nn.gelu(inner_sum, approximate=False)


def rank_matrix(sort_keys):
    row_count = sort_keys.shape[1]
    ranks = jnp.sum((sort_keys[:, None, :] < sort_keys[:, :, None]).astype(jnp.int32), axis=2)
    return (ranks[:, None, :] == jnp.arange(row_count, dtype=jnp.int32)[None, :, None]).astype(
        jnp.bfloat16
    )


def scatter_rows(row_block, placing, seq_count):
    head_count, row_count, features = row_block.shape
    picked = jnp.einsum(
        "hri,hif->hrf", placing, row_block, preferred_element_type=jnp.float32
    ).astype(jnp.bfloat16)
    return picked.reshape(head_count, seq_count, row_count // seq_count * features).transpose(
        1, 0, 2
    )


def collect_rows(packed, placing, features):
    seq_count, head_count, flat_width = packed.shape
    row_block = packed.transpose(1, 0, 2).reshape(
        head_count, seq_count * flat_width // features, features
    )
    return jnp.einsum(
        "hri,hrf->hif", placing, row_block, preferred_element_type=jnp.float32
    ).astype(jnp.bfloat16)


def cluster_scores(queries, keys_in, segment_ids, score_scale):
    scores = (
        jnp.einsum("nqd,nkd->nqk", queries, keys_in, preferred_element_type=jnp.float32)
        * score_scale
    )
    allowed = segment_ids[:, :, None] == segment_ids[:, None, :]
    return (scores, allowed, jnp.where(allowed, scores, NEGATIVE))


def cluster_forward(queries, keys_in, values, segment_ids, score_scale):
    scores, allowed, masked = cluster_scores(queries, keys_in, segment_ids, score_scale)
    highest = jnp.max(masked, axis=-1, keepdims=True)
    raised = jnp.exp(masked - highest)
    totals = jnp.sum(raised, axis=-1, keepdims=True)
    weights = raised / totals
    attended = jnp.einsum(
        "nqk,nkd->nqd", weights.astype(jnp.bfloat16), values, preferred_element_type=jnp.float32
    ).astype(jnp.bfloat16)
    log_total = highest[:, :, 0] + jnp.log(totals[:, :, 0])
    entropy = log_total - jnp.sum(weights * jnp.where(allowed, scores, 0.0), axis=-1)
    occupied = jnp.sum(allowed.astype(jnp.float32), axis=-1)
    return (attended, log_total, entropy, occupied)


def cluster_backward(queries, keys_in, values, segment_ids, log_total, grad_out, score_scale):
    masked = cluster_scores(queries, keys_in, segment_ids, score_scale)[2]
    weights = jnp.exp(masked - log_total[:, :, None])
    weight_grads = jnp.einsum("nqd,nkd->nqk", grad_out, values, preferred_element_type=jnp.float32)
    value_grads = jnp.einsum(
        "nqk,nqd->nkd", weights.astype(jnp.bfloat16), grad_out, preferred_element_type=jnp.float32
    )
    score_grads = (
        weights * (weight_grads - jnp.sum(weights * weight_grads, axis=-1, keepdims=True))
    ).astype(jnp.bfloat16)
    query_grads = (
        jnp.einsum("nqk,nkd->nqd", score_grads, keys_in, preferred_element_type=jnp.float32)
        * score_scale
    )
    key_grads = (
        jnp.einsum("nqk,nqd->nkd", score_grads, queries, preferred_element_type=jnp.float32)
        * score_scale
    )
    return jnp.stack([query_grads, key_grads, value_grads], axis=2).astype(jnp.bfloat16)


def body(
    tokens,
    segments,
    orders,
    owners,
    query_weight,
    query_bias,
    key_weight,
    value_weight,
    value_bias,
    out_weight,
    out_bias,
    first_gain,
    first_shift,
    inner_weight,
    inner_bias,
    outer_weight,
    outer_bias,
    second_gain,
    second_shift,
    cotangent,
):
    seq_count = lax.axis_size("seq")
    groups = lax.axis_size("rep")
    own_index = lax.axis_index("seq")
    row_count = tokens.shape[1]
    model_width = tokens.shape[2]
    order_table = orders[0]
    owner_table = owners[0]
    head_count, group_tokens = order_table.shape
    cluster_count = owner_table.shape[1]
    cluster = group_tokens // cluster_count
    head_dim = model_width // head_count
    per_owner = row_count // cluster
    score_scale = head_dim ** (-0.5)
    flat_tokens = tokens[0]
    local_index = jnp.arange(row_count, dtype=jnp.int32)
    factor = 1
    for candidate in range(1, seq_count + 1):
        if seq_count % candidate == 0 and candidate * row_count <= 2048:
            factor = candidate
    block_count = seq_count // factor
    block_width = factor * row_count
    order_blocks = order_table.reshape(head_count, block_count, block_width).transpose(1, 0, 2)
    owner_blocks = (
        jnp.repeat(owner_table, cluster, axis=1)
        .reshape(head_count, block_count, block_width)
        .transpose(1, 0, 2)
    )

    def find_target(total, block_item):
        order_block, owner_block = block_item
        local = order_block - own_index * row_count
        hits = local[:, :, None] == local_index[None, None, :]
        return (total + jnp.sum(jnp.where(hits, owner_block[:, :, None], 0), axis=1), None)

    target, unused = lax.scan(
        find_target, jnp.zeros((head_count, row_count), jnp.int32), (order_blocks, owner_blocks)
    )
    send_matrix = rank_matrix(target * row_count + local_index[None, :])
    mine = (owner_table == own_index).astype(jnp.int32)
    before = jnp.cumsum(mine, axis=1) - mine
    slot_hot = (mine[:, None, :] == 1) & (
        before[:, None, :] == jnp.arange(per_owner, dtype=jnp.int32)[None, :, None]
    )
    order_grid = order_table.reshape(head_count, cluster_count, cluster)
    owned_tokens = jnp.sum(
        jnp.where(slot_hot[:, :, :, None], order_grid[:, None, :, :], 0), axis=2
    ).reshape(head_count, row_count)
    arrive_matrix = rank_matrix(owned_tokens)
    w_three = jnp.concatenate([query_weight, key_weight, value_weight], axis=1)
    bias_three = jnp.concatenate(
        [
            query_bias.astype(jnp.float32),
            jnp.zeros((model_width,), jnp.float32),
            value_bias.astype(jnp.float32),
        ]
    )
    projected = (
        jnp.dot(flat_tokens, w_three, preferred_element_type=jnp.float32) + bias_three
    ).astype(jnp.bfloat16)
    token_rows = (
        projected.reshape(row_count, 3, head_count, head_dim)
        .transpose(2, 0, 1, 3)
        .reshape(head_count, row_count, 3 * head_dim)
    )
    segment_rows = jnp.broadcast_to(
        segments[0].astype(jnp.bfloat16)[None, :, None], (head_count, row_count, 1)
    )
    send_values = scatter_rows(token_rows, send_matrix, seq_count)
    send_segments = scatter_rows(segment_rows, send_matrix, seq_count)
    arrived, arrived_segments = (
        lax.all_to_all(send_values, "seq", split_axis=0, concat_axis=0, tiled=True),
        lax.all_to_all(send_segments, "seq", split_axis=0, concat_axis=0, tiled=True),
    )
    cluster_rows = collect_rows(arrived, arrive_matrix, 3 * head_dim).reshape(
        head_count * per_owner, cluster, 3, head_dim
    )
    cluster_segments = collect_rows(arrived_segments, arrive_matrix, 1).reshape(
        head_count * per_owner, cluster
    )
    queries = cluster_rows[:, :, 0]
    keys_in = cluster_rows[:, :, 1]
    values = cluster_rows[:, :, 2]
    attended, log_total, entropy, occupied = cluster_forward(
        queries, keys_in, values, cluster_segments, score_scale
    )
    per_head = jnp.stack(
        [
            jnp.sum(entropy.reshape(head_count, -1), axis=1),
            jnp.sum(occupied.reshape(head_count, -1), axis=1) / cluster,
        ]
    ) / (groups * row_count)
    column = (jnp.arange(seq_count, dtype=jnp.int32) == own_index).astype(jnp.float32)
    cluster_stats = lax.psum(per_head[:, :, None] * column, ("seq", "rep"))
    leaving = scatter_rows(
        attended.reshape(head_count, row_count, head_dim), arrive_matrix, seq_count
    )
    returned = lax.all_to_all(leaving, "seq", split_axis=0, concat_axis=0, tiled=True)
    attended_rows = (
        collect_rows(returned, send_matrix, head_dim)
        .transpose(1, 0, 2)
        .reshape(row_count, model_width)
    )
    branch = jnp.dot(
        attended_rows, out_weight, preferred_element_type=jnp.float32
    ) + out_bias.astype(jnp.float32)
    first_out, normed_one, root_one = norm_forward(
        flat_tokens.astype(jnp.float32) + branch, first_gain, first_shift
    )
    first_low = first_out.astype(jnp.bfloat16)
    inner_sum = jnp.dot(
        first_low, inner_weight, preferred_element_type=jnp.float32
    ) + inner_bias.astype(jnp.float32)
    activated, gelu_pull = jax.vjp(exact_gelu, inner_sum)
    activated_low = activated.astype(jnp.bfloat16)
    second = jnp.dot(
        activated_low, outer_weight, preferred_element_type=jnp.float32
    ) + outer_bias.astype(jnp.float32)
    result, normed_two, root_two = norm_forward(first_out + second, second_gain, second_shift)
    output = result.astype(jnp.bfloat16)[None]
    upstream = cotangent[0].astype(jnp.float32)
    gradient_second_gain = jnp.sum(upstream * normed_two, axis=0)
    gradient_second_shift = jnp.sum(upstream, axis=0)
    delta_two = norm_backward(upstream, normed_two, root_two, second_gain)
    delta_second = delta_two.astype(jnp.bfloat16)
    gradient_outer_bias = jnp.sum(delta_second.astype(jnp.float32), axis=0)
    gradient_outer_weight = jnp.einsum(
        "tf,td->fd", activated_low, delta_second, preferred_element_type=jnp.float32
    )
    delta_activated = jnp.einsum(
        "td,fd->tf", delta_second, outer_weight, preferred_element_type=jnp.float32
    )
    delta_inner = gelu_pull(delta_activated)[0].astype(jnp.bfloat16)
    gradient_inner_bias = jnp.sum(delta_inner.astype(jnp.float32), axis=0)
    gradient_inner_weight = jnp.einsum(
        "td,tf->df", first_low, delta_inner, preferred_element_type=jnp.float32
    )
    delta_first = delta_two + jnp.einsum(
        "tf,df->td", delta_inner, inner_weight, preferred_element_type=jnp.float32
    )
    gradient_first_gain = jnp.sum(delta_first * normed_one, axis=0)
    gradient_first_shift = jnp.sum(delta_first, axis=0)
    delta_one = norm_backward(delta_first, normed_one, root_one, first_gain)
    delta_branch = delta_one.astype(jnp.bfloat16)
    gradient_out_bias = jnp.sum(delta_branch.astype(jnp.float32), axis=0)
    gradient_out_weight = jnp.einsum(
        "td,te->de", attended_rows, delta_branch, preferred_element_type=jnp.float32
    )
    delta_attended = jnp.einsum(
        "te,de->td", delta_branch, out_weight, preferred_element_type=jnp.float32
    ).astype(jnp.bfloat16)
    delta_rows = delta_attended.reshape(row_count, head_count, head_dim).transpose(1, 0, 2)
    send_grads = scatter_rows(delta_rows, send_matrix, seq_count)
    grad_arrived = lax.all_to_all(send_grads, "seq", split_axis=0, concat_axis=0, tiled=True)
    kept_queries, kept_keys, kept_values, kept_segments = (
        queries,
        keys_in,
        values,
        cluster_segments,
    )
    grad_cluster = collect_rows(grad_arrived, arrive_matrix, head_dim).reshape(
        head_count * per_owner, cluster, head_dim
    )
    three_grads = cluster_backward(
        kept_queries, kept_keys, kept_values, kept_segments, log_total, grad_cluster, score_scale
    )
    leaving_grads = scatter_rows(
        three_grads.reshape(head_count, row_count, 3 * head_dim), arrive_matrix, seq_count
    )
    returned_grads = lax.all_to_all(leaving_grads, "seq", split_axis=0, concat_axis=0, tiled=True)
    delta_three = (
        collect_rows(returned_grads, send_matrix, 3 * head_dim)
        .reshape(head_count, row_count, 3, head_dim)
        .transpose(1, 2, 0, 3)
        .reshape(row_count, 3 * model_width)
    )
    bias_grads = jnp.sum(delta_three.astype(jnp.float32), axis=0)
    weight_grads = jnp.einsum(
        "td,te->de", flat_tokens, delta_three, preferred_element_type=jnp.float32
    )
    gradient_tokens = (
        delta_one
        + jnp.einsum("te,de->td", delta_three, w_three, preferred_element_type=jnp.float32)
    ).astype(jnp.bfloat16)[None]
    gradient_query_weight = weight_grads[:, :model_width]
    gradient_key_weight = weight_grads[:, model_width : 2 * model_width]
    gradient_value_weight = weight_grads[:, 2 * model_width :]
    gradient_query_bias = bias_grads[:model_width]
    gradient_value_bias = bias_grads[2 * model_width :]
    pieces = (
        lax.psum_scatter(gradient_query_weight, "seq", scatter_dimension=0, tiled=True),
        lax.psum_scatter(gradient_query_bias, "seq", scatter_dimension=0, tiled=True),
        lax.psum_scatter(gradient_key_weight, "seq", scatter_dimension=0, tiled=True),
        lax.psum_scatter(gradient_value_weight, "seq", scatter_dimension=0, tiled=True),
        lax.psum_scatter(gradient_value_bias, "seq", scatter_dimension=0, tiled=True),
        lax.psum_scatter(gradient_out_weight, "seq", scatter_dimension=0, tiled=True),
        lax.psum_scatter(gradient_out_bias, "seq", scatter_dimension=0, tiled=True),
        lax.psum_scatter(gradient_first_gain, "seq", scatter_dimension=0, tiled=True),
        lax.psum_scatter(gradient_first_shift, "seq", scatter_dimension=0, tiled=True),
        lax.psum_scatter(gradient_inner_weight, "seq", scatter_dimension=0, tiled=True),
        lax.psum_scatter(gradient_inner_bias, "seq", scatter_dimension=0, tiled=True),
        lax.psum_scatter(gradient_outer_weight, "seq", scatter_dimension=0, tiled=True),
        lax.psum_scatter(gradient_outer_bias, "seq", scatter_dimension=0, tiled=True),
        lax.psum_scatter(gradient_second_gain, "seq", scatter_dimension=0, tiled=True),
        lax.psum_scatter(gradient_second_shift, "seq", scatter_dimension=0, tiled=True),
    )
    summed = (
        lax.psum(pieces[0].astype(jnp.bfloat16), "rep").astype(jnp.float32),
        lax.psum(pieces[1].astype(jnp.bfloat16), "rep").astype(jnp.float32),
        lax.psum(pieces[2].astype(jnp.bfloat16), "rep").astype(jnp.float32),
        lax.psum(pieces[3].astype(jnp.bfloat16), "rep").astype(jnp.float32),
        lax.psum(pieces[4].astype(jnp.bfloat16), "rep").astype(jnp.float32),
        lax.psum(pieces[5].astype(jnp.bfloat16), "rep").astype(jnp.float32),
        lax.psum(pieces[6].astype(jnp.bfloat16), "rep").astype(jnp.float32),
        lax.psum(pieces[7].astype(jnp.bfloat16), "rep").astype(jnp.float32),
        lax.psum(pieces[8].astype(jnp.bfloat16), "rep").astype(jnp.float32),
        lax.psum(pieces[9].astype(jnp.bfloat16), "rep").astype(jnp.float32),
        lax.psum(pieces[10].astype(jnp.bfloat16), "rep").astype(jnp.float32),
        lax.psum(pieces[11].astype(jnp.bfloat16), "rep").astype(jnp.float32),
        lax.psum(pieces[12].astype(jnp.bfloat16), "rep").astype(jnp.float32),
        lax.psum(pieces[13].astype(jnp.bfloat16), "rep").astype(jnp.float32),
        lax.psum(pieces[14].astype(jnp.bfloat16), "rep").astype(jnp.float32),
    )
    return (output, gradient_tokens) + tuple(summed) + (cluster_stats,)


def solution(mesh):
    placed = (
        P("rep", "seq", None),
        P("rep", "seq"),
        P("rep", None, None),
        P("rep", None, None),
        P(),
        P(),
        P(),
        P(),
        P(),
        P(),
        P(),
        P(),
        P(),
        P(),
        P(),
        P(),
        P(),
        P(),
        P(),
        P("rep", "seq", None),
    )
    return jax.shard_map(
        body,
        mesh=mesh,
        in_specs=placed,
        out_specs=(
            P("rep", "seq", None),
            P("rep", "seq", None),
            P("seq", None),
            P("seq"),
            P("seq", None),
            P("seq", None),
            P("seq"),
            P("seq", None),
            P("seq"),
            P("seq"),
            P("seq"),
            P("seq", None),
            P("seq"),
            P("seq", None),
            P("seq"),
            P("seq"),
            P("seq"),
            P(),
        ),
        check_vma=False,
    )
```

profile of v0, /device:TPU:0, one launch (start us, length us, event | category | flops | bytes accessed | tf_op | source)
XLA Modules:
  0.0 915.4 jit_solution(11495916552296931971)
XLA Ops:
  9.9 9.5 %select_reduce_fusion = s32[12,256]{1,0:T(8,128)S(1)} fusion(s32[12,2048]{1,0:T(8,128)S(1)} %bitcast.169, s32[12,2048]{1,0:T(8,128)S(1)} %bitcast.167), kind=kLoop, calls=%fused_computation | loop fusion | flops 18871296 | bytes 208896 | tf_op jit(solution)/shard_map/while/body/eval_jaxpr/reduce_sum | solution.py:161
  21.9 7.3 all-to-all-start
  40.1 3.2 copy.156
  43.3 6.3 all-to-all-start.1
  51.9 34.1 %all-to-all-done.1 = bf16[8,12,6144]{2,1,0:T(8,128)(2,1)S(1)} async-done(((bf16[8,12,6144]{2,1,0:T(8,128)(2,1)}), bf16[8,12,6144]{2,1,0:T(8,128)(2,1)S(1)}, u32[]{:S(2)}, u32[]{:S(2)}) %all-to-all-start.1) | async-done | bytes 1179680 | tf_op jit(solution)/shard_map/all_to_all | solution.py:199
  87.7 3.0 reshape.279
  100.9 4.2 all-to-all-start.2
  108.1 11.6 %all-to-all-done.2 = bf16[8,12,2048]{2,1,0:T(8,128)(2,1)S(1)} async-done(((bf16[8,12,2048]{2,1,0:T(8,128)(2,1)}), bf16[8,12,2048]{2,1,0:T(8,128)(2,1)S(1)}, u32[]{:S(2)}, u32[]{:S(2)}) %all-to-all-start.2) | async-done | bytes 393248 | tf_op jit(solution)/shard_map/all_to_all | solution.py:225
  123.2 10.0 %multiply_convert_fusion = (bf16[256,3072]{1,0:T(8,128)(2,1)S(1)}, f32[256,3072]{1,0:T(8,128)S(1)}, f32[256,3072]{1,0:T(8,128)S(1)}) fusion(f32[3072]{0:T(1024)S(1)} %copy-done.52, bf16[768,3072]{1,0:T(8,128)(2,1)} %param.33, f32[256,768]{1,0:T(8,128)S(1)} %get-tuple-element.180, f32[768]{0:T(1024)S(1)} %convert_element_type.287, ...), kind=kOutput, calls=%fused_computation.10 | convolution fusion | flops 1260847104 | bytes 13389824 | tf_op jit(solution)/shard_map/dot_general | solution.py:238
  137.8 2.8 convert_reduce_fusion
  153.1 3.6 all-to-all-start.3
  160.3 11.1 %all-to-all-done.3 = bf16[8,12,2048]{2,1,0:T(8,128)(2,1)S(1)} async-done(((bf16[8,12,2048]{2,1,0:T(8,128)(2,1)}), bf16[8,12,2048]{2,1,0:T(8,128)(2,1)S(1)}, u32[]{:S(2)}, u32[]{:S(2)}) %all-to-all-start.3) | async-done | bytes 393248 | tf_op jit(solution)/shard_map/all_to_all | solution.py:281
  176.4 3.6 fusion.18
  184.6 3.2 convert_element_type.305
  191.8 3.0 reshape.289
  195.5 50.3 %all_to_all.25 = bf16[8,12,6144]{2,1,0:T(8,128)(2,1)S(1)} all-to-all(bf16[8,12,6144]{2,1,0:T(8,128)(2,1)S(1)} %copy.184), channel_id=1, replica_groups=mesh['seq'=8,'rep'=4] {'seq'}, dimensions={0} | all-to-all | bytes 2359296 | tf_op jit(solution)/shard_map/all_to_all | solution.py:297
  246.5 2.8 reshape.290
  253.8 3.0 fusion.95
  256.7 3.1 copy.207
  259.9 3.1 copy.205
  263.1 3.1 copy.203
  266.3 6.6 fusion.90
  274.0 6.5 fusion.81
  285.4 42.7 %reduce-scatter.23.cloned.1.call-done = f32[96,768]{1,0:T(8,128)} async-done(((f32[768,768]{1,0:T(8,128)}), f32[96,768]{1,0:T(8,128)}) %reduce-scatter.23.cloned.1.call-update) | async-done | bytes 294928
  329.9 69.7 %reduce-scatter.21.cloned.1.call-done = f32[96,768]{1,0:T(8,128)} async-done(((f32[768,768]{1,0:T(8,128)}), f32[96,768]{1,0:T(8,128)}) %reduce-scatter.21.cloned.1.call-update) | async-done | bytes 294928
  401.4 69.7 %reduce-scatter.19.cloned.1.call-done = f32[96,768]{1,0:T(8,128)} async-done(((f32[768,768]{1,0:T(8,128)}), f32[96,768]{1,0:T(8,128)}) %reduce-scatter.19.cloned.1.call-update) | async-done | bytes 294928
  472.9 164.0 %reduce-scatter.15.cloned.1.call-done = f32[96,3072]{1,0:T(8,128)} async-done(((f32[768,3072]{1,0:T(8,128)}), f32[96,3072]{1,0:T(8,128)}) %reduce-scatter.15.cloned.1.call-update) | async-done | bytes 1179664 | tf_op jit(solution)/shard_map/reduce_scatter | solution.py:327
  639.0 163.7 %reduce-scatter.17.cloned.1.call-done = f32[384,768]{1,0:T(8,128)} async-done(((f32[3072,768]{1,0:T(8,128)}), f32[384,768]{1,0:T(8,128)}) %reduce-scatter.17.cloned.1.call-update) | async-done | bytes 1179664 | tf_op jit(solution)/shard_map/reduce_scatter | solution.py:329
  805.0 39.9 %psum.127 = f32[2,12,8]{1,2,0:T(8,128)} all-reduce(f32[2,12,8]{1,2,0:T(8,128)S(1)} %broadcast_multiply_fusion), channel_id=1, replica_groups=mesh['seq'=8,'rep'=4] {'seq','rep'}, use_global_device_ids=true, to_apply=%region_59.60 | all-reduce | flops 192 | bytes 1536 | tf_op jit(solution)/shard_map/psum | solution.py:221
  845.5 37.3 %all-reduce.9 = (bf16[768]{0:T(1024)(128)(2,1)S(1)}, bf16[768]{0:T(1024)(128)(2,1)S(1)}, bf16[768]{0:T(1024)(128)(2,1)S(1)}, bf16[768]{0:T(1024)(128)(2,1)S(1)},...) all-reduce(f32[768]{0:T(1024)S(1)} %slice.35, ...), channel_id=3, replica_groups=mesh['seq'=8,'rep'=4] {'seq'}, use_global_device_ids=true, to_apply=%region_19.20.clone | all-reduce | flops 9216 | bytes 55296
  883.4 5.7 all-reduce.10
  893.9 4.0 fusion.48
  (309 shorter events, 106.7 us)
Async XLA Ops:
  7.2 114.3 %copy-start = (bf16[768,768]{1,0:T(8,128)(2,1)S(1)}, bf16[768,768]{1,0:T(8,128)(2,1)}, u32[]{:S(2)}) copy-start(bf16[768,768]{1,0:T(8,128)(2,1)} %param.29) | copy-start | bytes 3538948
  7.2 23.4 %copy-start.21 = (bf16[768,768]{1,0:T(8,128)(2,1)S(1)}, bf16[768,768]{1,0:T(8,128)(2,1)}, u32[]{:S(2)}) copy-start(bf16[768,768]{1,0:T(8,128)(2,1)} %param.24) | copy-start | bytes 3538948
  20.5 13.6 %copy-start.44 = (s32[12,256]{1,0:T(8,128)}, s32[12,256]{1,0:T(8,128)S(1)}, u32[]{:S(2)}) copy-start(s32[12,256]{1,0:T(8,128)S(1)} %convert_reduce_fusion.2) | copy-start | bytes 36868
  21.9 21.4 %all-to-all-start = ((bf16[8,2,192]{2,1,0:T(2,128)(2,1)}), bf16[8,2,192]{2,1,0:T(2,128)(2,1)S(1)}, u32[]{:S(2)}, u32[]{:S(2)}) async-start(bf16[8,2,192]{2,1,0:T(2,128)(2,1)} %reshape.315), calls=%async_computation | async-start | bytes 16384 | tf_op jit(solution)/shard_map/all_to_all | solution.py:200
  43.3 42.7 %all-to-all-start.1 = ((bf16[8,12,6144]{2,1,0:T(8,128)(2,1)}), bf16[8,12,6144]{2,1,0:T(8,128)(2,1)S(1)}, u32[]{:S(2)}, u32[]{:S(2)}) async-start(bf16[8,12,6144]{2,1,0:T(8,128)(2,1)} %copy.156), calls=%async_computation.1 | async-start | bytes 3145728 | tf_op jit(solution)/shard_map/all_to_all | solution.py:199
  51.1 39.6 %copy-start.46 = (s32[12,256]{1,0:T(8,128)}, s32[12,256]{1,0:T(8,128)S(1)}, u32[]{:S(2)}) copy-start(s32[12,256]{1,0:T(8,128)S(1)} %convert_reduce_fusion.1) | copy-start | bytes 36868
  98.8 21.9 %copy-start.45 = (s32[12,256]{1,0:T(8,128)S(1)}, s32[12,256]{1,0:T(8,128)}, u32[]{:S(2)}) copy-start(s32[12,256]{1,0:T(8,128)} %copy-done.44) | copy-start | bytes 36868
  99.8 21.7 %copy-start.13 = (bf16[1,256,768]{2,1,0:T(8,128)(2,1)S(1)}, bf16[1,256,768]{2,1,0:T(8,128)(2,1)}, u32[]{:S(2)}) copy-start(bf16[1,256,768]{2,1,0:T(8,128)(2,1)} %param.20) | copy-start | bytes 1179652
  100.9 18.8 %all-to-all-start.2 = ((bf16[8,12,2048]{2,1,0:T(8,128)(2,1)}), bf16[8,12,2048]{2,1,0:T(8,128)(2,1)S(1)}, u32[]{:S(2)}, u32[]{:S(2)}) async-start(bf16[8,12,2048]{2,1,0:T(8,128)(2,1)} %copy.167), calls=%async_computation.2 | async-start | bytes 1048576 | tf_op jit(solution)/shard_map/all_to_all | solution.py:225
  123.0 19.9 %copy-start.38 = (f32[256]{0:T(256)}, f32[256]{0:T(256)S(1)}, u32[]{:S(2)}) copy-start(f32[256]{0:T(256)S(1)} %broadcast_multiply_fusion.6) | copy-start | bytes 3076
  123.2 19.6 %copy-start.49 = (f32[256]{0:T(256)}, f32[256]{0:T(256)S(1)}, u32[]{:S(2)}) copy-start(f32[256]{0:T(256)S(1)} %add_rsqrt_fusion.1) | copy-start | bytes 3076
  153.1 18.3 %all-to-all-start.3 = ((bf16[8,12,2048]{2,1,0:T(8,128)(2,1)}), bf16[8,12,2048]{2,1,0:T(8,128)(2,1)S(1)}, u32[]{:S(2)}, u32[]{:S(2)}) async-start(bf16[8,12,2048]{2,1,0:T(8,128)(2,1)} %copy.172), calls=%async_computation.3 | async-start | bytes 1048576 | tf_op jit(solution)/shard_map/all_to_all | solution.py:281
  156.8 127.0 %reduce-scatter.13.cloned.1.call-start = ((), (), s32[]{:S(2)}) async-start(), calls=%async_computation.11 | async-start | bytes 2654208 | tf_op jit(solution)/shard_map/reduce_scatter | solution.py:323
  160.0 13.3 %copy-start.48 = (s32[12,256]{1,0:T(8,128)S(1)}, s32[12,256]{1,0:T(8,128)}, u32[]{:S(2)}) copy-start(s32[12,256]{1,0:T(8,128)} %copy-done.46) | copy-start | bytes 36868
  160.0 16.3 %copy-start.29 = (f32[24,128]{1,0:T(8,128)S(1)}, f32[24,128]{1,0:T(8,128)}, u32[]{:S(2)}) copy-start(f32[24,128]{1,0:T(8,128)} %log_add_fusion) | copy-start | bytes 36868
  160.1 16.3 %copy-start.34 = (f32[24,128]{1,0:T(8,128)S(1)}, f32[24,128]{1,0:T(8,128)}, u32[]{:S(2)}) copy-start(f32[24,128]{1,0:T(8,128)} %copy-done.33) | copy-start | bytes 36868
  160.1 16.3 %copy-start.36 = (f32[24,128]{1,0:T(8,128)S(1)}, f32[24,128]{1,0:T(8,128)}, u32[]{:S(2)}) copy-start(f32[24,128]{1,0:T(8,128)} %copy-done.35) | copy-start | bytes 36868
  160.1 168.1 %reduce-scatter.23.cloned.1.call-start = ((), (), s32[]{:S(2)}) async-start(), calls=%async_computation.16 | async-start | bytes 2654208
  259.9 139.8 %reduce-scatter.21.cloned.1.call-start = ((), (), s32[]{:S(2)}) async-start(), calls=%async_computation.15 | async-start | bytes 2654208
  263.0 208.1 %reduce-scatter.19.cloned.1.call-start = ((), (), s32[]{:S(2)}) async-start(), calls=%async_computation.14 | async-start | bytes 2654208
  266.2 370.7 %reduce-scatter.15.cloned.1.call-start = ((), (), s32[]{:S(2)}) async-start(), calls=%async_computation.12 | async-start | bytes 10616832 | tf_op jit(solution)/shard_map/reduce_scatter | solution.py:327
  272.9 529.9 %reduce-scatter.17.cloned.1.call-start = ((), (), s32[]{:S(2)}) async-start(), calls=%async_computation.13 | async-start | bytes 10616832 | tf_op jit(solution)/shard_map/reduce_scatter | solution.py:329
  280.6 617.3 %all-reduce.14.cloned.1.call-start = ((), (), s32[]{:S(2)}) async-start(), calls=%async_computation.17 | async-start | bytes 3833856 | tf_op jit(solution)/shard_map/psum | solution.py:335
  329.9 515.0 %copy-start.7 = (bf16[12,256,192]{1,2,0:T(8,128)(2,1)S(1)}, bf16[12,256,192]{1,2,0:T(8,128)(2,1)}, u32[]{:S(2)}) copy-start(bf16[12,256,192]{1,2,0:T(8,128)(2,1)} %copy-done.6) | copy-start | bytes 3538948
  472.9 372.6 %copy-start.41 = (f32[768]{0:T(1024)S(1)}, f32[768]{0:T(1024)}, u32[]{:S(2)}) copy-start(f32[768]{0:T(1024)} %get-tuple-element.130) | copy-start | bytes 9220
  472.9 372.6 %copy-start.42 = (f32[768]{0:T(1024)S(1)}, f32[768]{0:T(1024)}, u32[]{:S(2)}) copy-start(f32[768]{0:T(1024)} %get-tuple-element.160) | copy-start | bytes 9220
  472.9 372.6 %copy-start.43 = (f32[768]{0:T(1024)S(1)}, f32[768]{0:T(1024)}, u32[]{:S(2)}) copy-start(f32[768]{0:T(1024)} %get-tuple-element.162) | copy-start | bytes 9220
  472.9 372.6 %copy-start.53 = (f32[3072]{0:T(1024)S(1)}, f32[3072]{0:T(1024)}, u32[]{:S(2)}) copy-start(f32[3072]{0:T(1024)} %get-tuple-element.186) | copy-start | bytes 36868
  472.9 372.6 %copy-start.56 = (f32[768]{0:T(1024)S(1)}, f32[768]{0:T(1024)}, u32[]{:S(2)}) copy-start(f32[768]{0:T(1024)} %get-tuple-element.128) | copy-start | bytes 9220
  472.9 372.6 %copy-start.57 = (f32[768]{0:T(1024)S(1)}, f32[768]{0:T(1024)}, u32[]{:S(2)}) copy-start(f32[768]{0:T(1024)} %get-tuple-element.133) | copy-start | bytes 9220
  472.9 421.0 %copy-start.3 = (bf16[12,256,3,64]{1,3,0,2:T(8,128)(2,1)S(1)}, bf16[12,256,3,64]{1,3,0,2:T(8,128)(2,1)}, u32[]{:S(2)}) copy-start(bf16[12,256,3,64]{1,3,0,2:T(8,128)(2,1)} %copy-done.2) | copy-start | bytes 3538948
  893.9 14.3 %copy-start.1 = (bf16[768,768]{1,0:T(8,128)(2,1)S(1)}, bf16[768,768]{1,0:T(8,128)(2,1)}, u32[]{:S(2)}) copy-start(bf16[768,768]{1,0:T(8,128)(2,1)} %param.29) | copy-start | bytes 3538948
  (49 other events, 210.1 us)
Sparse Core Ops, SparseCore 0:
  161.1 82.6 reduce-scatter.12
  260.0 68.0 reduce-scatter.22
  331.6 67.9 reduce-scatter.20
  403.0 68.0 reduce-scatter.18
  474.5 162.3 reduce-scatter.14
  640.3 162.3 reduce-scatter.16
  806.1 49.5 all-reduce.13
where the time goes:
time: 922 us; the launch traced here: 915 us
  waiting for transfers between devices  567 us (61%)
  blocking collectives  133 us (14%)
  local copies, waits for them, and re-layouts  73.1 us (8%)
  matrix products  61.9 us (7%)
  other arithmetic  41.4 us (4%)
  starting transfers between devices  21.9 us (2%)
  between operations  17.1 us (2%)
    unnamed x10, waiting for transfers between devices  182 us
    reduce_scatter x1, waiting for transfers between devices, body(): lax.psum_scatter(gradient_inner_weight, 'seq', scatter_dimension=0, tiled...  164 us
    reduce_scatter x1, waiting for transfers between devices, body(): lax.psum_scatter(gradient_outer_weight, 'seq', scatter_dimension=0, tiled...  164 us
    all_to_all x1, blocking collectives, body(): lax.all_to_all(leaving_grads, 'seq', split_axis=0, concat_axis=0, tiled=T...  50.3 us
    psum x1, blocking collectives, body(): cluster_stats = lax.psum(per_head[:, :, None] * column, ('seq', 'rep'))  39.9 us
    unnamed x1, blocking collectives  37.3 us
    all_to_all x1, waiting for transfers between devices, body(): lax.all_to_all(send_values, 'seq', split_axis=0, concat_axis=0, tiled=True)  34.1 us
    unnamed x169, local copies, waits for them, and re-layouts  27.2 us
  transfers between devices with their start and end apart: 11, of which 8 were waited for; matrix products, arithmetic and copies ran while one was open for 11% of the time, Pallas kernels for 0%

commit v1 on v0

--- a/solution.py
+++ b/solution.py
@@ -1,6 +1,10 @@
+import functools
+
 import jax
 import jax.numpy as jnp
 from jax import lax
+from jax.experimental import pallas as pl
+from jax.experimental.pallas import tpu as pltpu
 from jax.sharding import PartitionSpec as P
 
 EPSILON = 1e-12
@@ -102,6 +106,152 @@
         * score_scale
     )
     return jnp.stack([query_grads, key_grads, value_grads], axis=2).astype(jnp.bfloat16)
+
+
+MESH = pl.DeviceIdType.MESH
+
+
+def reduce_kernel(
+    parts, g_ref, f_ref, core_in, a_one, b_one, ab_two, z_one, z_two, gathered, send_sem, recv_sem
+):
+    s, r = lax.axis_index("seq"), lax.axis_index("rep")
+    zh, zl, x = s // 4, (s // 2) % 2, s % 2
+    y, c = r // 2, r % 2
+    q = g_ref.shape[3] // 8
+    width = g_ref.shape[4] // parts
+    over_x, over_zl, over_zh = (s + 1 - 2 * x, r), (s + 2 - 4 * zl, r), (s + 4 - 8 * zh, r)
+    over_y, over_c = (s, r + 2 - 4 * y), (s, r + 1 - 2 * c)
+    peers = (over_c, over_x, over_y, over_zl, over_zh)
+
+    barrier = pltpu.get_barrier_semaphore()
+    for peer in peers:
+        pl.semaphore_signal(barrier, inc=1, device_id=peer, device_id_type=MESH)
+    pl.semaphore_wait(barrier, len(peers))
+
+    def rows(start, size):
+        return pl.ds(pl.multiple_of(start * q, 16), size * q)
+
+    def send(step, k, src, dst, peer):
+        copy = pltpu.make_async_remote_copy(
+            src_ref=src,
+            dst_ref=dst,
+            send_sem=send_sem.at[step, k],
+            recv_sem=recv_sem.at[step, k],
+            device_id=peer,
+            device_id_type=MESH,
+        )
+        copy.start()
+        return copy
+
+    def add(count, target, other):
+        def one(i, carry):
+            target(i)[...] = (
+                target(i)[...].astype(jnp.float32) + other(i)[...].astype(jnp.float32)
+            ).astype(jnp.bfloat16)
+            return carry
+
+        lax.fori_loop(0, count, one, 0)
+
+    columns = [pl.ds(k * width, width) for k in range(parts)]
+    zero = [
+        send(0, k, g_ref.at[:, :, :, rows(4 * (1 - c), 4), cols], core_in.at[:, :, :, :, cols], over_c)
+        for k, cols in enumerate(columns)
+    ]
+    first, second, third, fourth, fifth, sixth = [], [], [], [], [], []
+    for k, cols in enumerate(columns):
+        zero[k].wait()
+        add(
+            8,
+            lambda i: core_in.at[i // 4, (i // 2) % 2, i % 2, :, cols],
+            lambda i: g_ref.at[i // 4, (i // 2) % 2, i % 2, rows(4 * c, 4), cols],
+        )
+        first.append(
+            (
+                send(1, k, core_in.at[:, :, 1 - x, pl.ds(0, 2 * q), cols], a_one.at[:, :, :, cols], over_x),
+                send(2, k, core_in.at[:, :, :, rows(3 - y, 1), cols], b_one.at[:, :, :, :, cols], over_y),
+            )
+        )
+    for k, cols in enumerate(columns):
+        first[k][0].wait()
+        add(
+            4,
+            lambda i: a_one.at[i // 2, i % 2, :, cols],
+            lambda i: core_in.at[i // 2, i % 2, x, pl.ds(0, 2 * q), cols],
+        )
+        copy_a = send(3, k, a_one.at[:, :, rows(1 - y, 1), cols], ab_two.at[0, :, :, :, cols], over_y)
+        first[k][1].wait()
+        add(
+            8,
+            lambda i: b_one.at[i // 4, (i // 2) % 2, i % 2, :, cols],
+            lambda i: core_in.at[i // 4, (i // 2) % 2, i % 2, rows(2 + y, 1), cols],
+        )
+        copy_b = send(4, k, b_one.at[:, :, 1 - x, :, cols], ab_two.at[1, :, :, :, cols], over_x)
+        second.append((copy_a, copy_b))
+    for k, cols in enumerate(columns):
+        second[k][0].wait()
+        add(
+            4,
+            lambda i: ab_two.at[0, i // 2, i % 2, :, cols],
+            lambda i: a_one.at[i // 2, i % 2, rows(y, 1), cols],
+        )
+        second[k][1].wait()
+        add(
+            4,
+            lambda i: ab_two.at[1, i // 2, i % 2, :, cols],
+            lambda i: b_one.at[i // 2, i % 2, x, :, cols],
+        )
+        third.append(send(5, k, ab_two.at[:, :, 1 - zl, :, cols], z_one.at[:, :, :, cols], over_zl))
+    for k, cols in enumerate(columns):
+        third[k].wait()
+        add(
+            4,
+            lambda i: z_one.at[i // 2, i % 2, :, cols],
+            lambda i: ab_two.at[i // 2, i % 2, zl, :, cols],
+        )
+        fourth.append(send(6, k, z_one.at[:, 1 - zh, :, cols], z_two.at[:, :, cols], over_zh))
+    for k, cols in enumerate(columns):
+        fourth[k].wait()
+        for part in range(2):
+            gathered[c, part, y, :, cols] = (
+                z_two[part, :, cols].astype(jnp.float32) + z_one[part, zh, :, cols].astype(jnp.float32)
+            ).astype(jnp.bfloat16)
+        own = gathered.at[c, :, y, :, cols]
+        fifth.append(send(7, k, own, own, over_y))
+    for k, cols in enumerate(columns):
+        fifth[k].wait()
+        both = gathered.at[c, :, :, :, cols]
+        sixth.append(send(8, k, both, both, over_c))
+    for copy in sixth:
+        copy.wait()
+    f_ref[...] = gathered[...]
+
+
+def reduce_rows(grads, parts, collective_id):
+    seq_count, row_count, width = grads.shape
+    q = row_count // 8
+    low = jnp.bfloat16
+    out = pl.pallas_call(
+        functools.partial(reduce_kernel, parts),
+        out_shape=jax.ShapeDtypeStruct((2, 2, 2, q, width), low),
+        in_specs=[pl.BlockSpec(memory_space=pltpu.VMEM)],
+        out_specs=pl.BlockSpec(memory_space=pltpu.VMEM),
+        scratch_shapes=[
+            pltpu.VMEM((2, 2, 2, 4 * q, width), low),
+            pltpu.VMEM((2, 2, 2 * q, width), low),
+            pltpu.VMEM((2, 2, 2, q, width), low),
+            pltpu.VMEM((2, 2, 2, q, width), low),
+            pltpu.VMEM((2, 2, q, width), low),
+            pltpu.VMEM((2, q, width), low),
+            pltpu.VMEM((2, 2, 2, q, width), low),
+            pltpu.SemaphoreType.DMA((9, parts)),
+            pltpu.SemaphoreType.DMA((9, parts)),
+        ],
+        compiler_params=pltpu.CompilerParams(
+            collective_id=collective_id, has_side_effects=True, vmem_limit_bytes=56 << 20
+        ),
+        name="reduce_rows",
+    )(grads.reshape(2, 2, 2, row_count, width))
+    return out.reshape(row_count, width)
 
 
 def body(
@@ -351,7 +501,288 @@
     return (output, gradient_tokens) + tuple(summed) + (cluster_stats,)
 
 
+def square_body(
+    tokens,
+    segments,
+    orders,
+    owners,
+    query_weight,
+    query_bias,
+    key_weight,
+    value_weight,
+    value_bias,
+    out_weight,
+    out_bias,
+    first_gain,
+    first_shift,
+    inner_weight,
+    inner_bias,
+    outer_weight,
+    outer_bias,
+    second_gain,
+    second_shift,
+    cotangent,
+):
+    seq_count = lax.axis_size("seq")
+    groups = lax.axis_size("rep")
+    own_index = lax.axis_index("seq")
+    row_count = tokens.shape[1]
+    model_width = tokens.shape[2]
+    order_table = orders[0]
+    owner_table = owners[0]
+    head_count, group_tokens = order_table.shape
+    cluster_count = owner_table.shape[1]
+    cluster = group_tokens // cluster_count
+    head_dim = model_width // head_count
+    per_owner = row_count // cluster
+    score_scale = head_dim ** (-0.5)
+    flat_tokens = tokens[0]
+    local_index = jnp.arange(row_count, dtype=jnp.int32)
+    factor = 1
+    for candidate in range(1, seq_count + 1):
+        if seq_count % candidate == 0 and candidate * row_count <= 2048:
+            factor = candidate
+    block_count = seq_count // factor
+    block_width = factor * row_count
+    order_blocks = order_table.reshape(head_count, block_count, block_width).transpose(1, 0, 2)
+    owner_blocks = (
+        jnp.repeat(owner_table, cluster, axis=1)
+        .reshape(head_count, block_count, block_width)
+        .transpose(1, 0, 2)
+    )
+
+    def find_target(total, block_item):
+        order_block, owner_block = block_item
+        local = order_block - own_index * row_count
+        hits = local[:, :, None] == local_index[None, None, :]
+        return (total + jnp.sum(jnp.where(hits, owner_block[:, :, None], 0), axis=1), None)
+
+    target, unused = lax.scan(
+        find_target, jnp.zeros((head_count, row_count), jnp.int32), (order_blocks, owner_blocks)
+    )
+    send_matrix = rank_matrix(target * row_count + local_index[None, :])
+    mine = (owner_table == own_index).astype(jnp.int32)
+    before = jnp.cumsum(mine, axis=1) - mine
+    slot_hot = (mine[:, None, :] == 1) & (
+        before[:, None, :] == jnp.arange(per_owner, dtype=jnp.int32)[None, :, None]
+    )
+    order_grid = order_table.reshape(head_count, cluster_count, cluster)
+    owned_tokens = jnp.sum(
+        jnp.where(slot_hot[:, :, :, None], order_grid[:, None, :, :], 0), axis=2
+    ).reshape(head_count, row_count)
+    arrive_matrix = rank_matrix(owned_tokens)
+    w_three = jnp.concatenate([query_weight, key_weight, value_weight], axis=1)
+    bias_three = jnp.concatenate(
+        [
+            query_bias.astype(jnp.float32),
+            jnp.zeros((model_width,), jnp.float32),
+            value_bias.astype(jnp.float32),
+        ]
+    )
+    projected = (
+        jnp.dot(flat_tokens, w_three, preferred_element_type=jnp.float32) + bias_three
+    ).astype(jnp.bfloat16)
+    token_rows = (
+        projected.reshape(row_count, 3, head_count, head_dim)
+        .transpose(2, 0, 1, 3)
+        .reshape(head_count, row_count, 3 * head_dim)
+    )
+    segment_rows = jnp.broadcast_to(
+        segments[0].astype(jnp.bfloat16)[None, :, None], (head_count, row_count, 1)
+    )
+    send_values = scatter_rows(token_rows, send_matrix, seq_count)
+    send_segments = scatter_rows(segment_rows, send_matrix, seq_count)
+    arrived, arrived_segments = (
+        lax.all_to_all(send_values, "seq", split_axis=0, concat_axis=0, tiled=True),
+        lax.all_to_all(send_segments, "seq", split_axis=0, concat_axis=0, tiled=True),
+    )
+    cluster_rows = collect_rows(arrived, arrive_matrix, 3 * head_dim).reshape(
+        head_count * per_owner, cluster, 3, head_dim
+    )
+    cluster_segments = collect_rows(arrived_segments, arrive_matrix, 1).reshape(
+        head_count * per_owner, cluster
+    )
+    queries = cluster_rows[:, :, 0]
+    keys_in = cluster_rows[:, :, 1]
+    values = cluster_rows[:, :, 2]
+    attended, log_total, entropy, occupied = cluster_forward(
+        queries, keys_in, values, cluster_segments, score_scale
+    )
+    per_head = jnp.stack(
+        [
+            jnp.sum(entropy.reshape(head_count, -1), axis=1),
+            jnp.sum(occupied.reshape(head_count, -1), axis=1) / cluster,
+        ]
+    ) / (groups * row_count)
+    column = (jnp.arange(seq_count, dtype=jnp.int32) == own_index).astype(jnp.float32)
+    cluster_stats = lax.psum(per_head[:, :, None] * column, ("seq", "rep"))
+    leaving = scatter_rows(
+        attended.reshape(head_count, row_count, head_dim), arrive_matrix, seq_count
+    )
+    returned = lax.all_to_all(leaving, "seq", split_axis=0, concat_axis=0, tiled=True)
+    attended_rows = (
+        collect_rows(returned, send_matrix, head_dim)
+        .transpose(1, 0, 2)
+        .reshape(row_count, model_width)
+    )
+    branch = jnp.dot(
+        attended_rows, out_weight, preferred_element_type=jnp.float32
+    ) + out_bias.astype(jnp.float32)
+    first_out, normed_one, root_one = norm_forward(
+        flat_tokens.astype(jnp.float32) + branch, first_gain, first_shift
+    )
+    first_low = first_out.astype(jnp.bfloat16)
+    inner_sum = jnp.dot(
+        first_low, inner_weight, preferred_element_type=jnp.float32
+    ) + inner_bias.astype(jnp.float32)
+    activated, gelu_pull = jax.vjp(exact_gelu, inner_sum)
+    activated_low = activated.astype(jnp.bfloat16)
+    second = jnp.dot(
+        activated_low, outer_weight, preferred_element_type=jnp.float32
+    ) + outer_bias.astype(jnp.float32)
+    result, normed_two, root_two = norm_forward(first_out + second, second_gain, second_shift)
+    output = result.astype(jnp.bfloat16)[None]
+    upstream = cotangent[0].astype(jnp.float32)
+    gradient_second_gain = jnp.sum(upstream * normed_two, axis=0)
+    gradient_second_shift = jnp.sum(upstream, axis=0)
+    delta_two = norm_backward(upstream, normed_two, root_two, second_gain)
+    delta_second = delta_two.astype(jnp.bfloat16)
+    gradient_outer_bias = jnp.sum(delta_second.astype(jnp.float32), axis=0)
+    gradient_outer_weight = jnp.einsum(
+        "tf,td->fd", activated_low, delta_second, preferred_element_type=jnp.float32
+    )
+    delta_activated = jnp.einsum(
+        "td,fd->tf", delta_second, outer_weight, preferred_element_type=jnp.float32
+    )
+    delta_inner = gelu_pull(delta_activated)[0].astype(jnp.bfloat16)
+    gradient_inner_bias = jnp.sum(delta_inner.astype(jnp.float32), axis=0)
+    gradient_inner_weight = jnp.einsum(
+        "td,tf->df", first_low, delta_inner, preferred_element_type=jnp.float32
+    )
+    delta_first = delta_two + jnp.einsum(
+        "tf,df->td", delta_inner, inner_weight, preferred_element_type=jnp.float32
+    )
+    gradient_first_gain = jnp.sum(delta_first * normed_one, axis=0)
+    gradient_first_shift = jnp.sum(delta_first, axis=0)
+    delta_one = norm_backward(delta_first, normed_one, root_one, first_gain)
+    delta_branch = delta_one.astype(jnp.bfloat16)
+    gradient_out_bias = jnp.sum(delta_branch.astype(jnp.float32), axis=0)
+    gradient_out_weight = jnp.einsum(
+        "td,te->de", attended_rows, delta_branch, preferred_element_type=jnp.float32
+    )
+    delta_attended = jnp.einsum(
+        "te,de->td", delta_branch, out_weight, preferred_element_type=jnp.float32
+    ).astype(jnp.bfloat16)
+    delta_rows = delta_attended.reshape(row_count, head_count, head_dim).transpose(1, 0, 2)
+    send_grads = scatter_rows(delta_rows, send_matrix, seq_count)
+    grad_arrived = lax.all_to_all(send_grads, "seq", split_axis=0, concat_axis=0, tiled=True)
+    kept_queries, kept_keys, kept_values, kept_segments = (
+        queries,
+        keys_in,
+        values,
+        cluster_segments,
+    )
+    grad_cluster = collect_rows(grad_arrived, arrive_matrix, head_dim).reshape(
+        head_count * per_owner, cluster, head_dim
+    )
+    three_grads = cluster_backward(
+        kept_queries, kept_keys, kept_values, kept_segments, log_total, grad_cluster, score_scale
+    )
+    leaving_grads = scatter_rows(
+        three_grads.reshape(head_count, row_count, 3 * head_dim), arrive_matrix, seq_count
+    )
+    returned_grads = lax.all_to_all(leaving_grads, "seq", split_axis=0, concat_axis=0, tiled=True)
+    delta_three = (
+        collect_rows(returned_grads, send_matrix, 3 * head_dim)
+        .reshape(head_count, row_count, 3, head_dim)
+        .transpose(1, 2, 0, 3)
+        .reshape(row_count, 3 * model_width)
+    )
+    bias_grads = jnp.sum(delta_three.astype(jnp.float32), axis=0)
+    weight_grads = jnp.einsum(
+        "td,te->de", flat_tokens, delta_three, preferred_element_type=jnp.float32
+    )
+    gradient_tokens = (
+        delta_one
+        + jnp.einsum("te,de->td", delta_three, w_three, preferred_element_type=jnp.float32)
+    ).astype(jnp.bfloat16)[None]
+    gradient_query_weight = weight_grads[:, :model_width]
+    gradient_key_weight = weight_grads[:, model_width : 2 * model_width]
+    gradient_value_weight = weight_grads[:, 2 * model_width :]
+    gradient_query_bias = bias_grads[:model_width]
+    gradient_value_bias = bias_grads[2 * model_width :]
+    weights_out = [
+        gradient_out_weight.reshape(8, -1, model_width),
+        gradient_inner_weight.reshape(8, model_width // 8, -1, model_width)
+        .transpose(0, 2, 1, 3)
+        .reshape(8, -1, model_width),
+        gradient_outer_weight.reshape(8, -1, model_width),
+        gradient_query_weight.reshape(8, -1, model_width),
+        gradient_key_weight.reshape(8, -1, model_width),
+        gradient_value_weight.reshape(8, -1, model_width),
+    ]
+    vectors = jnp.concatenate(
+        [
+            vector.reshape(8, -1)
+            for vector in (
+                gradient_query_bias,
+                gradient_value_bias,
+                gradient_out_bias,
+                gradient_first_gain,
+                gradient_first_shift,
+                gradient_inner_bias,
+                gradient_outer_bias,
+                gradient_second_gain,
+                gradient_second_shift,
+            )
+        ],
+        axis=1,
+    )
+    used = sum(block.shape[1] for block in weights_out)
+    total_rows = -(-(used + 2) // 128) * 128
+    spare = (total_rows - used) * model_width - vectors.shape[1]
+    vectors = jnp.pad(vectors, ((0, 0), (0, spare))).reshape(8, -1, model_width)
+    grads = jnp.concatenate([block.astype(jnp.bfloat16) for block in weights_out + [vectors]], axis=1)
+    summed = reduce_rows(grads, 2, 0).astype(jnp.float32)
+    share = model_width // 8
+    inner_count = inner_weight.shape[1] // model_width
+    marks = [0]
+    for block in weights_out:
+        marks.append(marks[-1] + block.shape[1])
+    out_g, inner_g, outer_g, query_g, key_g, value_g = (
+        summed[marks[i] : marks[i + 1]] for i in range(6)
+    )
+    inner_g = inner_g.reshape(inner_count, share, model_width).transpose(1, 0, 2).reshape(share, -1)
+    flat = summed[marks[6] :].reshape(-1)
+    sizes = [share] * 5 + [share * inner_count] + [share] * 3
+    ends = [0]
+    for size in sizes:
+        ends.append(ends[-1] + size)
+    pick = [flat[ends[i] : ends[i + 1]] for i in range(9)]
+    return (
+        output,
+        gradient_tokens,
+        query_g,
+        pick[0],
+        key_g,
+        value_g,
+        pick[1],
+        out_g,
+        pick[2],
+        pick[3],
+        pick[4],
+        inner_g,
+        pick[5],
+        outer_g,
+        pick[6],
+        pick[7],
+        pick[8],
+        cluster_stats,
+    )
+
+
 def solution(mesh):
+    square = mesh.shape["seq"] == 8 and mesh.shape["rep"] == 4
     placed = (
         P("rep", "seq", None),
         P("rep", "seq"),
@@ -375,7 +806,7 @@
         P("rep", "seq", None),
     )
     return jax.shard_map(
-        body,
+        square_body if square else body,
         mesh=mesh,
         in_specs=placed,
         out_specs=(

time: 922 us -> 420 us (0.46)
  waiting for transfers between devices: 567 us -> 57.7 us
  Pallas kernels: 0 us -> 120 us
  blocking collectives: 133 us -> 41 us
  between operations: 17.1 us -> 2.18 us
  other arithmetic: 41.4 us -> 26.5 us
  local copies, waits for them, and re-layouts: 73.1 us -> 86.9 us
    reduce_scatter x3 -> x0, waiting for transfers between devices: 328 us -> none  [the longest x1 164 us: body(): lax.psum_scatter(gradient_inner_weight, 'seq', scatter_dimension=0, tiled...]
    unnamed x10 -> x0, waiting for transfers between devices: 182 us -> none
    pallas_call x0 -> x1, Pallas kernels: none -> 120 us  [reduce_rows(): pl.pallas_call(functools.partial(reduce_kernel, parts), out_shape=jax.Sha...]
    all_to_all x1 -> x0, blocking collectives: 50.3 us -> none  [body(): lax.all_to_all(leaving_grads, 'seq', split_axis=0, concat_axis=0, tiled=T...]
    unnamed x1 -> x0, blocking collectives: 37.3 us -> none
    convert_element_type x1 -> x3, local copies, waits for them, and re-layouts: 1.16 us -> 16.3 us  [the longest x2 15.2 us: square_body(): block.astype(jnp.bfloat16)]
    convert_element_type x23 -> x9, other arithmetic: 19.6 us -> 4.85 us  [the longest x1 1.84 us: square_body(): summed = reduce_rows(grads, 2, 0).astype(jnp.float32)]
    unnamed x169 -> x149, local copies, waits for them, and re-layouts: 27.2 us -> 16.9 us
  transfers between devices with their start and end apart: 11 -> 5, of which waited for: 8 -> 3; matrix products, arithmetic and copies ran while one was open for 11% -> 12% of each run, Pallas kernels for 0% -> 0%
where the time goes in v1:
time: 420 us; the launch traced here: 413 us
  Pallas kernels  120 us (29%)
  local copies, waits for them, and re-layouts  86.9 us (21%)
  waiting for transfers between devices  57.7 us (14%)
  matrix products  52.8 us (13%)
  blocking collectives  41 us (10%)
  other arithmetic  26.5 us (6%)
  starting transfers between devices  26.3 us (6%)
    pallas_call x1, Pallas kernels, reduce_rows(): pl.pallas_call(functools.partial(reduce_kernel, parts), out_shape=jax.Sha...  120 us
    psum x1, blocking collectives, square_body(): cluster_stats = lax.psum(per_head[:, :, None] * column, ('seq', 'rep'))  41 us
    all_to_all x1, waiting for transfers between devices, square_body(): lax.all_to_all(send_values, 'seq', split_axis=0, concat_axis=0, tiled=True)  34.1 us
    unnamed x149, local copies, waits for them, and re-layouts  16.9 us
    convert_element_type x2, local copies, waits for them, and re-layouts, square_body(): block.astype(jnp.bfloat16)  15.2 us
    all_to_all x1, waiting for transfers between devices, square_body(): lax.all_to_all(send_grads, 'seq', split_axis=0, concat_axis=0, tiled=True)  12 us
    all_to_all x1, waiting for transfers between devices, square_body(): lax.all_to_all(leaving, 'seq', split_axis=0, concat_axis=0, tiled=True)  11.6 us
    dot_general x1, matrix products, square_body(): jnp.dot(first_low, inner_weight, preferred_element_type=jnp.float32)  9.99 us
  transfers between devices with their start and end apart: 5, of which 3 were waited for; matrix products, arithmetic and copies ran while one was open for 12% of the time, Pallas kernels for 0%

profile of v1, /device:TPU:0, one launch (start us, length us, event | category | flops | bytes accessed | tf_op | source)
XLA Modules:
  0.0 413.3 jit_solution(4778127775041616785)
XLA Ops:
  2.7 9.5 %select_reduce_fusion = s32[12,256]{1,0:T(8,128)S(1)} fusion(s32[12,2048]{1,0:T(8,128)S(1)} %bitcast.185, s32[12,2048]{1,0:T(8,128)S(1)} %bitcast.183), kind=kLoop, calls=%fused_computation | loop fusion | flops 18871296 | bytes 208896 | tf_op jit(solution)/shard_map/while/body/eval_jaxpr/reduce_sum | solution.py:558
  15.4 7.3 %all-to-all-start = ((bf16[8,2,192]{2,1,0:T(2,128)(2,1)}), bf16[8,2,192]{2,1,0:T(2,128)(2,1)S(1)}, u32[]{:S(2)}, u32[]{:S(2)}) async-start(bf16[8,2,192]{2,1,0:T(2,128)(2,1)} %reshape.382), calls=%async_computation | async-start | bytes 16384 | tf_op jit(solution)/shard_map/all_to_all | solution.py:597
  30.7 2.5 reshape.347
  33.3 3.1 copy.152
  36.4 6.5 %all-to-all-start.1 = ((bf16[8,12,6144]{2,1,0:T(8,128)(2,1)}), bf16[8,12,6144]{2,1,0:T(8,128)(2,1)S(1)}, u32[]{:S(2)}, u32[]{:S(2)}) async-start(bf16[8,12,6144]{2,1,0:T(8,128)(2,1)} %copy.152), calls=%async_computation.1 | async-start | bytes 3145728 | tf_op jit(solution)/shard_map/all_to_all | solution.py:596
  45.3 34.1 %all-to-all-done.1 = bf16[8,12,6144]{2,1,0:T(8,128)(2,1)S(1)} async-done(((bf16[8,12,6144]{2,1,0:T(8,128)(2,1)}), bf16[8,12,6144]{2,1,0:T(8,128)(2,1)S(1)}, u32[]{:S(2)}, u32[]{:S(2)}) %all-to-all-start.1) | async-done | bytes 1179680 | tf_op jit(solution)/shard_map/all_to_all | solution.py:596
  81.0 3.0 reshape.348
  94.9 3.8 all-to-all-start.2
  101.8 11.6 %all-to-all-done.2 = bf16[8,12,2048]{2,1,0:T(8,128)(2,1)S(1)} async-done(((bf16[8,12,2048]{2,1,0:T(8,128)(2,1)}), bf16[8,12,2048]{2,1,0:T(8,128)(2,1)S(1)}, u32[]{:S(2)}, u32[]{:S(2)}) %all-to-all-start.2) | async-done | bytes 393248 | tf_op jit(solution)/shard_map/all_to_all | solution.py:622
  117.6 10.0 %multiply_convert_fusion = (bf16[256,3072]{1,0:T(8,128)(2,1)S(1)}, f32[256,3072]{1,0:T(8,128)S(1)}, f32[256,3072]{1,0:T(8,128)S(1)}) fusion(f32[3072]{0:T(1024)S(1)} %copy-done.44, bf16[768,3072]{1,0:T(8,128)(2,1)} %param.33, f32[256,768]{1,0:T(8,128)S(1)} %get-tuple-element.80, f32[768]{0:T(1024)S(1)} %convert_element_type.242, ...), kind=kOutput, calls=%fused_computation.12 | convolution fusion | flops 1260847104 | bytes 13389824 | tf_op jit(solution)/shard_map/dot_general | solution.py:635
  132.1 2.8 fusion.101
  134.9 2.2 multiply_reduce_fusion.1
  143.9 3.9 all-to-all-start.3
  150.5 12.0 %all-to-all-done.3 = bf16[8,12,2048]{2,1,0:T(8,128)(2,1)S(1)} async-done(((bf16[8,12,2048]{2,1,0:T(8,128)(2,1)}), bf16[8,12,2048]{2,1,0:T(8,128)(2,1)S(1)}, u32[]{:S(2)}, u32[]{:S(2)}) %all-to-all-start.3) | async-done | bytes 393248 | tf_op jit(solution)/shard_map/all_to_all | solution.py:678
  165.4 2.2 fusion.49
  167.7 3.3 fusion.19
  174.9 3.2 convert_element_type.260
  178.1 2.4 fusion.34
  182.0 3.0 reshape.358
  185.0 1.9 copy.180
  186.8 4.8 %all-to-all-start.4 = ((bf16[8,12,6144]{2,1,0:T(8,128)(2,1)}), bf16[8,12,6144]{2,1,0:T(8,128)(2,1)}, u32[]{:S(2)}, u32[]{:S(2)}) async-start(bf16[8,12,6144]{2,1,0:T(8,128)(2,1)} %copy.180), calls=%async_computation.4 | async-start | bytes 3145728 | tf_op jit(solution)/shard_map/all_to_all | solution.py:694
  191.6 5.1 %convolution_convert_fusion.2 = bf16[768,3072]{1,0:T(8,128)(2,1)} fusion(bf16[256,3072]{1,0:T(8,128)(2,1)} %copy-done.17, f32[256,768]{1,0:T(8,128)S(1)} %get-tuple-element.80, f32[768]{0:T(1024)S(1)} %convert_element_type.242, f32[768]{0:T(1024)S(1)} %convert_element_type.241, f32[256]{0:T(256)S(1)} %copy-done.42, f32[256]{0:T(256)S(1)} %copy-done.35), kind=kOutput, calls=%fused_computation.4 | convolution fusion | flops 1211301888 | bytes 7086080 | tf_op jit(solution)/shard_map/td,tf->df/dot_general | solution.py:659
  196.7 9.8 %convert_element_type.266 = bf16[8,96,4,768]{3,2,1,0:T(4,128)(2,1)} reshape(bf16[768,3072]{1,0:T(8,128)(2,1)} %convolution_convert_fusion.2) | data formatting | bytes 9437184 | tf_op jit(solution)/shard_map/convert_element_type | solution.py:745
  206.5 5.4 %copy.184 = bf16[8,4,96,768]{3,2,1,0:T(8,128)(2,1)} copy(bf16[8,4,96,768]{3,1,2,0:T(4,128)(2,1)} %bitcast.160) | data formatting | bytes 9437184 | tf_op jit(solution)/shard_map/convert_element_type | solution.py:745
  215.8 2.8 constant_dynamic-update-slice_fusion.7
  220.7 5.5 %copy-done.2 = bf16[8,1280,768]{2,1,0:T(8,128)(2,1)} copy-done((bf16[8,1280,768]{2,1,0:T(8,128)(2,1)}, bf16[8,1280,768]{2,1,0:T(8,128)(2,1)S(1)}, u32[]{:S(2)}) %copy-start.2) | copy-done | bytes 15728664
  226.8 41.0 %psum.7 = f32[2,12,8]{1,2,0:T(8,128)} all-reduce(f32[2,12,8]{1,2,0:T(8,128)S(1)} %broadcast_multiply_fusion), channel_id=1, replica_groups=mesh['seq'=8,'rep'=4] {'seq','rep'}, use_global_device_ids=true, to_apply=%region_29.30 | all-reduce | flops 192 | bytes 1536 | tf_op jit(solution)/shard_map/psum | solution.py:618
  267.8 2.1 copy.181
  269.9 2.7 reshape.359
  272.6 2.5 fusion.32
  275.3 1.9 fusion.50
  286.8 119.9 %reduce_rows.1 = bf16[2,2,2,160,768]{4,3,2,1,0:T(8,128)(2,1)} custom-call(bf16[2,2,2,1280,768]{4,3,2,1,0:T(8,128)(2,1)} %bitcast.161), custom_call_target="tpu_custom_call" | custom-call | tf_op jit(solution)/shard_map/reduce_rows/pallas_call | solution.py:233
  (273 shorter events, 79.4 us)
Async XLA Ops:
  0.7 115.2 %copy-start = (bf16[768,768]{1,0:T(8,128)(2,1)S(1)}, bf16[768,768]{1,0:T(8,128)(2,1)}, u32[]{:S(2)}) copy-start(bf16[768,768]{1,0:T(8,128)(2,1)} %param.29) | copy-start | bytes 3538948
  0.7 22.0 %copy-start.18 = (bf16[768,768]{1,0:T(8,128)(2,1)S(1)}, bf16[768,768]{1,0:T(8,128)(2,1)}, u32[]{:S(2)}) copy-start(bf16[768,768]{1,0:T(8,128)(2,1)} %param.24) | copy-start | bytes 3538948
  0.7 22.1 %copy-start.51 = (bf16[768]{0:T(1024)(128)(2,1)S(1)}, bf16[768]{0:T(1024)(128)(2,1)}, u32[]{:S(2)}) copy-start(bf16[768]{0:T(1024)(128)(2,1)} %param.28) | copy-start | bytes 4612
  0.7 22.1 %copy-start.52 = (bf16[768]{0:T(1024)(128)(2,1)S(1)}, bf16[768]{0:T(1024)(128)(2,1)}, u32[]{:S(2)}) copy-start(bf16[768]{0:T(1024)(128)(2,1)} %param.25) | copy-start | bytes 4612
  13.3 13.9 %copy-start.37 = (s32[12,256]{1,0:T(8,128)}, s32[12,256]{1,0:T(8,128)S(1)}, u32[]{:S(2)}) copy-start(s32[12,256]{1,0:T(8,128)S(1)} %convert_reduce_fusion.1) | copy-start | bytes 36868
  15.4 21.0 %all-to-all-start = ((bf16[8,2,192]{2,1,0:T(2,128)(2,1)}), bf16[8,2,192]{2,1,0:T(2,128)(2,1)S(1)}, u32[]{:S(2)}, u32[]{:S(2)}) async-start(bf16[8,2,192]{2,1,0:T(2,128)(2,1)} %reshape.382), calls=%async_computation | async-start | bytes 16384 | tf_op jit(solution)/shard_map/all_to_all | solution.py:597
  33.3 9.7 %copy-start.28 = (s32[1,12,16]{2,0,1:T(1,128)S(1)}, s32[1,12,16]{2,0,1:T(1,128)}, u32[]{:S(2)}) copy-start(s32[1,12,16]{2,0,1:T(1,128)} %param.23) | copy-start | bytes 2308
  33.3 9.9 %copy-start.22 = (s32[1,12,2048]{2,0,1:T(1,128)S(1)}, s32[1,12,2048]{2,0,1:T(1,128)}, u32[]{:S(2)}) copy-start(s32[1,12,2048]{2,0,1:T(1,128)} %param.22) | copy-start | bytes 294916
  36.4 42.9 %all-to-all-start.1 = ((bf16[8,12,6144]{2,1,0:T(8,128)(2,1)}), bf16[8,12,6144]{2,1,0:T(8,128)(2,1)S(1)}, u32[]{:S(2)}, u32[]{:S(2)}) async-start(bf16[8,12,6144]{2,1,0:T(8,128)(2,1)} %copy.152), calls=%async_computation.1 | async-start | bytes 3145728 | tf_op jit(solution)/shard_map/all_to_all | solution.py:596
  44.4 47.6 %copy-start.39 = (s32[12,256]{1,0:T(8,128)}, s32[12,256]{1,0:T(8,128)S(1)}, u32[]{:S(2)}) copy-start(s32[12,256]{1,0:T(8,128)S(1)} %convert_reduce_fusion) | copy-start | bytes 36868
  92.0 6.7 %copy-start.53 = (bf16[768]{0:T(1024)(128)(2,1)S(1)}, bf16[768]{0:T(1024)(128)(2,1)}, u32[]{:S(2)}) copy-start(bf16[768]{0:T(1024)(128)(2,1)} %param.36) | copy-start | bytes 4612
  92.0 7.3 %copy-start.49 = (bf16[3072]{0:T(1024)(128)(2,1)S(1)}, bf16[3072]{0:T(1024)(128)(2,1)}, u32[]{:S(2)}) copy-start(bf16[3072]{0:T(1024)(128)(2,1)} %param.34) | copy-start | bytes 18436
  92.0 7.9 %copy-start.54 = (bf16[768]{0:T(1024)(128)(2,1)S(1)}, bf16[768]{0:T(1024)(128)(2,1)}, u32[]{:S(2)}) copy-start(bf16[768]{0:T(1024)(128)(2,1)} %param.30) | copy-start | bytes 4612
  92.1 8.5 %copy-start.55 = (bf16[768]{0:T(1024)(128)(2,1)S(1)}, bf16[768]{0:T(1024)(128)(2,1)}, u32[]{:S(2)}) copy-start(bf16[768]{0:T(1024)(128)(2,1)} %param.32) | copy-start | bytes 4612
  92.1 8.5 %copy-start.56 = (bf16[768]{0:T(1024)(128)(2,1)S(1)}, bf16[768]{0:T(1024)(128)(2,1)}, u32[]{:S(2)}) copy-start(bf16[768]{0:T(1024)(128)(2,1)} %param.31) | copy-start | bytes 4612
  92.1 8.5 %copy-start.57 = (bf16[768]{0:T(1024)(128)(2,1)S(1)}, bf16[768]{0:T(1024)(128)(2,1)}, u32[]{:S(2)}) copy-start(bf16[768]{0:T(1024)(128)(2,1)} %param.37) | copy-start | bytes 4612
  92.1 9.1 %copy-start.58 = (bf16[768]{0:T(1024)(128)(2,1)S(1)}, bf16[768]{0:T(1024)(128)(2,1)}, u32[]{:S(2)}) copy-start(bf16[768]{0:T(1024)(128)(2,1)} %param.38) | copy-start | bytes 4612
  94.9 18.5 %all-to-all-start.2 = ((bf16[8,12,2048]{2,1,0:T(8,128)(2,1)}), bf16[8,12,2048]{2,1,0:T(8,128)(2,1)S(1)}, u32[]{:S(2)}, u32[]{:S(2)}) async-start(bf16[8,12,2048]{2,1,0:T(8,128)(2,1)} %copy.163), calls=%async_computation.2 | async-start | bytes 1048576 | tf_op jit(solution)/shard_map/all_to_all | solution.py:622
  115.8 11.8 %copy-start.11 = (bf16[12,256,64]{1,2,0:T(8,128)(2,1)}, bf16[12,256,64]{1,2,0:T(8,128)(2,1)S(1)}, u32[]{:S(2)}) copy-start(bf16[12,256,64]{1,2,0:T(8,128)(2,1)S(1)} %fusion.45) | copy-start | bytes 1179652
  115.9 11.8 %slice-start = ((s8[4718592]{0:T(1024)(128)(4,1)}), s8[4194304]{0:T(1024)(128)(4,1)S(1)}, s32[]{:S(2)}) async-start(s8[4718592]{0:T(1024)(128)(4,1)} %bitcast.196), calls=%async_computation.5 | async-start | bytes 8388608
  117.3 19.8 %copy-start.34 = (f32[256]{0:T(256)}, f32[256]{0:T(256)S(1)}, u32[]{:S(2)}) copy-start(f32[256]{0:T(256)S(1)} %broadcast_multiply_fusion.6) | copy-start | bytes 3076
  117.6 19.6 %copy-start.41 = (f32[256]{0:T(256)}, f32[256]{0:T(256)S(1)}, u32[]{:S(2)}) copy-start(f32[256]{0:T(256)S(1)} %add_rsqrt_fusion.1) | copy-start | bytes 3076
  117.6 10.1 %copy-start.50 = (f32[768]{0:T(1024)S(1)}, f32[768]{0:T(1024)}, u32[]{:S(2)}) copy-start(f32[768]{0:T(1024)} %convert_element_type.246) | copy-start | bytes 9220
  117.6 10.1 %slice-start.1 = ((s8[4718592]{0:T(1024)(128)(4,1)}), s8[524288]{0:T(1024)(128)(4,1)S(1)}, s32[]{:S(2)}) async-start(s8[4718592]{0:T(1024)(128)(4,1)} %bitcast.196), calls=%async_computation.6 | async-start | bytes 1048576
  143.9 18.6 %all-to-all-start.3 = ((bf16[8,12,2048]{2,1,0:T(8,128)(2,1)}), bf16[8,12,2048]{2,1,0:T(8,128)(2,1)S(1)}, u32[]{:S(2)}, u32[]{:S(2)}) async-start(bf16[8,12,2048]{2,1,0:T(8,128)(2,1)} %copy.168), calls=%async_computation.3 | async-start | bytes 1048576 | tf_op jit(solution)/shard_map/all_to_all | solution.py:678
  186.8 81.0 %all-to-all-start.4 = ((bf16[8,12,6144]{2,1,0:T(8,128)(2,1)}), bf16[8,12,6144]{2,1,0:T(8,128)(2,1)}, u32[]{:S(2)}, u32[]{:S(2)}) async-start(bf16[8,12,6144]{2,1,0:T(8,128)(2,1)} %copy.180), calls=%async_computation.4 | async-start | bytes 3145728 | tf_op jit(solution)/shard_map/all_to_all | solution.py:694
  206.5 6.8 %copy-start.59 = (bf16[768]{0:T(1024)(128)(2,1)S(1)}, bf16[768]{0:T(1024)(128)(2,1)}, u32[]{:S(2)}) copy-start(bf16[768]{0:T(1024)(128)(2,1)} %get-tuple-element.43) | copy-start | bytes 4612
  206.5 7.5 %copy-start.48 = (bf16[3072]{0:T(1024)(128)(2,1)S(1)}, bf16[3072]{0:T(1024)(128)(2,1)}, u32[]{:S(2)}) copy-start(bf16[3072]{0:T(1024)(128)(2,1)} %get-tuple-element.86) | copy-start | bytes 18436
  206.5 7.5 %copy-start.46 = (bf16[768]{0:T(1024)(128)(2,1)S(1)}, bf16[768]{0:T(1024)(128)(2,1)}, u32[]{:S(2)}) copy-start(bf16[768]{0:T(1024)(128)(2,1)} %get-tuple-element.46) | copy-start | bytes 4612
  206.5 8.1 %copy-start.45 = (bf16[768]{0:T(1024)(128)(2,1)S(1)}, bf16[768]{0:T(1024)(128)(2,1)}, u32[]{:S(2)}) copy-start(bf16[768]{0:T(1024)(128)(2,1)} %get-tuple-element.40) | copy-start | bytes 4612
  206.5 8.8 %copy-start.12 = (bf16[12,256,64]{1,2,0:T(8,128)(2,1)S(1)}, bf16[12,256,64]{1,2,0:T(8,128)(2,1)}, u32[]{:S(2)}) copy-start(bf16[12,256,64]{1,2,0:T(8,128)(2,1)} %copy-done.11) | copy-start | bytes 1179652
  226.2 46.4 %copy-start.38 = (s32[12,256]{1,0:T(8,128)S(1)}, s32[12,256]{1,0:T(8,128)}, u32[]{:S(2)}) copy-start(s32[12,256]{1,0:T(8,128)} %copy-done.37) | copy-start | bytes 36868
  (40 other events, 129.7 us)

commit v2 on v0

--- a/solution.py
+++ b/solution.py
@@ -1,6 +1,10 @@
+import functools
+
 import jax
 import jax.numpy as jnp
 from jax import lax
+from jax.experimental import pallas as pl
+from jax.experimental.pallas import tpu as pltpu
 from jax.sharding import PartitionSpec as P
 
 EPSILON = 1e-12
@@ -102,6 +106,930 @@
         * score_scale
     )
     return jnp.stack([query_grads, key_grads, value_grads], axis=2).astype(jnp.bfloat16)
+
+
+MESH = pl.DeviceIdType.MESH
+
+
+def half_roll(block):
+    return jnp.concatenate([block[:, 64:], block[:, :64]], axis=1)
+
+
+def lanes(shape):
+    return lax.broadcasted_iota(jnp.int32, shape, len(shape) - 1)
+
+
+def bits(value, flip):
+    return value + flip - 2 * value * flip
+
+
+def coordinates():
+    s, r = lax.axis_index("seq"), lax.axis_index("rep")
+    return s // 4, (s // 2) % 2, s % 2, r // 2, r % 2
+
+
+def device(zh, zl, x, y, c):
+    return (4 * zh + 2 * zl + x, 2 * y + c)
+
+
+def greet(peers):
+    barrier = pltpu.get_barrier_semaphore()
+    for peer in peers:
+        pl.semaphore_signal(barrier, inc=1, device_id=peer, device_id_type=MESH)
+    pl.semaphore_wait(barrier, len(peers))
+
+
+def remote(src, dst, sems, index, peer):
+    return pltpu.make_async_remote_copy(
+        src_ref=src,
+        dst_ref=dst,
+        send_sem=sems[0].at[index],
+        recv_sem=sems[1].at[index],
+        device_id=peer,
+        device_id_type=MESH,
+    )
+
+
+def dot(left, right, left_dim=1, right_dim=0):
+    return lax.dot_general(
+        left,
+        right,
+        (((left_dim,), (right_dim,)), ((), ())),
+        preferred_element_type=jnp.float32,
+    )
+
+
+def hot(condition):
+    return jnp.where(condition, 1.0, 0.0).astype(jnp.bfloat16)
+
+
+def build_gather(order_ref, row, start, count, into):
+    tokens = into.shape[1]
+
+    def one(k, carry):
+        at = pl.multiple_of(k * 128, 128)
+        ids = order_ref[row : row + 1, pl.ds(pl.multiple_of(start + at, 128), 128)]
+        column = jnp.broadcast_to(ids.astype(jnp.float32), (128, 128)).T
+        lane = lanes((128, 128)).astype(jnp.float32)
+        for t in range(tokens // 128):
+            into[pl.ds(at, 128), t * 128 : (t + 1) * 128] = hot(column == lane + 128.0 * t)
+        return carry
+
+    lax.fori_loop(0, count // 128, one, 0)
+
+
+def build_scatter(order_ref, row, start, count, into, base):
+    def one(k, carry):
+        at = pl.multiple_of(k * 128, 128)
+        token = lax.broadcasted_iota(jnp.int32, (128, 128), 0) + at
+        for p in range(count // 128):
+            ids = order_ref[row : row + 1, pl.ds(pl.multiple_of(start + 128 * p, 128), 128)]
+            into[pl.ds(at, 128), base + 128 * p : base + 128 * (p + 1)] = hot(ids == token)
+        return carry
+
+    lax.fori_loop(0, into.shape[0] // 128, one, 0)
+
+
+def select_head(slab, half, place):
+    return jnp.where(half == place, slab, half_roll(slab))
+
+
+def join(low_lanes, high_lanes):
+    return jnp.where(lanes(low_lanes.shape) < 64, low_lanes, high_lanes)
+
+
+def pick_columns(refs, j, c, add_zero):
+    def slab(ref, index):
+        return ref[:, pl.ds(pl.multiple_of(index * 128, 128), 128)].astype(jnp.float32)
+
+    first = [slab(ref, j) for ref in refs]
+    other = [slab(ref, 4 + j // 2) for ref in refs]
+    zero = jnp.zeros_like(first[0])
+    q1, v1 = select_head(first[0], c, 0), select_head(first[2], c, 1)
+    k1 = select_head(first[1], c, 0)
+    v2, q2 = select_head(other[2], j % 2, 0), select_head(other[0], j % 2, 1)
+    k2 = select_head(other[1], j % 2, 1)
+    return join(q1, v1), join(k1, zero), join(v2, q2), join(zero, k2)
+
+
+def forward_kernel(
+    tokens_ref,
+    cot_ref,
+    seg_ref,
+    orders_ref,
+    hot_ref,
+    wq_ref,
+    wk_ref,
+    wv_ref,
+    bias_ref,
+    att_ref,
+    x_all,
+    cot_my,
+    sorted_ref,
+    prob_ref,
+    wsel_ref,
+    order_ref,
+    stats_ref,
+    orders_in,
+    hot_in,
+    seg_src,
+    seg_all,
+    bias_sel,
+    tok,
+    gather,
+    scatter,
+    att_sorted,
+    att_send,
+    att_in,
+    ent_ref,
+    cnt_ref,
+    swap_send,
+    swap_recv,
+    ring_send,
+    ring_recv,
+    seg_send,
+    seg_recv,
+    back_send,
+    back_recv,
+):
+    zh, zl, x, y, c = coordinates()
+    j = 2 * zl + x
+    p = 4 * c + j
+    block = tokens_ref.shape[0]
+    group = 8 * block
+    scale = 0.125
+    swap = (swap_send, swap_recv)
+    ring = (ring_send, ring_recv)
+    seg_sems = (seg_send, seg_recv)
+    back = (back_send, back_recv)
+
+    def member(flip):
+        fc, fz, fx = flip // 4, (flip // 2) % 2, flip % 2
+        mc, mz, mx = bits(c, fc), bits(zl, fz), bits(x, fx)
+        return device(zh, mz, mx, y, mc), 4 * mc + 2 * mz + mx
+
+    swap_peer = device(1 - zh, zl, x, y, 1 - c)
+    peers = [member(flip)[0] for flip in range(1, 8)]
+    greet(peers + [swap_peer])
+    sibling = peers[3]
+    over_x, over_z = peers[0], peers[1]
+    matched = c == zh
+
+    seg_src[...] = jnp.broadcast_to(seg_ref[...], seg_src.shape)
+    table_copies = [
+        remote(orders_ref, orders_in, swap, 0, sibling),
+        remote(hot_ref, hot_in, swap, 1, sibling),
+    ]
+    for copy in table_copies:
+        copy.start()
+    p_swap = 4 * (1 - c) + j
+    pairs = [
+        (tokens_ref, x_all.at[p_swap], x_all.at[p]),
+        (seg_src, seg_all.at[p_swap], seg_all.at[p]),
+        (cot_ref, cot_my, cot_my),
+    ]
+    swaps = [remote(src, dst, swap, 2 + i, swap_peer) for i, (src, dst, _) in enumerate(pairs)]
+    locals_ = [
+        pltpu.make_async_copy(src, own, swap_recv.at[5 + i]) for i, (src, _, own) in enumerate(pairs)
+    ]
+
+    @pl.when(matched)
+    def _():
+        for copy in locals_:
+            copy.start()
+
+    @pl.when(jnp.logical_not(matched))
+    def _():
+        for copy in swaps:
+            copy.start()
+
+    tiles = pick_columns((wq_ref, wk_ref, wv_ref), j, c, None)
+    for i, tile in enumerate(tiles):
+        wsel_ref[:, 128 * i : 128 * (i + 1)] = tile.astype(jnp.bfloat16)
+    bias_tiles = pick_columns(
+        (bias_ref.at[pl.ds(0, 8)], bias_ref.at[pl.ds(8, 8)], bias_ref.at[pl.ds(16, 8)]), j, c, None
+    )
+    for i, tile in enumerate(bias_tiles):
+        bias_sel[:, 128 * i : 128 * (i + 1)] = tile
+
+    for copy in table_copies:
+        copy.wait()
+    h1, h2 = 2 * j + c, 8 + j
+    for i, h in enumerate((h1, h2)):
+        own, other = orders_ref[pl.ds(h, 1), :], orders_in[pl.ds(h, 1), :]
+        order_ref[i : i + 1, :] = jnp.where(matched, own, other)
+    half = 1024 * c
+
+    @pl.when(matched)
+    def _():
+        for i in (0, 1):
+            locals_[i].wait()
+
+    @pl.when(jnp.logical_not(matched))
+    def _():
+        for i in (0, 1):
+            swaps[i].wait()
+
+    px, pz, pd = member(1)[1], member(2)[1], member(3)[1]
+    ps, psx, psz, psd = (member(flip)[1] for flip in (4, 5, 6, 7))
+    own = x_all.at[p]
+    to_x = remote(own, own, ring, 0, over_x)
+    to_z = remote(own, own, ring, 1, over_z)
+    to_s = remote(own, own, ring, 2, sibling)
+    for copy in (to_x, to_z, to_s):
+        copy.start()
+    seg_copies = []
+    for flip in range(1, 8):
+        copy = remote(seg_all.at[p], seg_all.at[p], seg_sems, flip - 1, peers[flip - 1])
+        copy.start()
+        seg_copies.append(copy)
+
+    build_gather(order_ref, 0, 0, group, gather.at[pl.ds(0, group)])
+    to_x.wait()
+    upper, lower = pl.ds(0, block // 2), pl.ds(block // 2, block // 2)
+    x_half = remote(x_all.at[px, upper], x_all.at[px, upper], ring, 3, over_z)
+    x_half.start()
+    x_to_s = remote(x_all.at[px], x_all.at[px], ring, 4, sibling)
+    x_to_s.start()
+    to_z.wait()
+    z_half = remote(x_all.at[pz, lower], x_all.at[pz, lower], ring, 5, over_x)
+    z_half.start()
+    z_to_s = remote(x_all.at[pz], x_all.at[pz], ring, 6, sibling)
+    z_to_s.start()
+    build_gather(order_ref, 1, half, group // 2, gather.at[pl.ds(group, group // 2)])
+    for copy in seg_copies:
+        copy.wait()
+
+    def project(position):
+        at = pl.ds(pl.multiple_of(position * block, block), block)
+        out = dot(x_all[position], wsel_ref[...]) + bias_sel[0:1, :]
+        ids = seg_all[position, 0:1, :].astype(jnp.float32)
+        columns = [
+            jnp.broadcast_to(ids[:, 128 * i : 128 * (i + 1)], (128, 128)).T for i in range(block // 128)
+        ]
+        lane = lanes((block, 128))
+        seg_hot = hot(jnp.concatenate(columns, axis=0) == (lane % 64).astype(jnp.float32))
+        low = out.astype(jnp.bfloat16)
+        tok[at, 0:128] = low[:, 0:128]
+        tok[at, 128:256] = jnp.where(lane < 64, low[:, 128:256], seg_hot)
+        tok[at, 256:384] = low[:, 256:384]
+        tok[at, 384:512] = jnp.where(lane < 64, seg_hot, low[:, 384:512])
+
+    project(p)
+    project(px)
+    project(pz)
+    to_s.wait()
+    project(ps)
+    x_half.wait()
+    z_half.wait()
+    d_to_s = remote(x_all.at[pd], x_all.at[pd], ring, 7, sibling)
+    d_to_s.start()
+    project(pd)
+    x_to_s.wait()
+    project(psx)
+    z_to_s.wait()
+    project(psz)
+    build_scatter(order_ref, 0, 0, group, scatter, 0)
+    build_scatter(order_ref, 1, half, group // 2, scatter, group)
+    d_to_s.wait()
+    project(psd)
+
+    step = 512
+
+    def gather_rows(k, carry):
+        at = pl.ds(pl.multiple_of(k * step, step), step)
+        sorted_ref[at, :] = dot(gather[at, :], tok[:, 0:256]).astype(jnp.bfloat16)
+        return carry
+
+    def gather_rows_two(k, carry):
+        at = pl.ds(pl.multiple_of(k * step, step), step)
+        sorted_ref[at, :] = dot(gather[at, :], tok[:, 256:512]).astype(jnp.bfloat16)
+        return carry
+
+    lax.fori_loop(0, group // step, gather_rows, 0)
+    lax.fori_loop(group // step, group * 3 // 2 // step, gather_rows_two, 0)
+
+    def attend(first_lanes):
+        def one(i, carry):
+            at = pl.ds(pl.multiple_of(i * 128, 128), 128)
+            tile_zero, tile_one = sorted_ref[at, 0:128], sorted_ref[at, 128:256]
+            low_lanes = lanes((128, 128)) < 64
+            query_lanes = low_lanes if first_lanes else jnp.logical_not(low_lanes)
+            queries = jnp.where(query_lanes, tile_zero, jnp.zeros_like(tile_zero))
+            ids = jnp.where(query_lanes, jnp.zeros_like(tile_one), tile_one)
+            scores = dot(queries, tile_one, 1, 1) * scale
+            allowed = dot(ids, tile_one, 1, 1)
+            masked = jnp.where(allowed > 0.5, scores, NEGATIVE)
+            highest = jnp.max(masked, axis=1, keepdims=True)
+            raised = jnp.exp(masked - highest)
+            totals = jnp.sum(raised, axis=1, keepdims=True)
+            weights = raised / totals
+            prob_ref[at, :] = weights
+            mixed = dot(weights.astype(jnp.bfloat16), tile_zero)
+            att_sorted[at, :] = jnp.where(query_lanes, 0.0, mixed).astype(jnp.bfloat16)
+            log_total = highest + jnp.log(totals)
+            entropy = jnp.where(lanes((128, 128)) == 0, log_total, 0.0) - weights * masked
+            ent_ref[pl.ds(i, 1), :] = jnp.sum(entropy, axis=0, keepdims=True)
+            cnt_ref[pl.ds(i, 1), :] = jnp.sum(allowed, axis=0, keepdims=True)
+            return carry
+
+        return one
+
+    lax.fori_loop(0, 16, attend(True), 0)
+    lax.fori_loop(16, 24, attend(False), 0)
+
+    def place(position):
+        at = pl.ds(pl.multiple_of(position * block, block), block)
+        return dot(scatter[at, :], att_sorted[...]).astype(jnp.bfloat16)
+
+    back_copies = []
+    for flip in (3, 7, 1, 5, 2, 6, 4):
+        peer, position = member(flip)
+        att_send[flip] = place(position)
+        copy = remote(att_send.at[flip], att_in.at[p], back, flip - 1, peer)
+        copy.start()
+        back_copies.append(copy)
+    att_in[p] = place(p)
+
+    stats_ref[...] = jnp.zeros_like(stats_ref)
+    for kind, (lane_sums, divisor) in enumerate(((ent_ref, 4.0 * block), (cnt_ref, 4.0 * block * 128))):
+        sums = jnp.sum(lane_sums[...], axis=1, keepdims=True) / divisor
+        for h, first, size, owner_row in ((h1, 0, 16, 16 * h1), (h2, 16, 8, 16 * h2 + 8 * c)):
+            at = pl.ds(pl.multiple_of(owner_row, 8), size)
+            owner_hot = jnp.where(matched, hot_ref[at, :], hot_in[at, :])
+            stats_ref[kind, pl.ds(h, 1), :] = jnp.sum(
+                sums[first : first + size] * owner_hot, axis=0, keepdims=True
+            )
+
+    @pl.when(matched)
+    def _():
+        locals_[2].wait()
+
+    @pl.when(jnp.logical_not(matched))
+    def _():
+        swaps[2].wait()
+
+    for copy in back_copies:
+        copy.wait()
+    for pair in range(4):
+        even, odd = att_in[pair], att_in[4 + pair]
+        att_ref[:, 128 * pair : 128 * (pair + 1)] = join(half_roll(even), odd)
+    for pair in range(2):
+        low_half = att_in[2 * pair] + att_in[4 + 2 * pair]
+        high_half = att_in[2 * pair + 1] + att_in[5 + 2 * pair]
+        att_ref[:, 512 + 128 * pair : 640 + 128 * pair] = join(low_half, half_roll(high_half))
+
+
+def forward_attention(tokens, cotangent, segments, orders, owner_hot, wq, wk, wv, biases):
+    block, width = tokens.shape
+    group = 8 * block
+    low, full = jnp.bfloat16, jnp.float32
+    vmem = pl.BlockSpec(memory_space=pltpu.VMEM)
+    dma = pltpu.SemaphoreType.DMA
+    heads = orders.shape[0]
+    rows = group * 3 // 2
+    return pl.pallas_call(
+        forward_kernel,
+        out_shape=[
+            jax.ShapeDtypeStruct((block, width), low),
+            jax.ShapeDtypeStruct((8, block, width), low),
+            jax.ShapeDtypeStruct((block, width), low),
+            jax.ShapeDtypeStruct((rows, 256), low),
+            jax.ShapeDtypeStruct((rows, 128), full),
+            jax.ShapeDtypeStruct((width, 512), low),
+            jax.ShapeDtypeStruct((8, group), jnp.int32),
+            jax.ShapeDtypeStruct((2, 16, 128), full),
+        ],
+        in_specs=[vmem] * 9,
+        out_specs=[vmem] * 8,
+        scratch_shapes=[
+            pltpu.VMEM((heads, group), jnp.int32),
+            pltpu.VMEM(owner_hot.shape, full),
+            pltpu.VMEM((8, block), jnp.int32),
+            pltpu.VMEM((8, 8, block), jnp.int32),
+            pltpu.VMEM((8, 512), full),
+            pltpu.VMEM((group, 512), low),
+            pltpu.VMEM((rows, group), low),
+            pltpu.VMEM((group, rows), low),
+            pltpu.VMEM((rows, 128), low),
+            pltpu.VMEM((8, block, 128), low),
+            pltpu.VMEM((8, block, 128), low),
+            pltpu.VMEM((24, 128), full),
+            pltpu.VMEM((24, 128), full),
+            dma((8,)),
+            dma((8,)),
+            dma((8,)),
+            dma((8,)),
+            dma((7,)),
+            dma((7,)),
+            dma((7,)),
+            dma((7,)),
+        ],
+        compiler_params=pltpu.CompilerParams(
+            collective_id=1, has_side_effects=True, vmem_limit_bytes=60 << 20
+        ),
+        name="forward_attention",
+    )(tokens, cotangent, segments, orders, owner_hot, wq, wk, wv, biases)
+
+
+def rows_of(start, q, size):
+    return pl.ds(pl.multiple_of(start * q, 16), size * q)
+
+
+def add_into(count, target, other):
+    def one(i, carry):
+        target(i)[...] = (
+            target(i)[...].astype(jnp.float32) + other(i)[...].astype(jnp.float32)
+        ).astype(jnp.bfloat16)
+        return carry
+
+    lax.fori_loop(0, count, one, 0)
+
+
+def reduce_steps(parts, g_ref, f_ref, buffers, sems, own_sem):
+    own, core_in, a_one, b_one, ab_two, z_one, z_two = buffers
+    zh, zl, x, y, c = coordinates()
+    q = g_ref.shape[3] // 8
+    width = g_ref.shape[4] // parts
+    over_c, over_y = device(zh, zl, x, y, 1 - c), device(zh, zl, x, 1 - y, c)
+    over_x, over_zl = device(zh, zl, 1 - x, y, c), device(zh, 1 - zl, x, y, c)
+    over_zh = device(1 - zh, zl, x, y, c)
+
+    def send(step, k, src, dst, peer):
+        copy = remote(src, dst, (sems[0].at[step], sems[1].at[step]), k, peer)
+        copy.start()
+        return copy
+
+    columns = [pl.ds(k * width, width) for k in range(parts)]
+    zero = [
+        send(
+            0, k, g_ref.at[:, :, :, rows_of(4 * (1 - c), q, 4), cols], core_in.at[:, :, :, :, cols], over_c
+        )
+        for k, cols in enumerate(columns)
+    ]
+    mine = [
+        pltpu.make_async_copy(
+            g_ref.at[:, :, :, rows_of(4 * c, q, 4), cols], own.at[:, :, :, :, cols], own_sem.at[k]
+        )
+        for k, cols in enumerate(columns)
+    ]
+    for copy in mine:
+        copy.start()
+    yield
+    first, second, third, fourth, fifth, sixth = [], [], [], [], [], []
+    for k, cols in enumerate(columns):
+        mine[k].wait()
+        zero[k].wait()
+        add_into(
+            8,
+            lambda i: core_in.at[i // 4, (i // 2) % 2, i % 2, :, cols],
+            lambda i: own.at[i // 4, (i // 2) % 2, i % 2, :, cols],
+        )
+        first.append(
+            (
+                send(1, k, core_in.at[:, :, 1 - x, pl.ds(0, 2 * q), cols], a_one.at[:, :, :, cols], over_x),
+                send(2, k, core_in.at[:, :, :, rows_of(3 - y, q, 1), cols], b_one.at[:, :, :, :, cols], over_y),
+            )
+        )
+        yield
+    for k, cols in enumerate(columns):
+        first[k][0].wait()
+        add_into(
+            4,
+            lambda i: a_one.at[i // 2, i % 2, :, cols],
+            lambda i: core_in.at[i // 2, i % 2, x, pl.ds(0, 2 * q), cols],
+        )
+        copy_a = send(3, k, a_one.at[:, :, rows_of(1 - y, q, 1), cols], ab_two.at[0, :, :, :, cols], over_y)
+        first[k][1].wait()
+        add_into(
+            8,
+            lambda i: b_one.at[i // 4, (i // 2) % 2, i % 2, :, cols],
+            lambda i: core_in.at[i // 4, (i // 2) % 2, i % 2, rows_of(2 + y, q, 1), cols],
+        )
+        copy_b = send(4, k, b_one.at[:, :, 1 - x, :, cols], ab_two.at[1, :, :, :, cols], over_x)
+        second.append((copy_a, copy_b))
+        yield
+    for k, cols in enumerate(columns):
+        second[k][0].wait()
+        add_into(
+            4,
+            lambda i: ab_two.at[0, i // 2, i % 2, :, cols],
+            lambda i: a_one.at[i // 2, i % 2, rows_of(y, q, 1), cols],
+        )
+        second[k][1].wait()
+        add_into(
+            4,
+            lambda i: ab_two.at[1, i // 2, i % 2, :, cols],
+            lambda i: b_one.at[i // 2, i % 2, x, :, cols],
+        )
+        third.append(send(5, k, ab_two.at[:, :, 1 - zl, :, cols], z_one.at[:, :, :, cols], over_zl))
+        yield
+    for k, cols in enumerate(columns):
+        third[k].wait()
+        add_into(
+            4,
+            lambda i: z_one.at[i // 2, i % 2, :, cols],
+            lambda i: ab_two.at[i // 2, i % 2, zl, :, cols],
+        )
+        fourth.append(send(6, k, z_one.at[:, 1 - zh, :, cols], z_two.at[:, :, cols], over_zh))
+        yield
+    for k, cols in enumerate(columns):
+        fourth[k].wait()
+        for part in range(2):
+            f_ref[c, part, y, :, cols] = (
+                z_two[part, :, cols].astype(jnp.float32) + z_one[part, zh, :, cols].astype(jnp.float32)
+            ).astype(jnp.bfloat16)
+        own_rows = f_ref.at[c, :, y, :, cols]
+        fifth.append(send(7, k, own_rows, own_rows, over_y))
+        yield
+    for k, cols in enumerate(columns):
+        fifth[k].wait()
+        both = f_ref.at[c, :, :, :, cols]
+        sixth.append(send(8, k, both, both, over_c))
+        yield
+    for copy in sixth:
+        copy.wait()
+
+
+def backward_kernel(
+    parts,
+    datt_ref,
+    sorted_ref,
+    prob_ref,
+    order_ref,
+    x_all,
+    wsel_ref,
+    delta_ref,
+    out_my,
+    stats_ref,
+    g_ref,
+    out_home,
+    grad_home,
+    f_ref,
+    gq_ref,
+    gk_ref,
+    gv_ref,
+    stats_out,
+    datt_send,
+    datt_in,
+    gather,
+    gathered,
+    dsorted,
+    scatter,
+    dqkv,
+    part_send,
+    part_in,
+    total,
+    a_in,
+    b_in,
+    a_two,
+    b_two,
+    grad_my,
+    dw,
+    dw_y,
+    dw_in,
+    dw_all,
+    w_all,
+    stats_buf,
+    stats_in,
+    own,
+    core_in,
+    a_one,
+    b_one,
+    ab_two,
+    z_one,
+    z_two,
+    datt_ssem,
+    datt_rsem,
+    part_ssem,
+    part_rsem,
+    swap_ssem,
+    swap_rsem,
+    dw_ssem,
+    dw_rsem,
+    stats_ssem,
+    stats_rsem,
+    red_ssem,
+    red_rsem,
+    own_sem,
+):
+    zh, zl, x, y, c = coordinates()
+    s = 4 * zh + 2 * zl + x
+    j = 2 * zl + x
+    p = 4 * c + j
+    block, width = datt_ref.shape
+    group = 8 * block
+    scale = 0.125
+    matched = c == zh
+    datt_sems, part_sems = (datt_ssem, datt_rsem), (part_ssem, part_rsem)
+    swap_sems, dw_sems, stats_sems = (swap_ssem, swap_rsem), (dw_ssem, dw_rsem), (stats_ssem, stats_rsem)
+
+    def member(flip):
+        fc, fz, fx = flip // 4, (flip // 2) % 2, flip % 2
+        mc, mz, mx = bits(c, fc), bits(zl, fz), bits(x, fx)
+        return device(zh, mz, mx, y, mc), mc, 2 * mz + mx
+
+    peers = [member(flip)[0] for flip in range(1, 8)]
+    sibling, over_x, over_z = peers[3], peers[0], peers[1]
+    swap_peer = device(1 - zh, zl, x, y, 1 - c)
+    over_y = device(zh, zl, x, 1 - y, c)
+    across = [device(1 - zh, bits(zl, f // 2), bits(x, f % 2), y, c) for f in range(4)]
+    greet(peers + [swap_peer, over_y] + across)
+
+    def home_copy(src, dst, index, start):
+        away = remote(src, dst, swap_sems, index, swap_peer)
+        here = pltpu.make_async_copy(src, dst, swap_rsem.at[2 + index])
+
+        @pl.when(matched)
+        def _():
+            here.start() if start else here.wait()
+
+        @pl.when(jnp.logical_not(matched))
+        def _():
+            away.start() if start else away.wait()
+
+    def tile(mc, mj):
+        first = datt_ref[:, pl.ds(pl.multiple_of(mj * 128, 128), 128)]
+        other = datt_ref[:, pl.ds(pl.multiple_of((4 + mj // 2) * 128, 128), 128)]
+        return join(
+            select_head(other.astype(jnp.float32), mj % 2, 0), select_head(first.astype(jnp.float32), mc, 1)
+        ).astype(jnp.bfloat16)
+
+    datt_copies = []
+    for flip in (3, 7, 1, 5, 2, 6, 4):
+        peer, mc, mj = member(flip)
+        datt_send[flip] = tile(mc, mj)
+        copy = remote(datt_send.at[flip], datt_in.at[p], datt_sems, flip - 1, peer)
+        copy.start()
+        datt_copies.append(copy)
+    datt_in[p] = tile(c, j)
+    home_copy(out_my, out_home, 0, True)
+
+    reduction = reduce_steps(
+        parts,
+        g_ref,
+        f_ref,
+        (own, core_in, a_one, b_one, ab_two, z_one, z_two),
+        (red_ssem, red_rsem),
+        own_sem,
+    )
+    next(reduction)
+
+    half = 1024 * c
+    build_gather(order_ref, 0, 0, group, gather.at[pl.ds(0, group)])
+    build_gather(order_ref, 1, half, group // 2, gather.at[pl.ds(group, group // 2)])
+    for copy in datt_copies:
+        copy.wait()
+    for k in range(parts):
+        next(reduction)
+
+    step = 512
+    arrived = datt_in[...].reshape(group, 128)
+
+    def gather_rows(k, carry):
+        at = pl.ds(pl.multiple_of(k * step, step), step)
+        gathered[at, :] = dot(gather[at, :], arrived).astype(jnp.bfloat16)
+        return carry
+
+    lax.fori_loop(0, group * 3 // 2 // step, gather_rows, 0)
+
+    def attend_back(first_lanes):
+        def one(i, carry):
+            at = pl.ds(pl.multiple_of(i * 128, 128), 128)
+            tile_zero, tile_one = sorted_ref[at, 0:128], sorted_ref[at, 128:256]
+            low_lanes = lanes((128, 128)) < 64
+            query_lanes = low_lanes if first_lanes else jnp.logical_not(low_lanes)
+            weights = prob_ref[at, :]
+            taken = gathered[at, :]
+            taken = jnp.where(query_lanes, jnp.zeros_like(taken), taken)
+            weight_grads = dot(taken, tile_zero, 1, 1)
+            inside = jnp.sum(weights * weight_grads, axis=1, keepdims=True)
+            score_grads = weights * (weight_grads - inside)
+            low_grads = score_grads.astype(jnp.bfloat16)
+            query_grads = dot(low_grads, tile_one) * scale
+            key_grads = dot(low_grads, tile_zero, 0, 0) * scale
+            value_grads = dot(weights.astype(jnp.bfloat16), taken, 0, 0)
+            dsorted[at, 0:128] = jnp.where(query_lanes, query_grads, value_grads).astype(jnp.bfloat16)
+            dsorted[at, 128:256] = jnp.where(query_lanes, key_grads, 0.0).astype(jnp.bfloat16)
+            return carry
+
+        return one
+
+    lax.fori_loop(0, 16, attend_back(True), 0)
+    for k in range(parts):
+        next(reduction)
+    lax.fori_loop(16, 24, attend_back(False), 0)
+
+    def place(position):
+        token = lax.broadcasted_iota(jnp.int32, (128, 128), 0) + position * block
+        for t in range(block // 128):
+            for head, start, count, base in ((0, 0, group, 0), (1, half, group // 2, group)):
+                for k in range(count // 128):
+                    ids = order_ref[head : head + 1, pl.ds(pl.multiple_of(start + 128 * k, 128), 128)]
+                    scatter[128 * t : 128 * (t + 1), base + 128 * k : base + 128 * (k + 1)] = hot(
+                        ids == token + 128 * t
+                    )
+        at = pl.ds(pl.multiple_of(position * block, block), block)
+        dqkv[at, 0:256] = dot(scatter[:, 0:group], dsorted[0:group, :]).astype(jnp.bfloat16)
+        dqkv[at, 256:512] = dot(scatter[:, group:], dsorted[group:, :]).astype(jnp.bfloat16)
+        return dot(dqkv[at, :], wsel_ref[...], 1, 1)
+
+    def away(k, carry):
+        part_send[k] = place(4 * (1 - c) + k).astype(jnp.bfloat16)
+        remote(part_send.at[k], part_in.at[k], part_sems, k, sibling).start()
+        return carry
+
+    lax.fori_loop(0, 4, away, 0)
+
+    def here(k, carry):
+        part = place(4 * c + k)
+        remote(part_send.at[k], part_in.at[k], part_sems, k, sibling).wait()
+        total[k // 2, k % 2] = (part + part_in[k].astype(jnp.float32)).astype(jnp.bfloat16)
+        return carry
+
+    lax.fori_loop(0, 4, here, 0)
+    upper, lower = pl.ds(0, block // 2), pl.ds(block // 2, block // 2)
+    a_copy = remote(total.at[:, 1 - x, upper], a_in, part_sems, 4, over_x)
+    b_copy = remote(total.at[1 - zl, :, lower], b_in, part_sems, 5, over_z)
+    a_copy.start()
+    b_copy.start()
+
+    for k in range(width // 128):
+        dw[128 * k : 128 * (k + 1), :] = dot(
+            x_all[:, 128 * k : 128 * (k + 1)], dqkv[...], 0, 0
+        ).astype(jnp.bfloat16)
+    bias_row = jnp.broadcast_to(
+        jnp.sum(dqkv[...].astype(jnp.float32), axis=0, keepdims=True), (16, 512)
+    ).astype(jnp.bfloat16)
+    share = width // 8
+    for d in range(8):
+        for h in range(2):
+            dw_y[h, d, 0:share, :] = dw[share * d : share * (d + 1), 256 * h : 256 * (h + 1)]
+            dw_y[h, d, share : share + 16, :] = bias_row[:, 256 * h : 256 * (h + 1)]
+    over_y_copy = remote(dw_y.at[1 - y], dw_in, dw_sems, 0, over_y)
+    over_y_copy.start()
+
+    a_copy.wait()
+    add_into(2, lambda i: a_in.at[i], lambda i: total.at[i, x, upper])
+    a_next = remote(a_in.at[1 - zl], a_two, part_sems, 6, over_z)
+    a_next.start()
+    b_copy.wait()
+    add_into(2, lambda i: b_in.at[i], lambda i: total.at[zl, i, lower])
+    b_next = remote(b_in.at[1 - x], b_two, part_sems, 7, over_x)
+    b_next.start()
+
+    over_y_copy.wait()
+    add_into(8, lambda i: dw_y.at[y, i], lambda i: dw_in.at[i])
+    dw_copies = []
+    targets = across + [over_x, over_z, peers[2]]
+    flips = [(1, f // 2, f % 2) for f in range(4)] + [(0, 0, 1), (0, 1, 0), (0, 1, 1)]
+    for i, (peer, (fh, fz, fx)) in enumerate(zip(targets, flips)):
+        d = 4 * bits(zh, fh) + 2 * bits(zl, fz) + bits(x, fx)
+        copy = remote(dw_y.at[y, d], dw_all.at[s], dw_sems, 1 + i, peer)
+        copy.start()
+        dw_copies.append(copy)
+    dw_all[s] = dw_y[y, s]
+
+    a_next.wait()
+    b_next.wait()
+    for start, first, second, index in ((0, a_two, a_in, zl), (block // 2, b_two, b_in, x)):
+        at = pl.ds(start, block // 2)
+        grad_my[at, :] = (
+            delta_ref[at, :] + first[...].astype(jnp.float32) + second[index].astype(jnp.float32)
+        ).astype(jnp.bfloat16)
+    home_copy(grad_my, grad_home, 1, True)
+
+    stats_buf[0] = stats_ref[...]
+    stats_peers = (sibling, over_x, over_z, across[0], over_y)
+    for k, peer in enumerate(stats_peers):
+        copy = remote(stats_buf.at[k], stats_in.at[k], stats_sems, k, peer)
+        copy.start()
+        copy.wait()
+        stats_buf[k + 1] = stats_buf[k] + stats_in[k]
+    stats_out[...] = stats_buf[len(stats_peers)]
+
+    for _ in range(parts):
+        next(reduction)
+
+    for copy in dw_copies:
+        copy.wait()
+    for k in range(4):
+        w_all[y, c, k] = (dw_all[k].astype(jnp.float32) + dw_all[4 + k].astype(jnp.float32)).astype(
+            jnp.bfloat16
+        )
+    w_copy = remote(w_all.at[y, c], w_all.at[y, c], dw_sems, 8, over_y)
+    w_copy.start()
+    next(reduction)
+    w_copy.wait()
+    w_copy = remote(w_all.at[:, c], w_all.at[:, c], dw_sems, 9, sibling)
+    w_copy.start()
+    for _ in reduction:
+        pass
+    w_copy.wait()
+    for pair in range(4):
+        at = slice(128 * pair, 128 * pair + 128)
+        low, high = (w_all[0, core, pair].astype(jnp.float32) for core in range(2))
+        gq_ref[:, at] = join(low[:, 0:128], half_roll(high[:, 0:128]))
+        gk_ref[:, at] = join(low[:, 128:256], half_roll(high[:, 128:256]))
+        gv_ref[:, at] = join(half_roll(low[:, 0:128]), high[:, 0:128])
+    for pair in range(2):
+        at = slice(512 + 128 * pair, 640 + 128 * pair)
+        low, high = (
+            w_all[1, 0, 2 * pair + i].astype(jnp.float32) + w_all[1, 1, 2 * pair + i].astype(jnp.float32)
+            for i in range(2)
+        )
+        gq_ref[:, at] = join(half_roll(low[:, 0:128]), high[:, 0:128])
+        gk_ref[:, at] = join(half_roll(low[:, 128:256]), high[:, 128:256])
+        gv_ref[:, at] = join(low[:, 0:128], half_roll(high[:, 0:128]))
+    home_copy(out_my, out_home, 0, False)
+    home_copy(grad_my, grad_home, 1, False)
+
+
+def backward_attention(datt, sorted_rows, prob, order, x_all, wsel, delta, output, stats, grads, parts):
+    block, width = datt.shape
+    group = 8 * block
+    rows = group * 3 // 2
+    row_count = grads.shape[1]
+    q = row_count // 8
+    share = width // 8 + 16
+    low, full = jnp.bfloat16, jnp.float32
+    vmem = pl.BlockSpec(memory_space=pltpu.VMEM)
+    dma = pltpu.SemaphoreType.DMA
+    outs = pl.pallas_call(
+        functools.partial(backward_kernel, parts),
+        out_shape=[
+            jax.ShapeDtypeStruct((block, width), low),
+            jax.ShapeDtypeStruct((block, width), low),
+            jax.ShapeDtypeStruct((2, 2, 2, q, width), low),
+            jax.ShapeDtypeStruct((share, width), full),
+            jax.ShapeDtypeStruct((share, width), full),
+            jax.ShapeDtypeStruct((share, width), full),
+            jax.ShapeDtypeStruct(stats.shape, full),
+        ],
+        in_specs=[vmem] * 9 + [pl.BlockSpec(memory_space=pl.ANY)],
+        out_specs=[vmem] * 7,
+        scratch_shapes=[
+            pltpu.VMEM((8, block, 128), low),
+            pltpu.VMEM((8, block, 128), low),
+            pltpu.VMEM((rows, group), low),
+            pltpu.VMEM((rows, 128), low),
+            pltpu.VMEM((rows, 256), low),
+            pltpu.VMEM((block, rows), low),
+            pltpu.VMEM((group, 512), low),
+            pltpu.VMEM((4, block, width), low),
+            pltpu.VMEM((4, block, width), low),
+            pltpu.VMEM((2, 2, block, width), low),
+            pltpu.VMEM((2, block // 2, width), low),
+            pltpu.VMEM((2, block // 2, width), low),
+            pltpu.VMEM((block // 2, width), low),
+            pltpu.VMEM((block // 2, width), low),
+            pltpu.VMEM((block, width), low),
+            pltpu.VMEM((width, 512), low),
+            pltpu.VMEM((2, 8, share, 256), low),
+            pltpu.VMEM((8, share, 256), low),
+            pltpu.VMEM((8, share, 256), low),
+            pltpu.VMEM((2, 2, 4, share, 256), low),
+            pltpu.VMEM((6,) + stats.shape, full),
+            pltpu.VMEM((5,) + stats.shape, full),
+            pltpu.VMEM((2, 2, 2, 4 * q, width), low),
+            pltpu.VMEM((2, 2, 2, 4 * q, width), low),
+            pltpu.VMEM((2, 2, 2 * q, width), low),
+            pltpu.VMEM((2, 2, 2, q, width), low),
+            pltpu.VMEM((2, 2, 2, q, width), low),
+            pltpu.VMEM((2, 2, q, width), low),
+            pltpu.VMEM((2, q, width), low),
+            dma((7,)),
+            dma((7,)),
+            dma((8,)),
+            dma((8,)),
+            dma((4,)),
+            dma((4,)),
+            dma((10,)),
+            dma((10,)),
+            dma((5,)),
+            dma((5,)),
+            dma((9, parts)),
+            dma((9, parts)),
+            dma((parts,)),
+        ],
+        compiler_params=pltpu.CompilerParams(
+            collective_id=2, has_side_effects=True, vmem_limit_bytes=60 << 20
+        ),
+        name="backward_attention",
+    )(
+        datt,
+        sorted_rows,
+        prob,
+        order,
+        x_all.reshape(group, width),
+        wsel,
+        delta,
+        output,
+        stats,
+        grads.reshape(2, 2, 2, row_count, width),
+    )
+    out_home, grad_home, reduced, gq, gk, gv, totals = outs
+    return out_home, grad_home, reduced.reshape(row_count, width), gq, gk, gv, totals
 
 
 def body(
@@ -351,7 +1279,168 @@
     return (output, gradient_tokens) + tuple(summed) + (cluster_stats,)
 
 
+def square_body(
+    tokens,
+    segments,
+    orders,
+    owners,
+    query_weight,
+    query_bias,
+    key_weight,
+    value_weight,
+    value_bias,
+    out_weight,
+    out_bias,
+    first_gain,
+    first_shift,
+    inner_weight,
+    inner_bias,
+    outer_weight,
+    outer_bias,
+    second_gain,
+    second_shift,
+    cotangent,
+):
+    own_index = lax.axis_index("seq")
+    position = 4 * lax.rem(lax.axis_index("rep"), 2) + lax.rem(own_index, 4)
+    head_count = orders.shape[1]
+    model_width = tokens.shape[2]
+    seq_count = 8
+    owner_hot = (owners[0][:, :, None] == jnp.arange(128, dtype=jnp.int32)).astype(jnp.float32)
+    biases = jnp.concatenate(
+        [
+            jnp.broadcast_to(bias.astype(jnp.float32), (8, model_width))
+            for bias in (query_bias, jnp.zeros_like(query_bias), value_bias)
+        ]
+    )
+    attended_rows, x_all, my_cotangent, sorted_rows, prob, wsel, order, stats = forward_attention(
+        tokens[0],
+        cotangent[0],
+        segments,
+        orders[0],
+        owner_hot.reshape(-1, 128),
+        query_weight,
+        key_weight,
+        value_weight,
+        biases,
+    )
+    flat_tokens = lax.dynamic_index_in_dim(x_all, position, 0, keepdims=False)
+    branch = jnp.dot(
+        attended_rows, out_weight, preferred_element_type=jnp.float32
+    ) + out_bias.astype(jnp.float32)
+    first_out, normed_one, root_one = norm_forward(
+        flat_tokens.astype(jnp.float32) + branch, first_gain, first_shift
+    )
+    first_low = first_out.astype(jnp.bfloat16)
+    inner_sum = jnp.dot(
+        first_low, inner_weight, preferred_element_type=jnp.float32
+    ) + inner_bias.astype(jnp.float32)
+    activated, gelu_pull = jax.vjp(exact_gelu, inner_sum)
+    activated_low = activated.astype(jnp.bfloat16)
+    second = jnp.dot(
+        activated_low, outer_weight, preferred_element_type=jnp.float32
+    ) + outer_bias.astype(jnp.float32)
+    result, normed_two, root_two = norm_forward(first_out + second, second_gain, second_shift)
+    output = result.astype(jnp.bfloat16)
+    upstream = my_cotangent.astype(jnp.float32)
+    gradient_second_gain = jnp.sum(upstream * normed_two, axis=0)
+    gradient_second_shift = jnp.sum(upstream, axis=0)
+    delta_two = norm_backward(upstream, normed_two, root_two, second_gain)
+    delta_second = delta_two.astype(jnp.bfloat16)
+    gradient_outer_bias = jnp.sum(delta_second.astype(jnp.float32), axis=0)
+    gradient_outer_weight = jnp.einsum(
+        "tf,td->fd", activated_low, delta_second, preferred_element_type=jnp.float32
+    )
+    delta_activated = jnp.einsum(
+        "td,fd->tf", delta_second, outer_weight, preferred_element_type=jnp.float32
+    )
+    delta_inner = gelu_pull(delta_activated)[0].astype(jnp.bfloat16)
+    gradient_inner_bias = jnp.sum(delta_inner.astype(jnp.float32), axis=0)
+    gradient_inner_weight = jnp.einsum(
+        "td,tf->df", first_low, delta_inner, preferred_element_type=jnp.float32
+    )
+    delta_first = delta_two + jnp.einsum(
+        "tf,df->td", delta_inner, inner_weight, preferred_element_type=jnp.float32
+    )
+    gradient_first_gain = jnp.sum(delta_first * normed_one, axis=0)
+    gradient_first_shift = jnp.sum(delta_first, axis=0)
+    delta_one = norm_backward(delta_first, normed_one, root_one, first_gain)
+    delta_branch = delta_one.astype(jnp.bfloat16)
+    gradient_out_bias = jnp.sum(delta_branch.astype(jnp.float32), axis=0)
+    gradient_out_weight = jnp.einsum(
+        "td,te->de", attended_rows, delta_branch, preferred_element_type=jnp.float32
+    )
+    delta_attended = jnp.einsum(
+        "te,de->td", delta_branch, out_weight, preferred_element_type=jnp.float32
+    ).astype(jnp.bfloat16)
+    weights_out = [
+        gradient_out_weight.reshape(8, -1, model_width),
+        gradient_inner_weight.reshape(8, model_width // 8, -1, model_width)
+        .transpose(0, 2, 1, 3)
+        .reshape(8, -1, model_width),
+        gradient_outer_weight.reshape(8, -1, model_width),
+    ]
+    vectors = jnp.concatenate(
+        [
+            vector.reshape(8, -1)
+            for vector in (
+                gradient_out_bias,
+                gradient_first_gain,
+                gradient_first_shift,
+                gradient_inner_bias,
+                gradient_outer_bias,
+                gradient_second_gain,
+                gradient_second_shift,
+            )
+        ],
+        axis=1,
+    )
+    used = sum(part.shape[1] for part in weights_out)
+    total_rows = -(-(used + 2) // 128) * 128
+    spare = (total_rows - used) * model_width - vectors.shape[1]
+    vectors = jnp.pad(vectors, ((0, 0), (0, spare))).reshape(8, -1, model_width)
+    grads = jnp.concatenate([part.astype(jnp.bfloat16) for part in weights_out + [vectors]], axis=1)
+    out_home, grad_home, summed, query_g, key_g, value_g, totals = backward_attention(
+        delta_attended, sorted_rows, prob, order, x_all, wsel, delta_one, output, stats, grads, 2
+    )
+    summed = summed.astype(jnp.float32)
+    share = model_width // 8
+    inner_count = inner_weight.shape[1] // model_width
+    marks = [0]
+    for part in weights_out:
+        marks.append(marks[-1] + part.shape[1])
+    out_g, inner_g, outer_g = (summed[marks[i] : marks[i + 1]] for i in range(3))
+    inner_g = inner_g.reshape(inner_count, share, model_width).transpose(1, 0, 2).reshape(share, -1)
+    flat = summed[marks[3] :].reshape(-1)
+    sizes = [share] * 3 + [share * inner_count] + [share] * 3
+    ends = [0]
+    for size in sizes:
+        ends.append(ends[-1] + size)
+    pick = [flat[ends[i] : ends[i + 1]] for i in range(7)]
+    return (
+        out_home[None],
+        grad_home[None],
+        query_g[:share],
+        lax.dynamic_slice_in_dim(query_g[share], share * own_index, share),
+        key_g[:share],
+        value_g[:share],
+        lax.dynamic_slice_in_dim(value_g[share], share * own_index, share),
+        out_g,
+        pick[0],
+        pick[1],
+        pick[2],
+        inner_g,
+        pick[3],
+        outer_g,
+        pick[4],
+        pick[5],
+        pick[6],
+        totals[:, :head_count, :seq_count],
+    )
+
+
 def solution(mesh):
+    square = mesh.shape["seq"] == 8 and mesh.shape["rep"] == 4
     placed = (
         P("rep", "seq", None),
         P("rep", "seq"),
@@ -375,7 +1464,7 @@
         P("rep", "seq", None),
     )
     return jax.shard_map(
-        body,
+        square_body if square else body,
         mesh=mesh,
         in_specs=placed,
         out_specs=(

time: 922 us -> 277 us (0.30)
  waiting for transfers between devices: 567 us -> 0 us
  Pallas kernels: 0 us -> 198 us
  blocking collectives: 133 us -> 0 us
  local copies, waits for them, and re-layouts: 73.1 us -> 30.3 us
  matrix products: 61.9 us -> 30.8 us
  other arithmetic: 41.4 us -> 16.7 us
  starting transfers between devices: 21.9 us -> 0 us
  between operations: 17.1 us -> 1.06 us
    reduce_scatter x3 -> x0, waiting for transfers between devices: 328 us -> none  [the longest x1 164 us: body(): lax.psum_scatter(gradient_inner_weight, 'seq', scatter_dimension=0, tiled...]
    pallas_call x0 -> x2, Pallas kernels: none -> 198 us  [the longest x1 134 us: backward_attention(): pl.pallas_call(functools.partial(backward_kernel, parts), out_shape=[jax....]
    unnamed x10 -> x0, waiting for transfers between devices: 182 us -> none
    all_to_all x4 -> x0, waiting for transfers between devices: 56.8 us -> none  [the longest x1 34.1 us: body(): lax.all_to_all(send_values, 'seq', split_axis=0, concat_axis=0, tiled=True)]
    all_to_all x1 -> x0, blocking collectives: 50.3 us -> none  [body(): lax.all_to_all(leaving_grads, 'seq', split_axis=0, concat_axis=0, tiled=T...]
    psum x2 -> x0, blocking collectives: 45.6 us -> none  [the longest x1 39.9 us: body(): cluster_stats = lax.psum(per_head[:, :, None] * column, ('seq', 'rep'))]
    unnamed x1 -> x0, blocking collectives: 37.3 us -> none
    dot_general x28 -> x9, matrix products: 61.9 us -> 30.8 us  [the longest x1 9.91 us: square_body(): jnp.dot(first_low, inner_weight, preferred_element_type=jnp.float32)]
  transfers between devices with their start and end apart: 11 -> 0, of which waited for: 8 -> 0; matrix products, arithmetic and copies ran while one was open for 11% -> 0% of each run, Pallas kernels for 0% -> 0%
where the time goes in v2:
time: 277 us
  Pallas kernels  198 us (71%)
  matrix products  30.8 us (11%)
  local copies, waits for them, and re-layouts  30.3 us (11%)
  other arithmetic  16.7 us (6%)
    pallas_call x1, Pallas kernels, backward_attention(): pl.pallas_call(functools.partial(backward_kernel, parts), out_shape=[jax....  134 us
    pallas_call x1, Pallas kernels, forward_attention(): pl.pallas_call(forward_kernel, out_shape=[jax.ShapeDtypeStruct((block, wi...  63.9 us
    convert_element_type x2, local copies, waits for them, and re-layouts, square_body(): part.astype(jnp.bfloat16)  15.3 us
    dot_general x1, matrix products, square_body(): jnp.dot(first_low, inner_weight, preferred_element_type=jnp.float32)  9.91 us
    concatenate x1, other arithmetic, square_body(): jnp.concatenate([part.astype(jnp.bfloat16) for part in weights_out + [vec...  9.54 us

profile of v2, /device:TPU:0, one launch (start us, length us, event | category | flops | bytes accessed | tf_op | source)
XLA Modules:
  0.0 276.8 jit_solution(676047210262330193)
XLA Ops:
  0.7 1.7 copy.45
  2.4 0.7 broadcast_in_dim.10
  3.8 0.7 pad_maximum_fusion.1.bias_ref
  4.5 0.7 reduce.4
  5.3 0.7 fusion.16.hot_ref
  6.1 63.9 %forward_attention.1 = (bf16[256,768]{1,0:T(8,128)(2,1)}, bf16[8,256,768]{2,1,0:T(8,128)(2,1)}, bf16[256,768]{1,0:T(8,128)(2,1)}, bf16[3072,256]{1,0:T(8,128)(2,...) custom-call(bf16[256,768]{1,0:T(8,128)(2,1)} %bitcast.53, ...), custom_call_target="tpu_custom_call" | custom-call | tf_op jit(solution)/shard_map/forward_attention/pallas_call | solution.py:491
  70.0 1.8 fusion.32
  72.2 9.9 %multiply_convert_fusion = (bf16[256,3072]{1,0:T(8,128)(2,1)S(1)}, f32[256,3072]{1,0:T(8,128)S(1)}, f32[256,3072]{1,0:T(8,128)S(1)}) fusion(f32[3072]{0:T(1024)S(1)} %convert_element_type.121, bf16[768,3072]{1,0:T(8,128)(2,1)} %param.33, f32[256,768]{1,0:T(8,128)S(1)} %get-tuple-element.90, f32[768]{0:T(1024)S(1)} %convert_element_type.119, ...), kind=kOutput, calls=%fused_computation.7 | convolution fusion | flops 1260847104 | bytes 13389824 | tf_op jit(solution)/shard_map/dot_general | solution.py:1335
  82.2 1.5 fusion.33
  84.0 1.2 fusion.14
  85.1 1.0 convert_reduce_fusion.1
  86.1 2.8 fusion.34
  88.9 1.1 copy-done.6
  90.0 3.8 %convolution_convert_fusion.1 = bf16[768,3072]{1,0:T(8,128)(2,1)} fusion(bf16[256,3072]{1,0:T(8,128)(2,1)S(1)} %get-tuple-element.96, f32[256,768]{1,0:T(8,128)S(1)} %get-tuple-element.90, f32[768]{0:T(1024)S(1)} %convert_element_type.119, f32[768]{0:T(1024)S(1)} %convert_element_type.118, f32[256]{0:T(256)S(1)} %add_rsqrt_fusion.1, ...), kind=kOutput, calls=%fused_computation.2 | convolution fusion | flops 1211301888 | bytes 7086080 | tf_op jit(solution)/shard_map/td,tf->df/dot_general | solution.py:1359
  93.8 9.7 %convert_element_type.135 = bf16[8,96,4,768]{3,2,1,0:T(4,128)(2,1)} reshape(bf16[768,3072]{1,0:T(8,128)(2,1)} %convolution_convert_fusion.1) | data formatting | bytes 9437184 | tf_op jit(solution)/shard_map/convert_element_type | solution.py:1402
  103.5 5.6 %copy.38 = bf16[8,96,4,768]{3,1,2,0:T(8,128)(2,1)} copy(bf16[8,96,4,768]{3,2,1,0:T(4,128)(2,1)} %convert_element_type.135) | data formatting | bytes 9437184 | tf_op jit(solution)/shard_map/convert_element_type | solution.py:1402
  109.1 4.7 %multiply_reduce_fusion = (bf16[768]{0:T(1024)(128)(2,1)}, f32[256]{0:T(256)S(1)}, f32[256]{0:T(256)S(1)}, bf16[768]{0:T(1024)(128)(2,1)}, f32[256,768]{1,0:T(8,128)S(1)}) fusion(f32[256,768]{1,0:T(8,128)S(1)} %get-tuple-element.90, f32[256]{0:T(256)S(1)} %add_rsqrt_fusion.1, f32[256]{0:T(256)S(1)} %broadcast_multiply_fusion.5, ...), kind=kOutput, calls=%fused_computation.38 | convolution fusion | flops 1209923584 | bytes 8660992 | tf_op jit(solution)/shard_map/tf,df->td/dot_general | solution.py:1362
  113.7 0.9 convert_reduce_fusion
  114.6 1.5 convolution_convert_fusion.2
  116.2 3.6 %convolution_convert_fusion = bf16[3072,768]{1,0:T(8,128)(2,1)} fusion(bf16[256,3072]{1,0:T(8,128)(2,1)S(1)} %copy-done.3, f32[256,768]{1,0:T(8,128)S(1)} %get-tuple-element.74), kind=kOutput, calls=%fused_computation.1 | convolution fusion | flops 1210515456 | bytes 7077888 | tf_op jit(solution)/shard_map/tf,td->fd/dot_general | solution.py:1351
  120.5 9.5 %pad_maximum_fusion.g_ref = bf16[2,2,2,896,768]{4,3,2,1,0:T(8,128)(2,1)} fusion(bf16[2,2,2,32,768]{4,3,2,1,0:T(8,128)(2,1)S(1)} %bitcast.50, bf16[2,2,2,384,768]{4,3,2,1,0:T(8,128)(2,1)} %bitcast.44, bf16[2,2,2,384,768]{4,3,2,1,0:T(8,128)(2,1)} %bitcast.45, bf16[2,2,2,96,768]{4,3,2,1,0:T(8,128)(2,1)} %bitcast.47), kind=kLoop, calls=%fused_computation | loop fusion | flops 44040192 | bytes 22020096 | tf_op jit(solution)/shard_map/concatenate | solution.py:1402
  130.1 1.3 convolution_convert_fusion.3.datt_ref
  131.3 134.1 %backward_attention.1 = (bf16[256,768]{1,0:T(8,128)(2,1)}, bf16[256,768]{1,0:T(8,128)(2,1)}, bf16[2,2,2,112,768]{4,3,2,1,0:T(8,128)(2,1)}, f32[112,768]{1,0:T(8,...) custom-call(bf16[256,768]{1,0:T(8,128)(2,1)} %convolution_convert_fusion.3.datt_ref, ...), custom_call_target="tpu_custom_call" | custom-call | tf_op jit(solution)/shard_map/backward_attention/pallas_call | solution.py:958
  265.4 1.5 bitcast_convert_fusion
  266.9 1.2 fusion.30
  268.1 1.1 copy.42
  269.3 0.7 slice.68
  271.3 0.7 slice.51
  272.0 0.7 slice.53
  272.7 0.7 slice.54
  275.3 0.7 copy.48
  276.1 0.7 copy.49
  (97 shorter events, 5.3 us)
Async XLA Ops:
  0.7 69.3 %copy-start = (bf16[768,768]{1,0:T(8,128)(2,1)S(1)}, bf16[768,768]{1,0:T(8,128)(2,1)}, u32[]{:S(2)}) copy-start(bf16[768,768]{1,0:T(8,128)(2,1)} %param.29) | copy-start | bytes 3538948
  0.7 69.3 %copy-start.19 = (bf16[768]{0:T(1024)(128)(2,1)S(1)}, bf16[768]{0:T(1024)(128)(2,1)}, u32[]{:S(2)}) copy-start(bf16[768]{0:T(1024)(128)(2,1)} %param.30) | copy-start | bytes 4612
  6.1 66.0 %copy-start.20 = (bf16[768]{0:T(1024)(128)(2,1)S(1)}, bf16[768]{0:T(1024)(128)(2,1)}, u32[]{:S(2)}) copy-start(bf16[768]{0:T(1024)(128)(2,1)} %param.31) | copy-start | bytes 4612
  6.1 66.0 %copy-start.21 = (bf16[768]{0:T(1024)(128)(2,1)S(1)}, bf16[768]{0:T(1024)(128)(2,1)}, u32[]{:S(2)}) copy-start(bf16[768]{0:T(1024)(128)(2,1)} %param.32) | copy-start | bytes 4612
  6.1 66.1 %copy-start.18 = (bf16[3072]{0:T(1024)(128)(2,1)S(1)}, bf16[3072]{0:T(1024)(128)(2,1)}, u32[]{:S(2)}) copy-start(bf16[3072]{0:T(1024)(128)(2,1)} %param.34) | copy-start | bytes 18436
  70.0 12.1 %slice-start = ((s8[4718592]{0:T(1024)(128)(4,1)}), s8[4194304]{0:T(1024)(128)(4,1)S(1)}, s32[]{:S(2)}) async-start(s8[4718592]{0:T(1024)(128)(4,1)} %bitcast.58), calls=%async_computation | async-start | bytes 8388608
  72.1 10.0 %copy-start.22 = (bf16[768]{0:T(1024)(128)(2,1)S(1)}, bf16[768]{0:T(1024)(128)(2,1)}, u32[]{:S(2)}) copy-start(bf16[768]{0:T(1024)(128)(2,1)} %param.36) | copy-start | bytes 4612
  72.2 10.0 %slice-start.1 = ((s8[4718592]{0:T(1024)(128)(4,1)}), s8[524288]{0:T(1024)(128)(4,1)S(1)}, s32[]{:S(2)}) async-start(s8[4718592]{0:T(1024)(128)(4,1)} %bitcast.58), calls=%async_computation.1 | async-start | bytes 1048576
  82.1 1.6 copy-start.2
  82.1 1.8 copy-start.23
  82.2 1.8 copy-start.24
  82.2 1.8 copy-start.5
  88.9 1.1 copy-start.6
  103.5 5.6 %copy-start.7 = (bf16[256,3072]{1,0:T(8,128)(2,1)S(1)}, bf16[256,3072]{1,0:T(8,128)(2,1)}, u32[]{:S(2)}) copy-start(bf16[256,3072]{1,0:T(8,128)(2,1)} %copy-done.6) | copy-start | bytes 4718596
  109.1 5.5 %copy-start.4 = (bf16[256,768]{1,0:T(8,128)(2,1)S(1)}, bf16[256,768]{1,0:T(8,128)(2,1)}, u32[]{:S(2)}) copy-start(bf16[256,768]{1,0:T(8,128)(2,1)} %get-tuple-element.34) | copy-start | bytes 1179652
  113.7 2.4 copy-start.3
  114.6 15.5 %copy-start.1 = (f32[256,768]{1,0:T(8,128)}, f32[256,768]{1,0:T(8,128)S(1)}, u32[]{:S(2)}) copy-start(f32[256,768]{1,0:T(8,128)S(1)} %get-tuple-element.76.delta_ref) | copy-start | bytes 2359300
  116.1 3.6 %copy-start.16 = (bf16[768]{0:T(1024)(128)(2,1)S(1)}, bf16[768]{0:T(1024)(128)(2,1)}, u32[]{:S(2)}) copy-start(bf16[768]{0:T(1024)(128)(2,1)} %get-tuple-element.75) | copy-start | bytes 4612
  116.2 3.7 %copy-start.26 = (bf16[768]{0:T(1024)(128)(2,1)S(1)}, bf16[768]{0:T(1024)(128)(2,1)}, u32[]{:S(2)}) copy-start(bf16[768]{0:T(1024)(128)(2,1)} %get-tuple-element.66) | copy-start | bytes 4612
  116.2 3.8 %copy-start.25 = (bf16[768]{0:T(1024)(128)(2,1)S(1)}, bf16[768]{0:T(1024)(128)(2,1)}, u32[]{:S(2)}) copy-start(bf16[768]{0:T(1024)(128)(2,1)} %get-tuple-element.71) | copy-start | bytes 4612
  116.2 3.9 %copy-start.17 = (bf16[3072]{0:T(1024)(128)(2,1)S(1)}, bf16[3072]{0:T(1024)(128)(2,1)}, u32[]{:S(2)}) copy-start(bf16[3072]{0:T(1024)(128)(2,1)} %get-tuple-element.95) | copy-start | bytes 18436
  116.2 3.9 %copy-start.15 = (bf16[768]{0:T(1024)(128)(2,1)S(1)}, bf16[768]{0:T(1024)(128)(2,1)}, u32[]{:S(2)}) copy-start(bf16[768]{0:T(1024)(128)(2,1)} %get-tuple-element.73) | copy-start | bytes 4612
  116.2 4.0 %copy-start.14 = (bf16[768]{0:T(1024)(128)(2,1)S(1)}, bf16[768]{0:T(1024)(128)(2,1)}, u32[]{:S(2)}) copy-start(bf16[768]{0:T(1024)(128)(2,1)} %get-tuple-element.82) | copy-start | bytes 4612
  266.9 4.3 %copy-start.11 = (f32[112,768]{1,0:T(8,128)S(1)}, f32[112,768]{1,0:T(8,128)}, u32[]{:S(2)}) copy-start(f32[112,768]{1,0:T(8,128)} %get-tuple-element.43) | copy-start | bytes 1032196
  268.1 3.9 %copy-start.12 = (f32[112,768]{1,0:T(8,128)S(1)}, f32[112,768]{1,0:T(8,128)}, u32[]{:S(2)}) copy-start(f32[112,768]{1,0:T(8,128)} %get-tuple-element.44) | copy-start | bytes 1032196
  268.1 4.6 %copy-start.10 = (f32[112,768]{1,0:T(8,128)S(1)}, f32[112,768]{1,0:T(8,128)}, u32[]{:S(2)}) copy-start(f32[112,768]{1,0:T(8,128)} %get-tuple-element.45) | copy-start | bytes 1032196
  268.1 6.5 %copy-start.13 = (f32[2,16,128]{2,1,0:T(8,128)S(1)}, f32[2,16,128]{2,1,0:T(8,128)}, u32[]{:S(2)}) copy-start(f32[2,16,128]{2,1,0:T(8,128)} %get-tuple-element.47) | copy-start | bytes 49156
  268.1 7.2 %copy-start.9 = (bf16[256,768]{1,0:T(8,128)(2,1)S(1)}, bf16[256,768]{1,0:T(8,128)(2,1)}, u32[]{:S(2)}) copy-start(bf16[256,768]{1,0:T(8,128)(2,1)} %get-tuple-element.41) | copy-start | bytes 1179652
  268.1 7.9 %copy-start.8 = (bf16[256,768]{1,0:T(8,128)(2,1)S(1)}, bf16[256,768]{1,0:T(8,128)(2,1)}, u32[]{:S(2)}) copy-start(bf16[256,768]{1,0:T(8,128)(2,1)} %get-tuple-element.42) | copy-start | bytes 1179652

commit v3 on v2

--- a/solution.py
+++ b/solution.py
@@ -111,6 +111,9 @@
 MESH = pl.DeviceIdType.MESH
 
 
+UNROLL = 4
+
+
 def half_roll(block):
     return jnp.concatenate([block[:, 64:], block[:, :64]], axis=1)
 
@@ -198,17 +201,15 @@
     return jnp.where(lanes(low_lanes.shape) < 64, low_lanes, high_lanes)
 
 
-def pick_columns(refs, j, c, add_zero):
-    def slab(ref, index):
-        return ref[:, pl.ds(pl.multiple_of(index * 128, 128), 128)].astype(jnp.float32)
-
-    first = [slab(ref, j) for ref in refs]
-    other = [slab(ref, 4 + j // 2) for ref in refs]
-    zero = jnp.zeros_like(first[0])
-    q1, v1 = select_head(first[0], c, 0), select_head(first[2], c, 1)
-    k1 = select_head(first[1], c, 0)
-    v2, q2 = select_head(other[2], j % 2, 0), select_head(other[0], j % 2, 1)
-    k2 = select_head(other[1], j % 2, 1)
+def pick_columns(pairs, j, c):
+    (q_one, q_two), (k_one, k_two), (v_one, v_two) = pairs
+    zero = jnp.zeros_like(q_one)
+    q1, v1, k1 = select_head(q_one, c, 0), select_head(v_one, c, 1), select_head(k_one, c, 0)
+    v2, q2, k2 = (
+        select_head(v_two, j % 2, 0),
+        select_head(q_two, j % 2, 1),
+        select_head(k_two, j % 2, 1),
+    )
     return join(q1, v1), join(k1, zero), join(v2, q2), join(zero, k2)
 
 
@@ -217,25 +218,34 @@
     cot_ref,
     seg_ref,
     orders_ref,
-    hot_ref,
-    wq_ref,
-    wk_ref,
-    wv_ref,
-    bias_ref,
+    owners_ref,
+    query_bias_ref,
+    value_bias_ref,
+    wq_hbm,
+    wk_hbm,
+    wv_hbm,
     att_ref,
-    x_all,
+    x_my,
     cot_my,
-    sorted_ref,
-    prob_ref,
     wsel_ref,
     order_ref,
     stats_ref,
+    x_hbm,
+    sorted_hbm,
+    prob_hbm,
+    x_all,
+    sorted_ref,
+    prob_ref,
+    weights,
     orders_in,
-    hot_in,
+    owners_in,
+    owner_pad,
     seg_src,
     seg_all,
+    bias_rows,
     bias_sel,
     tok,
+    partial,
     gather,
     scatter,
     att_sorted,
@@ -251,11 +261,12 @@
     seg_recv,
     back_send,
     back_recv,
+    local_sem,
 ):
     zh, zl, x, y, c = coordinates()
     j = 2 * zl + x
     p = 4 * c + j
-    block = tokens_ref.shape[0]
+    block, width = tokens_ref.shape
     group = 8 * block
     scale = 0.125
     swap = (swap_send, swap_recv)
@@ -270,95 +281,151 @@
 
     swap_peer = device(1 - zh, zl, x, y, 1 - c)
     peers = [member(flip)[0] for flip in range(1, 8)]
-    greet(peers + [swap_peer])
     sibling = peers[3]
     over_x, over_z = peers[0], peers[1]
     matched = c == zh
 
+    slabs = [
+        pltpu.make_async_copy(
+            src.at[:, pl.ds(pl.multiple_of(index * 128, 128), 128)],
+            weights.at[i, slot],
+            local_sem.at[3 * slot + i],
+        )
+        for i, src in enumerate((wq_hbm, wk_hbm, wv_hbm))
+        for slot, index in enumerate((j, 4 + j // 2))
+    ]
+    for copy in slabs:
+        copy.start()
+    greet(peers + [swap_peer])
     seg_src[...] = jnp.broadcast_to(seg_ref[...], seg_src.shape)
     table_copies = [
         remote(orders_ref, orders_in, swap, 0, sibling),
-        remote(hot_ref, hot_in, swap, 1, sibling),
+        remote(owners_ref, owners_in, swap, 1, sibling),
     ]
     for copy in table_copies:
         copy.start()
     p_swap = 4 * (1 - c) + j
-    pairs = [
-        (tokens_ref, x_all.at[p_swap], x_all.at[p]),
-        (seg_src, seg_all.at[p_swap], seg_all.at[p]),
-        (cot_ref, cot_my, cot_my),
-    ]
+    halves = [pl.ds(i * (block // 2), block // 2) for i in range(2)]
+    pairs = [(tokens_ref.at[at], x_all.at[p_swap, at], x_all.at[p, at]) for at in halves]
+    pairs.insert(0, (seg_src, seg_all.at[p_swap], seg_all.at[p]))
+    pairs.append((cot_ref, cot_my, cot_my))
     swaps = [remote(src, dst, swap, 2 + i, swap_peer) for i, (src, dst, _) in enumerate(pairs)]
     locals_ = [
-        pltpu.make_async_copy(src, own, swap_recv.at[5 + i]) for i, (src, _, own) in enumerate(pairs)
+        pltpu.make_async_copy(src, own, swap_recv.at[6 + i]) for i, (src, _, own) in enumerate(pairs)
     ]
+
+    px, pz, pd = member(1)[1], member(2)[1], member(3)[1]
+
+    def share_block(index, position, i, peer):
+        view = x_all.at[position, halves[i]]
+        return remote(view, view, ring, index, peer)
+
+    own_to_x = [share_block(i, p, i, over_x) for i in range(2)]
+    own_to_z = [share_block(2 + i, p, i, over_z) for i in range(2)]
+    own_to_s = [share_block(4 + i, p, i, sibling) for i in range(2)]
+    x_to_z = share_block(6, px, 0, over_z)
+    z_to_x = share_block(7, pz, 1, over_x)
+    x_to_s = [share_block(8 + i, px, i, sibling) for i in range(2)]
+    z_to_s = [share_block(10 + i, pz, i, sibling) for i in range(2)]
+    d_to_s = [share_block(12 + i, pd, i, sibling) for i in range(2)]
+    seg_copies = [
+        remote(seg_all.at[p], seg_all.at[p], seg_sems, flip - 1, peers[flip - 1]) for flip in range(1, 8)
+    ]
+    opposite = jnp.logical_not(matched)
+
+    def own_half(i, arrivals):
+        arrivals[1 + i].wait()
+        own_to_x[i].start()
+        own_to_z[i].start()
+        own_to_s[i].start()
+
+    def segments_out(arrivals):
+        arrivals[0].wait()
+        for copy in seg_copies:
+            copy.start()
+
+    def forward_first():
+        own_to_x[0].wait()
+        x_to_z.start()
+        x_to_s[0].start()
+        own_to_z[0].wait()
+        z_to_s[0].start()
+
+    def forward_second():
+        own_to_z[1].wait()
+        z_to_x.start()
+        z_to_s[1].start()
+        own_to_x[1].wait()
+        x_to_s[1].start()
+
+    def forward_last():
+        x_to_z.wait()
+        d_to_s[0].start()
+        z_to_x.wait()
+        d_to_s[1].start()
+
+    def wait_sibling():
+        for copy in own_to_s + x_to_s + z_to_s + d_to_s:
+            copy.wait_recv()
 
     @pl.when(matched)
     def _():
         for copy in locals_:
             copy.start()
-
-    @pl.when(jnp.logical_not(matched))
+        segments_out(locals_)
+        own_half(0, locals_)
+        own_half(1, locals_)
+
+    @pl.when(opposite)
     def _():
-        for copy in swaps:
+        for copy in swaps[:3]:
             copy.start()
 
-    tiles = pick_columns((wq_ref, wk_ref, wv_ref), j, c, None)
+    for copy in slabs:
+        copy.wait()
+    tiles = pick_columns([[weights[i, slot].astype(jnp.float32) for slot in range(2)] for i in range(3)], j, c)
     for i, tile in enumerate(tiles):
         wsel_ref[:, 128 * i : 128 * (i + 1)] = tile.astype(jnp.bfloat16)
-    bias_tiles = pick_columns(
-        (bias_ref.at[pl.ds(0, 8)], bias_ref.at[pl.ds(8, 8)], bias_ref.at[pl.ds(16, 8)]), j, c, None
-    )
-    for i, tile in enumerate(bias_tiles):
-        bias_sel[:, 128 * i : 128 * (i + 1)] = tile
+    for i, ref in enumerate((query_bias_ref, None, value_bias_ref)):
+        row = jnp.zeros((1, width), jnp.float32) if ref is None else ref[...].astype(jnp.float32).reshape(1, width)
+        bias_rows[i : i + 1, :] = row
+    bias_pairs = [
+        [bias_rows[i : i + 1, pl.ds(pl.multiple_of(index * 128, 128), 128)] for index in (j, 4 + j // 2)]
+        for i in range(3)
+    ]
+    for i, tile in enumerate(pick_columns(bias_pairs, j, c)):
+        bias_sel[0:1, 128 * i : 128 * (i + 1)] = tile
 
     for copy in table_copies:
         copy.wait()
     h1, h2 = 2 * j + c, 8 + j
     for i, h in enumerate((h1, h2)):
-        own, other = orders_ref[pl.ds(h, 1), :], orders_in[pl.ds(h, 1), :]
-        order_ref[i : i + 1, :] = jnp.where(matched, own, other)
+        order_ref[i : i + 1, :] = jnp.where(matched, orders_ref[h], orders_in[h])
     half = 1024 * c
+
+    build_gather(order_ref, 0, 0, group, gather.at[pl.ds(0, group)])
 
     @pl.when(matched)
     def _():
-        for i in (0, 1):
-            locals_[i].wait()
-
-    @pl.when(jnp.logical_not(matched))
+        forward_first()
+        forward_second()
+
+    @pl.when(opposite)
     def _():
-        for i in (0, 1):
-            swaps[i].wait()
-
-    px, pz, pd = member(1)[1], member(2)[1], member(3)[1]
-    ps, psx, psz, psd = (member(flip)[1] for flip in (4, 5, 6, 7))
-    own = x_all.at[p]
-    to_x = remote(own, own, ring, 0, over_x)
-    to_z = remote(own, own, ring, 1, over_z)
-    to_s = remote(own, own, ring, 2, sibling)
-    for copy in (to_x, to_z, to_s):
-        copy.start()
-    seg_copies = []
-    for flip in range(1, 8):
-        copy = remote(seg_all.at[p], seg_all.at[p], seg_sems, flip - 1, peers[flip - 1])
-        copy.start()
-        seg_copies.append(copy)
-
-    build_gather(order_ref, 0, 0, group, gather.at[pl.ds(0, group)])
-    to_x.wait()
-    upper, lower = pl.ds(0, block // 2), pl.ds(block // 2, block // 2)
-    x_half = remote(x_all.at[px, upper], x_all.at[px, upper], ring, 3, over_z)
-    x_half.start()
-    x_to_s = remote(x_all.at[px], x_all.at[px], ring, 4, sibling)
-    x_to_s.start()
-    to_z.wait()
-    z_half = remote(x_all.at[pz, lower], x_all.at[pz, lower], ring, 5, over_x)
-    z_half.start()
-    z_to_s = remote(x_all.at[pz], x_all.at[pz], ring, 6, sibling)
-    z_to_s.start()
+        segments_out(swaps)
+        own_half(0, swaps)
+
     build_gather(order_ref, 1, half, group // 2, gather.at[pl.ds(group, group // 2)])
-    for copy in seg_copies:
-        copy.wait()
+
+    @pl.when(matched)
+    def _():
+        forward_last()
+
+    @pl.when(opposite)
+    def _():
+        own_half(1, swaps)
+        swaps[3].start()
+        forward_first()
 
     def project(position):
         at = pl.ds(pl.multiple_of(position * block, block), block)
@@ -375,39 +442,56 @@
         tok[at, 256:384] = low[:, 256:384]
         tok[at, 384:512] = jnp.where(lane < 64, seg_hot, low[:, 384:512])
 
-    project(p)
-    project(px)
-    project(pz)
-    to_s.wait()
-    project(ps)
-    x_half.wait()
-    z_half.wait()
-    d_to_s = remote(x_all.at[pd], x_all.at[pd], ring, 7, sibling)
-    d_to_s.start()
-    project(pd)
-    x_to_s.wait()
-    project(psx)
-    z_to_s.wait()
-    project(psz)
+    step = 512
+    early, late = group // 2 * zh, group // 2 * (1 - zh)
+
+    def gather_rows(start, add):
+        tokens = pl.ds(pl.multiple_of(start, group // 2), group // 2)
+
+        def one(first, columns):
+            def body(k, carry):
+                at = pl.ds(pl.multiple_of(k * step, step), step)
+                rows = dot(gather[at, tokens], tok[tokens, columns])
+                if add:
+                    sorted_ref[at, :] = (rows + partial[at, :].astype(jnp.float32)).astype(jnp.bfloat16)
+                else:
+                    partial[at, :] = rows.astype(jnp.bfloat16)
+                return carry
+
+            return body
+
+        lax.fori_loop(0, group // step, one(0, pl.ds(0, 256)), 0)
+        lax.fori_loop(group // step, group * 3 // 2 // step, one(1, pl.ds(256, 256)), 0)
+
+    for copy in seg_copies:
+        copy.wait()
+    pl.when(opposite)(wait_sibling)
+    for k in range(4):
+        project(4 * zh + k)
+
+    @pl.when(opposite)
+    def _():
+        forward_second()
+
+    gather_rows(early, False)
+
+    @pl.when(opposite)
+    def _():
+        forward_last()
+
+    pl.when(matched)(wait_sibling)
+    for k in range(4):
+        project(4 * (1 - zh) + k)
+    stores = [
+        pltpu.make_async_copy(src, dst, local_sem.at[6 + i])
+        for i, (src, dst) in enumerate(((x_all, x_hbm), (sorted_ref, sorted_hbm), (prob_ref, prob_hbm)))
+    ]
+    stores[0].start()
+    x_my[...] = x_all[p]
+
+    gather_rows(late, True)
     build_scatter(order_ref, 0, 0, group, scatter, 0)
     build_scatter(order_ref, 1, half, group // 2, scatter, group)
-    d_to_s.wait()
-    project(psd)
-
-    step = 512
-
-    def gather_rows(k, carry):
-        at = pl.ds(pl.multiple_of(k * step, step), step)
-        sorted_ref[at, :] = dot(gather[at, :], tok[:, 0:256]).astype(jnp.bfloat16)
-        return carry
-
-    def gather_rows_two(k, carry):
-        at = pl.ds(pl.multiple_of(k * step, step), step)
-        sorted_ref[at, :] = dot(gather[at, :], tok[:, 256:512]).astype(jnp.bfloat16)
-        return carry
-
-    lax.fori_loop(0, group // step, gather_rows, 0)
-    lax.fori_loop(group // step, group * 3 // 2 // step, gather_rows_two, 0)
 
     def attend(first_lanes):
         def one(i, carry):
@@ -435,8 +519,10 @@
 
         return one
 
-    lax.fori_loop(0, 16, attend(True), 0)
-    lax.fori_loop(16, 24, attend(False), 0)
+    lax.fori_loop(0, 16, attend(True), 0, unroll=UNROLL)
+    lax.fori_loop(16, 24, attend(False), 0, unroll=UNROLL)
+    stores[1].start()
+    stores[2].start()
 
     def place(position):
         at = pl.ds(pl.multiple_of(position * block, block), block)
@@ -452,25 +538,32 @@
     att_in[p] = place(p)
 
     stats_ref[...] = jnp.zeros_like(stats_ref)
-    for kind, (lane_sums, divisor) in enumerate(((ent_ref, 4.0 * block), (cnt_ref, 4.0 * block * 128))):
-        sums = jnp.sum(lane_sums[...], axis=1, keepdims=True) / divisor
-        for h, first, size, owner_row in ((h1, 0, 16, 16 * h1), (h2, 16, 8, 16 * h2 + 8 * c)):
-            at = pl.ds(pl.multiple_of(owner_row, 8), size)
-            owner_hot = jnp.where(matched, hot_ref[at, :], hot_in[at, :])
-            stats_ref[kind, pl.ds(h, 1), :] = jnp.sum(
-                sums[first : first + size] * owner_hot, axis=0, keepdims=True
-            )
+    owner_pad[...] = jnp.full_like(owner_pad, -1.0)
+    clusters = owners_ref.shape[2]
+    for h, first, size, skip in ((h1, 0, clusters, 0), (h2, clusters, clusters // 2, c)):
+        ids = jnp.where(matched, owners_ref[h], owners_in[h])
+        owner_pad[0:1, 0:clusters] = ids.astype(jnp.float32)
+        column = jnp.broadcast_to(owner_pad[0:1, :], (128, 128)).T
+        column = jnp.where(skip == 1, column[clusters // 2 : clusters // 2 + size], column[0:size])
+        owned = jnp.where(column == lanes((size, 128)).astype(jnp.float32), 1.0, 0.0)
+        for kind, (lane_sums, divisor) in enumerate(((ent_ref, 4.0 * block), (cnt_ref, 4.0 * block * 128))):
+            sums = jnp.sum(lane_sums[first : first + size, :], axis=1, keepdims=True) / divisor
+            stats_ref[kind, pl.ds(h, 1), :] = jnp.sum(sums * owned, axis=0, keepdims=True)
 
     @pl.when(matched)
     def _():
-        locals_[2].wait()
+        locals_[3].wait()
 
     @pl.when(jnp.logical_not(matched))
     def _():
-        swaps[2].wait()
+        swaps[3].wait()
 
     for copy in back_copies:
         copy.wait()
+    for copy in stores:
+        copy.wait()
+    for copy in own_to_s + x_to_s + z_to_s + d_to_s:
+        copy.wait_send()
     for pair in range(4):
         even, odd = att_in[pair], att_in[4 + pair]
         att_ref[:, 128 * pair : 128 * (pair + 1)] = join(half_roll(even), odd)
@@ -480,35 +573,46 @@
         att_ref[:, 512 + 128 * pair : 640 + 128 * pair] = join(low_half, half_roll(high_half))
 
 
-def forward_attention(tokens, cotangent, segments, orders, owner_hot, wq, wk, wv, biases):
+def forward_attention(
+    tokens, cotangent, segments, orders, owners, query_bias, value_bias, wq, wk, wv
+):
     block, width = tokens.shape
     group = 8 * block
     low, full = jnp.bfloat16, jnp.float32
     vmem = pl.BlockSpec(memory_space=pltpu.VMEM)
+    hbm = pl.BlockSpec(memory_space=pl.ANY)
     dma = pltpu.SemaphoreType.DMA
-    heads = orders.shape[0]
+    shape = jax.ShapeDtypeStruct
     rows = group * 3 // 2
     return pl.pallas_call(
         forward_kernel,
         out_shape=[
-            jax.ShapeDtypeStruct((block, width), low),
-            jax.ShapeDtypeStruct((8, block, width), low),
-            jax.ShapeDtypeStruct((block, width), low),
-            jax.ShapeDtypeStruct((rows, 256), low),
-            jax.ShapeDtypeStruct((rows, 128), full),
-            jax.ShapeDtypeStruct((width, 512), low),
-            jax.ShapeDtypeStruct((8, group), jnp.int32),
-            jax.ShapeDtypeStruct((2, 16, 128), full),
+            shape((block, width), low),
+            shape((block, width), low),
+            shape((block, width), low),
+            shape((width, 512), low),
+            shape((8, group), jnp.int32),
+            shape((2, 16, 128), full),
+            shape((8, block, width), low),
+            shape((rows, 256), low),
+            shape((rows, 128), full),
         ],
-        in_specs=[vmem] * 9,
-        out_specs=[vmem] * 8,
+        in_specs=[vmem] * 7 + [hbm] * 3,
+        out_specs=[vmem] * 6 + [hbm] * 3,
         scratch_shapes=[
-            pltpu.VMEM((heads, group), jnp.int32),
-            pltpu.VMEM(owner_hot.shape, full),
+            pltpu.VMEM((8, block, width), low),
+            pltpu.VMEM((rows, 256), low),
+            pltpu.VMEM((rows, 128), full),
+            pltpu.VMEM((3, 2, width, 128), low),
+            pltpu.VMEM(orders.shape, jnp.int32),
+            pltpu.VMEM(owners.shape, jnp.int32),
+            pltpu.VMEM((8, 128), full),
             pltpu.VMEM((8, block), jnp.int32),
             pltpu.VMEM((8, 8, block), jnp.int32),
+            pltpu.VMEM((8, width), full),
             pltpu.VMEM((8, 512), full),
             pltpu.VMEM((group, 512), low),
+            pltpu.VMEM((rows, 256), low),
             pltpu.VMEM((rows, group), low),
             pltpu.VMEM((group, rows), low),
             pltpu.VMEM((rows, 128), low),
@@ -516,20 +620,197 @@
             pltpu.VMEM((8, block, 128), low),
             pltpu.VMEM((24, 128), full),
             pltpu.VMEM((24, 128), full),
-            dma((8,)),
-            dma((8,)),
-            dma((8,)),
-            dma((8,)),
+            dma((10,)),
+            dma((10,)),
+            dma((14,)),
+            dma((14,)),
             dma((7,)),
             dma((7,)),
             dma((7,)),
             dma((7,)),
+            dma((9,)),
         ],
         compiler_params=pltpu.CompilerParams(
             collective_id=1, has_side_effects=True, vmem_limit_bytes=60 << 20
         ),
         name="forward_attention",
-    )(tokens, cotangent, segments, orders, owner_hot, wq, wk, wv, biases)
+    )(tokens, cotangent, segments, orders, owners, query_bias, value_bias, wq, wk, wv)
+
+
+def normalize(hidden):
+    centre = hidden - jnp.mean(hidden, axis=1, keepdims=True)
+    root_inverse = lax.rsqrt(jnp.mean(centre * centre, axis=1, keepdims=True) + EPSILON)
+    return centre * root_inverse, root_inverse
+
+
+def normalize_back(scaled, normed, root_inverse):
+    return root_inverse * (
+        scaled
+        - jnp.mean(scaled, axis=1, keepdims=True)
+        - normed * jnp.mean(scaled * normed, axis=1, keepdims=True)
+    )
+
+
+def mlp_kernel(
+    tile,
+    att_ref,
+    x_ref,
+    cot_ref,
+    out_bias_ref,
+    first_gain_ref,
+    first_shift_ref,
+    outer_bias_ref,
+    second_gain_ref,
+    second_shift_ref,
+    inner_bias_ref,
+    out_w_hbm,
+    inner_w_hbm,
+    outer_w_hbm,
+    output_ref,
+    delta_ref,
+    datt_ref,
+    low_ref,
+    dsecond_ref,
+    dbranch_ref,
+    vec_out,
+    act_hbm,
+    dinner_hbm,
+    act_ref,
+    dinner_ref,
+    bias_ref,
+    out_w,
+    inner_w,
+    outer_w,
+    slope,
+    total,
+    normed_ref,
+    first_ref,
+    load_sem,
+):
+    width = x_ref.shape[1]
+    inner_width = inner_w.shape[1]
+    tiles = inner_width // tile
+    parts = [slice(tile * t, tile * (t + 1)) for t in range(tiles)]
+    loads = [pltpu.make_async_copy(out_w_hbm, out_w, load_sem.at[0])]
+    for t, at in enumerate(parts):
+        loads.append(
+            pltpu.make_async_copy(inner_w_hbm.at[:, at], inner_w.at[:, at], load_sem.at[1 + 2 * t])
+        )
+        loads.append(pltpu.make_async_copy(outer_w_hbm.at[at], outer_w.at[at], load_sem.at[2 + 2 * t]))
+    for copy in loads:
+        copy.start()
+    stores = [
+        [
+            pltpu.make_async_copy(src.at[:, at], dst.at[:, at], load_sem.at[1 + 2 * tiles + 2 * t + i])
+            for i, (src, dst) in enumerate(((act_ref, act_hbm), (dinner_ref, dinner_hbm)))
+        ]
+        for t, at in enumerate(parts)
+    ]
+    bias_ref[0:1, :] = inner_bias_ref[...].astype(jnp.float32).reshape(1, inner_width)
+    out_bias, first_gain, first_shift, outer_bias, second_gain, second_shift = (
+        ref[...].astype(jnp.float32).reshape(1, width)
+        for ref in (
+            out_bias_ref,
+            first_gain_ref,
+            first_shift_ref,
+            outer_bias_ref,
+            second_gain_ref,
+            second_shift_ref,
+        )
+    )
+    loads[0].wait()
+    branch = dot(att_ref[...], out_w[...]) + out_bias
+    normed, root_one = normalize(x_ref[...].astype(jnp.float32) + branch)
+    first = normed * first_gain + first_shift
+    first_ref[...] = first
+    normed_ref[...] = normed
+    low_ref[...] = first.astype(jnp.bfloat16)
+    total[...] = jnp.zeros_like(total)
+
+    for t, at in enumerate(parts):
+        loads[1 + 2 * t].wait()
+        inner = dot(low_ref[...], inner_w[:, at]) + bias_ref[0:1, at]
+        cumulative = 0.5 + 0.5 * lax.erf(inner * (0.5**0.5))
+        density = jnp.exp(-0.5 * inner * inner) * 0.3989422804014327
+        slope[:, at] = cumulative + inner * density
+        act = (inner * cumulative).astype(jnp.bfloat16)
+        act_ref[:, at] = act
+        stores[t][0].start()
+        loads[2 + 2 * t].wait()
+        total[...] += dot(act, outer_w[at, :])
+    normed_two, root_two = normalize(first_ref[...] + total[...] + outer_bias)
+    output_ref[...] = (normed_two * second_gain + second_shift).astype(jnp.bfloat16)
+    upstream = cot_ref[...].astype(jnp.float32)
+    vec_out[4:5, :] = jnp.sum(upstream * normed_two, axis=0, keepdims=True)
+    vec_out[5:6, :] = jnp.sum(upstream, axis=0, keepdims=True)
+    delta_two = normalize_back(upstream * second_gain, normed_two, root_two)
+    low_two = delta_two.astype(jnp.bfloat16)
+    dsecond_ref[...] = low_two
+    vec_out[3:4, :] = jnp.sum(low_two.astype(jnp.float32), axis=0, keepdims=True)
+    total[...] = delta_two
+    for t, at in enumerate(parts):
+        dact = dot(dsecond_ref[...], outer_w[at, :], 1, 1)
+        dinner = (dact * slope[:, at]).astype(jnp.bfloat16)
+        dinner_ref[:, at] = dinner
+        stores[t][1].start()
+        bias_ref[0:1, at] = jnp.sum(dinner.astype(jnp.float32), axis=0, keepdims=True)
+        total[...] += dot(dinner, inner_w[:, at], 1, 1)
+    for i in range(inner_width // width):
+        vec_out[6 + i : 7 + i, :] = bias_ref[0:1, width * i : width * (i + 1)]
+    delta_first = total[...]
+    normed = normed_ref[...]
+    vec_out[1:2, :] = jnp.sum(delta_first * normed, axis=0, keepdims=True)
+    vec_out[2:3, :] = jnp.sum(delta_first, axis=0, keepdims=True)
+    delta_one = normalize_back(delta_first * first_gain, normed, root_one)
+    delta_ref[...] = delta_one
+    low_one = delta_one.astype(jnp.bfloat16)
+    dbranch_ref[...] = low_one
+    vec_out[0:1, :] = jnp.sum(low_one.astype(jnp.float32), axis=0, keepdims=True)
+    vec_out[10:16, :] = jnp.zeros((6, width), jnp.float32)
+    datt_ref[...] = dot(low_one, out_w[...], 1, 1).astype(jnp.bfloat16)
+    for pair in stores:
+        for copy in pair:
+            copy.wait()
+
+
+def mlp(att, x_my, cot_my, vectors, out_weight, inner_weight, outer_weight, tile):
+    block, width = x_my.shape
+    inner_width = inner_weight.shape[1]
+    low, full = jnp.bfloat16, jnp.float32
+    vmem = pl.BlockSpec(memory_space=pltpu.VMEM)
+    hbm = pl.BlockSpec(memory_space=pl.ANY)
+    shape = jax.ShapeDtypeStruct
+    return pl.pallas_call(
+        functools.partial(mlp_kernel, tile),
+        out_shape=[
+            shape((block, width), low),
+            shape((block, width), full),
+            shape((block, width), low),
+            shape((block, width), low),
+            shape((block, width), low),
+            shape((block, width), low),
+            shape((16, width), full),
+            shape((block, inner_width), low),
+            shape((block, inner_width), low),
+        ],
+        in_specs=[vmem] * 10 + [hbm] * 3,
+        out_specs=[vmem] * 7 + [hbm] * 2,
+        scratch_shapes=[
+            pltpu.VMEM((block, inner_width), low),
+            pltpu.VMEM((block, inner_width), low),
+            pltpu.VMEM((8, inner_width), full),
+            pltpu.VMEM(out_weight.shape, low),
+            pltpu.VMEM(inner_weight.shape, low),
+            pltpu.VMEM(outer_weight.shape, low),
+            pltpu.VMEM((block, inner_width), full),
+            pltpu.VMEM((block, width), full),
+            pltpu.VMEM((block, width), full),
+            pltpu.VMEM((block, width), full),
+            pltpu.SemaphoreType.DMA((1 + 4 * (inner_width // tile),)),
+        ],
+        compiler_params=pltpu.CompilerParams(vmem_limit_bytes=60 << 20),
+        name="mlp",
+    )(att, x_my, cot_my, *vectors, out_weight, inner_weight, outer_weight)
 
 
 def rows_of(start, q, size):
@@ -546,8 +827,8 @@
     lax.fori_loop(0, count, one, 0)
 
 
-def reduce_steps(parts, g_ref, f_ref, buffers, sems, own_sem):
-    own, core_in, a_one, b_one, ab_two, z_one, z_two = buffers
+def reduce_steps(parts, g_ref, f_ref, buffers, sems):
+    core_in, a_one, b_one, ab_two, z_one, z_two = buffers
     zh, zl, x, y, c = coordinates()
     q = g_ref.shape[3] // 8
     width = g_ref.shape[4] // parts
@@ -567,23 +848,14 @@
         )
         for k, cols in enumerate(columns)
     ]
-    mine = [
-        pltpu.make_async_copy(
-            g_ref.at[:, :, :, rows_of(4 * c, q, 4), cols], own.at[:, :, :, :, cols], own_sem.at[k]
-        )
-        for k, cols in enumerate(columns)
-    ]
-    for copy in mine:
-        copy.start()
     yield
     first, second, third, fourth, fifth, sixth = [], [], [], [], [], []
     for k, cols in enumerate(columns):
-        mine[k].wait()
         zero[k].wait()
         add_into(
             8,
             lambda i: core_in.at[i // 4, (i // 2) % 2, i % 2, :, cols],
-            lambda i: own.at[i // 4, (i // 2) % 2, i % 2, :, cols],
+            lambda i: g_ref.at[i // 4, (i // 2) % 2, i % 2, rows_of(4 * c, q, 4), cols],
         )
         first.append(
             (
@@ -654,22 +926,38 @@
 def backward_kernel(
     parts,
     datt_ref,
-    sorted_ref,
-    prob_ref,
     order_ref,
-    x_all,
-    wsel_ref,
-    delta_ref,
     out_my,
     stats_ref,
-    g_ref,
+    vec_ref,
+    att_hbm,
+    dbranch_hbm,
+    low_hbm,
+    dsecond_hbm,
+    act_hbm,
+    dinner_hbm,
+    sorted_hbm,
+    prob_hbm,
+    wsel_hbm,
+    x_hbm,
+    delta_hbm,
     out_home,
     grad_home,
     f_ref,
-    gq_ref,
-    gk_ref,
-    gv_ref,
+    w_all,
     stats_out,
+    att_ref,
+    dbranch_ref,
+    low_ref,
+    dsecond_ref,
+    act_ref,
+    dinner_ref,
+    sorted_ref,
+    prob_ref,
+    wsel_ref,
+    x_all,
+    delta_ref,
+    g_ref,
     datt_send,
     datt_in,
     gather,
@@ -689,10 +977,8 @@
     dw_y,
     dw_in,
     dw_all,
-    w_all,
     stats_buf,
     stats_in,
-    own,
     core_in,
     a_one,
     b_one,
@@ -711,7 +997,7 @@
     stats_rsem,
     red_ssem,
     red_rsem,
-    own_sem,
+    load_sem,
 ):
     zh, zl, x, y, c = coordinates()
     s = 4 * zh + 2 * zl + x
@@ -734,11 +1020,31 @@
     swap_peer = device(1 - zh, zl, x, y, 1 - c)
     over_y = device(zh, zl, x, 1 - y, c)
     across = [device(1 - zh, bits(zl, f // 2), bits(x, f % 2), y, c) for f in range(4)]
+    loads = [
+        pltpu.make_async_copy(src, dst, load_sem.at[i])
+        for i, (src, dst) in enumerate(
+            (
+                (att_hbm, att_ref),
+                (dbranch_hbm, dbranch_ref),
+                (low_hbm, low_ref),
+                (dsecond_hbm, dsecond_ref),
+                (act_hbm, act_ref),
+                (dinner_hbm, dinner_ref),
+                (sorted_hbm, sorted_ref),
+                (prob_hbm, prob_ref),
+                (wsel_hbm, wsel_ref),
+                (x_hbm, x_all),
+                (delta_hbm, delta_ref),
+            )
+        )
+    ]
+    for copy in loads:
+        copy.start()
     greet(peers + [swap_peer, over_y] + across)
 
     def home_copy(src, dst, index, start):
         away = remote(src, dst, swap_sems, index, swap_peer)
-        here = pltpu.make_async_copy(src, dst, swap_rsem.at[2 + index])
+        here = pltpu.make_async_copy(src, dst, swap_rsem.at[3 + index])
 
         @pl.when(matched)
         def _():
@@ -763,35 +1069,108 @@
         copy.start()
         datt_copies.append(copy)
     datt_in[p] = tile(c, j)
-    home_copy(out_my, out_home, 0, True)
-
+
+    def stats_steps():
+        stats_buf[0] = stats_ref[...]
+        stats_peers = (sibling, over_x, over_z, across[0], over_y)
+        for k, peer in enumerate(stats_peers):
+            copy = remote(stats_buf.at[k], stats_in.at[k], stats_sems, k, peer)
+            copy.start()
+            yield
+            copy.wait()
+            stats_buf[k + 1] = stats_buf[k] + stats_in[k]
+        stats_out[...] = stats_buf[len(stats_peers)]
+        yield
+
+    totals = stats_steps()
+    next(totals)
+
+    share = width // 8
+    q = g_ref.shape[3] // 8
+    top = 4 * q
+
+    def outer_grads():
+        def one(d, carry):
+            columns = pl.ds(pl.multiple_of(d * 4 * share, 128), 4 * share)
+            g_ref[d // 4, (d // 2) % 2, d % 2, top : top + 4 * share, :] = dot(
+                act_ref[:, columns], dsecond_ref[...], 0, 0
+            ).astype(jnp.bfloat16)
+            return carry
+
+        lax.fori_loop(0, 8, one, 0)
+
+    def inner_grads():
+        def one(i, carry):
+            z, n = i // 4, i % 4
+            rows = pl.ds(pl.multiple_of(z * 4 * share, 128), 4 * share)
+            columns = pl.ds(pl.multiple_of(n * width, 128), width)
+            grads = dot(low_ref[:, rows], dinner_ref[:, columns], 0, 0).astype(jnp.bfloat16)
+            for k in range(4):
+                at = pl.ds(pl.multiple_of(n * share, 16), share)
+                g_ref[z, k // 2, k % 2, at, :] = grads[share * k : share * (k + 1)]
+            return carry
+
+        lax.fori_loop(0, 8, one, 0)
+
+    for copy in loads[:6]:
+        copy.wait()
+    vectors = vec_ref[...].astype(jnp.bfloat16)
+    for z in range(2):
+        grads = dot(att_ref[:, 4 * share * z : 4 * share * (z + 1)], dbranch_ref[...], 0, 0).astype(jnp.bfloat16)
+        for k in range(4):
+            rows = grads[share * k : share * (k + 1)]
+            g_ref[z, k // 2, k % 2, 4 * share : 4 * share + share // 2, :] = rows[: share // 2]
+            g_ref[z, k // 2, k % 2, 4 * share + share // 2 : top, :] = jnp.zeros_like(vectors)
+            g_ref[z, k // 2, k % 2, top + 4 * share : top + 4 * share + share // 2, :] = rows[share // 2 :]
+            g_ref[z, k // 2, k % 2, top + 4 * share + share // 2 :, :] = vectors
+    pl.when(c == 0)(outer_grads)
+    pl.when(c == 1)(inner_grads)
     reduction = reduce_steps(
         parts,
         g_ref,
         f_ref,
-        (own, core_in, a_one, b_one, ab_two, z_one, z_two),
+        (core_in, a_one, b_one, ab_two, z_one, z_two),
         (red_ssem, red_rsem),
-        own_sem,
     )
     next(reduction)
+    pl.when(c == 0)(inner_grads)
+    pl.when(c == 1)(outer_grads)
 
     half = 1024 * c
-    build_gather(order_ref, 0, 0, group, gather.at[pl.ds(0, group)])
-    build_gather(order_ref, 1, half, group // 2, gather.at[pl.ds(group, group // 2)])
+    step = gather.shape[1]
+    chunks = group * 3 // 2 // step
+
+    def build(k):
+        head, start = (0, k * step) if k * step < group else (1, half + k * step - group)
+        build_gather(order_ref, head, start, step, gather.at[k % 2])
+
+    def take(k):
+        gathered[k * step : (k + 1) * step, :] = dot(
+            gather[k % 2], datt_in[...].reshape(group, 128)
+        ).astype(jnp.bfloat16)
+
+    next(totals)
+    build(0)
+    next(reduction)
+    build(1)
     for copy in datt_copies:
         copy.wait()
-    for k in range(parts):
-        next(reduction)
-
-    step = 512
-    arrived = datt_in[...].reshape(group, 128)
-
-    def gather_rows(k, carry):
-        at = pl.ds(pl.multiple_of(k * step, step), step)
-        gathered[at, :] = dot(gather[at, :], arrived).astype(jnp.bfloat16)
-        return carry
-
-    lax.fori_loop(0, group * 3 // 2 // step, gather_rows, 0)
+    take(0)
+    build(2)
+    take(1)
+    next(reduction)
+    build(3)
+    take(2)
+    build(4)
+    take(3)
+    next(totals)
+    next(reduction)
+    build(5)
+    take(4)
+    take(5)
+    for copy in loads[6:]:
+        copy.wait()
+    home_copy(out_my, out_home, 0, True)
 
     def attend_back(first_lanes):
         def one(i, carry):
@@ -815,10 +1194,13 @@
 
         return one
 
-    lax.fori_loop(0, 16, attend_back(True), 0)
-    for k in range(parts):
-        next(reduction)
-    lax.fori_loop(16, 24, attend_back(False), 0)
+    lax.fori_loop(0, 8, attend_back(True), 0, unroll=4)
+    next(totals)
+    next(reduction)
+    lax.fori_loop(8, 16, attend_back(True), 0, unroll=4)
+    next(totals)
+    lax.fori_loop(16, 24, attend_back(False), 0, unroll=4)
+    next(reduction)
 
     def place(position):
         token = lax.broadcasted_iota(jnp.int32, (128, 128), 0) + position * block
@@ -849,10 +1231,14 @@
 
     lax.fori_loop(0, 4, here, 0)
     upper, lower = pl.ds(0, block // 2), pl.ds(block // 2, block // 2)
-    a_copy = remote(total.at[:, 1 - x, upper], a_in, part_sems, 4, over_x)
-    b_copy = remote(total.at[1 - zl, :, lower], b_in, part_sems, 5, over_z)
-    a_copy.start()
-    b_copy.start()
+    pieces = [pl.ds(i * (width // 2), width // 2) for i in range(2)]
+    a_copies, b_copies = [], []
+    for i, cols in enumerate(pieces):
+        a_copies.append(remote(total.at[:, 1 - x, upper, cols], a_in.at[:, :, cols], part_sems, 4 + i, over_x))
+        b_copies.append(remote(total.at[1 - zl, :, lower, cols], b_in.at[:, :, cols], part_sems, 6 + i, over_z))
+        a_copies[i].start()
+        b_copies[i].start()
+    next(reduction)
 
     for k in range(width // 128):
         dw[128 * k : 128 * (k + 1), :] = dot(
@@ -861,7 +1247,6 @@
     bias_row = jnp.broadcast_to(
         jnp.sum(dqkv[...].astype(jnp.float32), axis=0, keepdims=True), (16, 512)
     ).astype(jnp.bfloat16)
-    share = width // 8
     for d in range(8):
         for h in range(2):
             dw_y[h, d, 0:share, :] = dw[share * d : share * (d + 1), 256 * h : 256 * (h + 1)]
@@ -869,15 +1254,16 @@
     over_y_copy = remote(dw_y.at[1 - y], dw_in, dw_sems, 0, over_y)
     over_y_copy.start()
 
-    a_copy.wait()
-    add_into(2, lambda i: a_in.at[i], lambda i: total.at[i, x, upper])
-    a_next = remote(a_in.at[1 - zl], a_two, part_sems, 6, over_z)
-    a_next.start()
-    b_copy.wait()
-    add_into(2, lambda i: b_in.at[i], lambda i: total.at[zl, i, lower])
-    b_next = remote(b_in.at[1 - x], b_two, part_sems, 7, over_x)
-    b_next.start()
-
+    a_next, b_next = [], []
+    for i, cols in enumerate(pieces):
+        a_copies[i].wait()
+        add_into(2, lambda k: a_in.at[k, :, cols], lambda k: total.at[k, x, upper, cols])
+        a_next.append(remote(a_in.at[1 - zl, :, cols], a_two.at[:, cols], part_sems, 8 + i, over_z))
+        a_next[i].start()
+        b_copies[i].wait()
+        add_into(2, lambda k: b_in.at[k, :, cols], lambda k: total.at[zl, k, lower, cols])
+        b_next.append(remote(b_in.at[1 - x, :, cols], b_two.at[:, cols], part_sems, 10 + i, over_x))
+        b_next[i].start()
     over_y_copy.wait()
     add_into(8, lambda i: dw_y.at[y, i], lambda i: dw_in.at[i])
     dw_copies = []
@@ -889,25 +1275,18 @@
         copy.start()
         dw_copies.append(copy)
     dw_all[s] = dw_y[y, s]
-
-    a_next.wait()
-    b_next.wait()
-    for start, first, second, index in ((0, a_two, a_in, zl), (block // 2, b_two, b_in, x)):
-        at = pl.ds(start, block // 2)
-        grad_my[at, :] = (
-            delta_ref[at, :] + first[...].astype(jnp.float32) + second[index].astype(jnp.float32)
-        ).astype(jnp.bfloat16)
-    home_copy(grad_my, grad_home, 1, True)
-
-    stats_buf[0] = stats_ref[...]
-    stats_peers = (sibling, over_x, over_z, across[0], over_y)
-    for k, peer in enumerate(stats_peers):
-        copy = remote(stats_buf.at[k], stats_in.at[k], stats_sems, k, peer)
-        copy.start()
-        copy.wait()
-        stats_buf[k + 1] = stats_buf[k] + stats_in[k]
-    stats_out[...] = stats_buf[len(stats_peers)]
-
+    for i, cols in enumerate(pieces):
+        a_next[i].wait()
+        b_next[i].wait()
+        for start, first, second, index in ((0, a_two, a_in, zl), (block // 2, b_two, b_in, x)):
+            at = pl.ds(start, block // 2)
+            grad_my[at, cols] = (
+                delta_ref[at, cols]
+                + first[:, cols].astype(jnp.float32)
+                + second[index, :, cols].astype(jnp.float32)
+            ).astype(jnp.bfloat16)
+        home_copy(grad_my.at[:, cols], grad_home.at[:, cols], 1 + i, True)
+    next(totals)
     for _ in range(parts):
         next(reduction)
 
@@ -919,59 +1298,76 @@
         )
     w_copy = remote(w_all.at[y, c], w_all.at[y, c], dw_sems, 8, over_y)
     w_copy.start()
-    next(reduction)
+    for _ in range(parts):
+        next(reduction)
     w_copy.wait()
     w_copy = remote(w_all.at[:, c], w_all.at[:, c], dw_sems, 9, sibling)
     w_copy.start()
     for _ in reduction:
         pass
     w_copy.wait()
-    for pair in range(4):
-        at = slice(128 * pair, 128 * pair + 128)
-        low, high = (w_all[0, core, pair].astype(jnp.float32) for core in range(2))
-        gq_ref[:, at] = join(low[:, 0:128], half_roll(high[:, 0:128]))
-        gk_ref[:, at] = join(low[:, 128:256], half_roll(high[:, 128:256]))
-        gv_ref[:, at] = join(half_roll(low[:, 0:128]), high[:, 0:128])
-    for pair in range(2):
-        at = slice(512 + 128 * pair, 640 + 128 * pair)
-        low, high = (
-            w_all[1, 0, 2 * pair + i].astype(jnp.float32) + w_all[1, 1, 2 * pair + i].astype(jnp.float32)
-            for i in range(2)
-        )
-        gq_ref[:, at] = join(half_roll(low[:, 0:128]), high[:, 0:128])
-        gk_ref[:, at] = join(half_roll(low[:, 128:256]), high[:, 128:256])
-        gv_ref[:, at] = join(low[:, 0:128], half_roll(high[:, 0:128]))
     home_copy(out_my, out_home, 0, False)
-    home_copy(grad_my, grad_home, 1, False)
-
-
-def backward_attention(datt, sorted_rows, prob, order, x_all, wsel, delta, output, stats, grads, parts):
+    for i, cols in enumerate(pieces):
+        home_copy(grad_my.at[:, cols], grad_home.at[:, cols], 1 + i, False)
+
+
+def backward_attention(
+    datt,
+    order,
+    output,
+    stats,
+    vectors,
+    att,
+    dbranch,
+    low_first,
+    dsecond,
+    act,
+    dinner,
+    sorted_rows,
+    prob,
+    wsel,
+    x_all,
+    delta,
+    parts,
+):
     block, width = datt.shape
+    inner_width = act.shape[1]
     group = 8 * block
     rows = group * 3 // 2
-    row_count = grads.shape[1]
-    q = row_count // 8
+    q = (9 * width // 8 + 32) // 8
     share = width // 8 + 16
     low, full = jnp.bfloat16, jnp.float32
     vmem = pl.BlockSpec(memory_space=pltpu.VMEM)
+    hbm = pl.BlockSpec(memory_space=pl.ANY)
     dma = pltpu.SemaphoreType.DMA
-    outs = pl.pallas_call(
+    shape = jax.ShapeDtypeStruct
+    return pl.pallas_call(
         functools.partial(backward_kernel, parts),
         out_shape=[
-            jax.ShapeDtypeStruct((block, width), low),
-            jax.ShapeDtypeStruct((block, width), low),
-            jax.ShapeDtypeStruct((2, 2, 2, q, width), low),
-            jax.ShapeDtypeStruct((share, width), full),
-            jax.ShapeDtypeStruct((share, width), full),
-            jax.ShapeDtypeStruct((share, width), full),
-            jax.ShapeDtypeStruct(stats.shape, full),
+            shape((block, width), low),
+            shape((block, width), low),
+            shape((2, 2, 2, q, width), low),
+            shape((2, 2, 4, share, 256), low),
+            shape(stats.shape, full),
         ],
-        in_specs=[vmem] * 9 + [pl.BlockSpec(memory_space=pl.ANY)],
-        out_specs=[vmem] * 7,
+        in_specs=[vmem] * 5 + [hbm] * 11,
+        out_specs=[vmem] * 5,
         scratch_shapes=[
+            pltpu.VMEM((block, width), low),
+            pltpu.VMEM((block, width), low),
+            pltpu.VMEM((block, width), low),
+            pltpu.VMEM((block, width), low),
+            pltpu.VMEM((block, inner_width), low),
+            pltpu.VMEM((block, inner_width), low),
+            pltpu.VMEM((rows, 256), low),
+            pltpu.VMEM((rows, 128), full),
+            pltpu.VMEM((width, 512), low),
+            pltpu.VMEM((group, width), low),
+            pltpu.VMEM((block, width), full),
+            pltpu.VMEM((2, 2, 2, 8 * q, width), low),
             pltpu.VMEM((8, block, 128), low),
             pltpu.VMEM((8, block, 128), low),
-            pltpu.VMEM((rows, group), low),
+            pltpu.VMEM((2, 512, group), low),
             pltpu.VMEM((rows, 128), low),
             pltpu.VMEM((rows, 256), low),
             pltpu.VMEM((block, rows), low),
@@ -988,10 +1384,8 @@
             pltpu.VMEM((2, 8, share, 256), low),
             pltpu.VMEM((8, share, 256), low),
             pltpu.VMEM((8, share, 256), low),
-            pltpu.VMEM((2, 2, 4, share, 256), low),
             pltpu.VMEM((6,) + stats.shape, full),
             pltpu.VMEM((5,) + stats.shape, full),
-            pltpu.VMEM((2, 2, 2, 4 * q, width), low),
             pltpu.VMEM((2, 2, 2, 4 * q, width), low),
             pltpu.VMEM((2, 2, 2 * q, width), low),
             pltpu.VMEM((2, 2, 2, q, width), low),
@@ -1000,36 +1394,154 @@
             pltpu.VMEM((2, q, width), low),
             dma((7,)),
             dma((7,)),
-            dma((8,)),
-            dma((8,)),
-            dma((4,)),
-            dma((4,)),
+            dma((12,)),
+            dma((12,)),
+            dma((6,)),
+            dma((6,)),
             dma((10,)),
             dma((10,)),
             dma((5,)),
             dma((5,)),
             dma((9, parts)),
             dma((9, parts)),
-            dma((parts,)),
+            dma((11,)),
         ],
         compiler_params=pltpu.CompilerParams(
-            collective_id=2, has_side_effects=True, vmem_limit_bytes=60 << 20
+            collective_id=2, has_side_effects=True, vmem_limit_bytes=62 << 20
         ),
         name="backward_attention",
     )(
         datt,
+        order,
+        output,
+        stats,
+        vectors,
+        att,
+        dbranch,
+        low_first,
+        dsecond,
+        act,
+        dinner,
         sorted_rows,
         prob,
-        order,
+        wsel,
         x_all.reshape(group, width),
-        wsel,
         delta,
-        output,
-        stats,
-        grads.reshape(2, 2, 2, row_count, width),
-    )
-    out_home, grad_home, reduced, gq, gk, gv, totals = outs
-    return out_home, grad_home, reduced.reshape(row_count, width), gq, gk, gv, totals
+    )
+
+
+def finish_kernel(
+    f_ref,
+    w_ref,
+    out_ref,
+    grad_ref,
+    stats_ref,
+    output,
+    grad_tokens,
+    gq_out,
+    gqb_out,
+    gk_out,
+    gv_out,
+    gvb_out,
+    go_out,
+    gob_out,
+    gfg_out,
+    gfs_out,
+    gi_out,
+    gib_out,
+    gu_out,
+    gub_out,
+    gsg_out,
+    gss_out,
+    stats_out,
+    gq_ref,
+    gv_ref,
+    vec_ref,
+):
+    s = lax.axis_index("seq")
+    output[0] = out_ref[...]
+    grad_tokens[0] = grad_ref[...]
+    stats_out[...] = stats_ref[:, : stats_out.shape[1], : stats_out.shape[2]]
+    share, width = gk_out.shape
+    top = f_ref.shape[0] // 2
+    full = jnp.float32
+    for n in range(gi_out.shape[1] // width):
+        gi_out[:, n * width : (n + 1) * width] = f_ref[n * share : (n + 1) * share, :].astype(full)
+    gu_out[...] = f_ref[top : top + 4 * share, :].astype(full)
+    part = share // 2
+    go_out[0:part, :] = f_ref[4 * share : 4 * share + part, :].astype(full)
+    go_out[part:, :] = f_ref[top + 4 * share : top + 4 * share + part, :].astype(full)
+    vec_ref[...] = f_ref[top + 4 * share + part :, :].astype(full)
+    for pair in range(4):
+        at = slice(128 * pair, 128 * pair + 128)
+        low, high = (w_ref[0, core, pair].astype(full) for core in range(2))
+        gq_ref[:, at] = join(low[:, 0:128], half_roll(high[:, 0:128]))
+        gk_out[:, at] = join(low[:, 128:256], half_roll(high[:, 128:256]))[:share]
+        gv_ref[:, at] = join(half_roll(low[:, 0:128]), high[:, 0:128])
+    for pair in range(2):
+        at = slice(512 + 128 * pair, 640 + 128 * pair)
+        low, high = (
+            w_ref[1, 0, 2 * pair + i].astype(full) + w_ref[1, 1, 2 * pair + i].astype(full) for i in range(2)
+        )
+        gq_ref[:, at] = join(half_roll(low[:, 0:128]), high[:, 0:128])
+        gk_out[:, at] = join(half_roll(low[:, 128:256]), high[:, 128:256])[:share]
+        gv_ref[:, at] = join(low[:, 0:128], half_roll(high[:, 0:128]))
+    gq_out[...] = gq_ref[:share, :]
+    gv_out[...] = gv_ref[:share, :]
+
+    def mine(rows):
+        return pltpu.roll(rows, width - share * s, 1)[:, :share]
+
+    short = mine(vec_ref[...])
+    for row, ref in enumerate((gob_out, gfg_out, gfs_out, gub_out, gsg_out, gss_out)):
+        ref[...] = short[row]
+    gqb_out[...] = mine(gq_ref[share : share + 8, :])[0]
+    gvb_out[...] = mine(gv_ref[share : share + 8, :])[0]
+    row = vec_ref[pl.ds(6 + s // 2, 1), :]
+    gib_out[...] = jnp.where(s % 2 == 1, row[:, 4 * share :], row[:, : 4 * share])[0]
+
+
+def finish(reduced, w_all, output, grad, totals, head_count, inner_width):
+    block, width = output.shape
+    row_count = 8 * reduced.shape[3]
+    share = width // 8
+    low, full = jnp.bfloat16, jnp.float32
+    vmem = pl.BlockSpec(memory_space=pltpu.VMEM)
+    shape = jax.ShapeDtypeStruct
+    square, vector = shape((share, width), full), shape((share,), full)
+    out_shape = [
+        shape((1, block, width), low),
+        shape((1, block, width), low),
+        square,
+        vector,
+        square,
+        square,
+        vector,
+        square,
+        vector,
+        vector,
+        vector,
+        shape((share, inner_width), full),
+        shape((inner_width // 8,), full),
+        shape((inner_width // 8, width), full),
+        vector,
+        vector,
+        vector,
+        shape((2, head_count, 8), full),
+    ]
+    return pl.pallas_call(
+        finish_kernel,
+        out_shape=out_shape,
+        in_specs=[vmem] * 5,
+        out_specs=[vmem] * len(out_shape),
+        scratch_shapes=[
+            pltpu.VMEM((share + 16, width), full),
+            pltpu.VMEM((share + 16, width), full),
+            pltpu.VMEM((16, width), full),
+        ],
+        compiler_params=pltpu.CompilerParams(vmem_limit_bytes=40 << 20),
+        name="finish",
+    )(reduced.reshape(row_count, width), w_all, output, grad, totals)
 
 
 def body(
@@ -1301,141 +1813,44 @@
     second_shift,
     cotangent,
 ):
-    own_index = lax.axis_index("seq")
-    position = 4 * lax.rem(lax.axis_index("rep"), 2) + lax.rem(own_index, 4)
-    head_count = orders.shape[1]
     model_width = tokens.shape[2]
-    seq_count = 8
-    owner_hot = (owners[0][:, :, None] == jnp.arange(128, dtype=jnp.int32)).astype(jnp.float32)
-    biases = jnp.concatenate(
-        [
-            jnp.broadcast_to(bias.astype(jnp.float32), (8, model_width))
-            for bias in (query_bias, jnp.zeros_like(query_bias), value_bias)
-        ]
-    )
-    attended_rows, x_all, my_cotangent, sorted_rows, prob, wsel, order, stats = forward_attention(
+    att, x_my, cot_my, wsel, order, stats, x_all, sorted_rows, prob = forward_attention(
         tokens[0],
         cotangent[0],
         segments,
-        orders[0],
-        owner_hot.reshape(-1, 128),
+        orders.transpose(1, 0, 2),
+        owners.transpose(1, 0, 2),
+        query_bias,
+        value_bias,
         query_weight,
         key_weight,
         value_weight,
-        biases,
-    )
-    flat_tokens = lax.dynamic_index_in_dim(x_all, position, 0, keepdims=False)
-    branch = jnp.dot(
-        attended_rows, out_weight, preferred_element_type=jnp.float32
-    ) + out_bias.astype(jnp.float32)
-    first_out, normed_one, root_one = norm_forward(
-        flat_tokens.astype(jnp.float32) + branch, first_gain, first_shift
-    )
-    first_low = first_out.astype(jnp.bfloat16)
-    inner_sum = jnp.dot(
-        first_low, inner_weight, preferred_element_type=jnp.float32
-    ) + inner_bias.astype(jnp.float32)
-    activated, gelu_pull = jax.vjp(exact_gelu, inner_sum)
-    activated_low = activated.astype(jnp.bfloat16)
-    second = jnp.dot(
-        activated_low, outer_weight, preferred_element_type=jnp.float32
-    ) + outer_bias.astype(jnp.float32)
-    result, normed_two, root_two = norm_forward(first_out + second, second_gain, second_shift)
-    output = result.astype(jnp.bfloat16)
-    upstream = my_cotangent.astype(jnp.float32)
-    gradient_second_gain = jnp.sum(upstream * normed_two, axis=0)
-    gradient_second_shift = jnp.sum(upstream, axis=0)
-    delta_two = norm_backward(upstream, normed_two, root_two, second_gain)
-    delta_second = delta_two.astype(jnp.bfloat16)
-    gradient_outer_bias = jnp.sum(delta_second.astype(jnp.float32), axis=0)
-    gradient_outer_weight = jnp.einsum(
-        "tf,td->fd", activated_low, delta_second, preferred_element_type=jnp.float32
-    )
-    delta_activated = jnp.einsum(
-        "td,fd->tf", delta_second, outer_weight, preferred_element_type=jnp.float32
-    )
-    delta_inner = gelu_pull(delta_activated)[0].astype(jnp.bfloat16)
-    gradient_inner_bias = jnp.sum(delta_inner.astype(jnp.float32), axis=0)
-    gradient_inner_weight = jnp.einsum(
-        "td,tf->df", first_low, delta_inner, preferred_element_type=jnp.float32
-    )
-    delta_first = delta_two + jnp.einsum(
-        "tf,df->td", delta_inner, inner_weight, preferred_element_type=jnp.float32
-    )
-    gradient_first_gain = jnp.sum(delta_first * normed_one, axis=0)
-    gradient_first_shift = jnp.sum(delta_first, axis=0)
-    delta_one = norm_backward(delta_first, normed_one, root_one, first_gain)
-    delta_branch = delta_one.astype(jnp.bfloat16)
-    gradient_out_bias = jnp.sum(delta_branch.astype(jnp.float32), axis=0)
-    gradient_out_weight = jnp.einsum(
-        "td,te->de", attended_rows, delta_branch, preferred_element_type=jnp.float32
-    )
-    delta_attended = jnp.einsum(
-        "te,de->td", delta_branch, out_weight, preferred_element_type=jnp.float32
-    ).astype(jnp.bfloat16)
-    weights_out = [
-        gradient_out_weight.reshape(8, -1, model_width),
-        gradient_inner_weight.reshape(8, model_width // 8, -1, model_width)
-        .transpose(0, 2, 1, 3)
-        .reshape(8, -1, model_width),
-        gradient_outer_weight.reshape(8, -1, model_width),
-    ]
-    vectors = jnp.concatenate(
-        [
-            vector.reshape(8, -1)
-            for vector in (
-                gradient_out_bias,
-                gradient_first_gain,
-                gradient_first_shift,
-                gradient_inner_bias,
-                gradient_outer_bias,
-                gradient_second_gain,
-                gradient_second_shift,
-            )
-        ],
-        axis=1,
-    )
-    used = sum(part.shape[1] for part in weights_out)
-    total_rows = -(-(used + 2) // 128) * 128
-    spare = (total_rows - used) * model_width - vectors.shape[1]
-    vectors = jnp.pad(vectors, ((0, 0), (0, spare))).reshape(8, -1, model_width)
-    grads = jnp.concatenate([part.astype(jnp.bfloat16) for part in weights_out + [vectors]], axis=1)
-    out_home, grad_home, summed, query_g, key_g, value_g, totals = backward_attention(
-        delta_attended, sorted_rows, prob, order, x_all, wsel, delta_one, output, stats, grads, 2
-    )
-    summed = summed.astype(jnp.float32)
-    share = model_width // 8
-    inner_count = inner_weight.shape[1] // model_width
-    marks = [0]
-    for part in weights_out:
-        marks.append(marks[-1] + part.shape[1])
-    out_g, inner_g, outer_g = (summed[marks[i] : marks[i + 1]] for i in range(3))
-    inner_g = inner_g.reshape(inner_count, share, model_width).transpose(1, 0, 2).reshape(share, -1)
-    flat = summed[marks[3] :].reshape(-1)
-    sizes = [share] * 3 + [share * inner_count] + [share] * 3
-    ends = [0]
-    for size in sizes:
-        ends.append(ends[-1] + size)
-    pick = [flat[ends[i] : ends[i + 1]] for i in range(7)]
-    return (
-        out_home[None],
-        grad_home[None],
-        query_g[:share],
-        lax.dynamic_slice_in_dim(query_g[share], share * own_index, share),
-        key_g[:share],
-        value_g[:share],
-        lax.dynamic_slice_in_dim(value_g[share], share * own_index, share),
-        out_g,
-        pick[0],
-        pick[1],
-        pick[2],
-        inner_g,
-        pick[3],
-        outer_g,
-        pick[4],
-        pick[5],
-        pick[6],
-        totals[:, :head_count, :seq_count],
+    )
+    vectors = (out_bias, first_gain, first_shift, outer_bias, second_gain, second_shift, inner_bias)
+    output, delta, datt, low_first, dsecond, dbranch, vector_grads, act, dinner = mlp(
+        att, x_my, cot_my, vectors, out_weight, inner_weight, outer_weight, 2 * model_width
+    )
+    output, grad, reduced, w_all, totals = backward_attention(
+        datt,
+        order,
+        output,
+        stats,
+        vector_grads,
+        att,
+        dbranch,
+        low_first,
+        dsecond,
+        act,
+        dinner,
+        sorted_rows,
+        prob,
+        wsel,
+        x_all,
+        delta,
+        3,
+    )
+    return tuple(
+        finish(reduced, w_all, output, grad, totals, orders.shape[1], inner_weight.shape[1])
     )
 
 

time: 277 us -> 201 us (0.73)
  matrix products: 30.8 us -> 0 us
  local copies, waits for them, and re-layouts: 30.3 us -> 5.9 us
  other arithmetic: 16.7 us -> 0 us
  Pallas kernels: 198 us -> 194 us
    dot_general x9 -> x0, matrix products: 30.8 us -> none  [the longest x1 9.91 us: square_body(): jnp.dot(first_low, inner_weight, preferred_element_type=jnp.float32)]
    convert_element_type x2 -> x0, local copies, waits for them, and re-layouts: 15.3 us -> none  [square_body(): part.astype(jnp.bfloat16)]
    concatenate x2 -> x0, other arithmetic: 10.2 us -> none  [the longest x1 9.54 us: square_body(): jnp.concatenate([part.astype(jnp.bfloat16) for part in weights_out + [vec...]
    slice x10 -> x0, local copies, waits for them, and re-layouts: 5.36 us -> none  [the longest x2 1.9 us: square_body(): out_g, inner_g, outer_g = (summed[marks[i]:marks[i + 1]] for i in range(3))]
    pallas_call x2 -> x4, Pallas kernels: 198 us -> 194 us  [the longest x1 118 us: backward_attention(): pl.pallas_call(functools.partial(backward_kernel, parts), out_shape=[shap...]
    reduce_sum x5 -> x0, other arithmetic: 3.42 us -> none  [the longest x1 1.15 us: square_body(): gradient_second_gain = jnp.sum(upstream * normed_two, axis=0)]
where the time goes in v3:
time: 201 us
  Pallas kernels  194 us (97%)
  local copies, waits for them, and re-layouts  5.9 us (3%)
    pallas_call x1, Pallas kernels, backward_attention(): pl.pallas_call(functools.partial(backward_kernel, parts), out_shape=[shap...  118 us
    pallas_call x1, Pallas kernels, forward_attention(): pl.pallas_call(forward_kernel, out_shape=[shape((block, width), low), sha...  60 us
    pallas_call x1, Pallas kernels, mlp(): pl.pallas_call(functools.partial(mlp_kernel, tile), out_shape=[shape((blo...  13.7 us
    unnamed x10, local copies, waits for them, and re-layouts  5.22 us

profile of v3, /device:TPU:0, one launch (start us, length us, event | category | flops | bytes accessed | tf_op | source)
XLA Modules:
  0.0 201.0 jit_solution(18429354588690829184)
XLA Ops:
  0.7 60.0 %forward_attention.1 = (bf16[256,768]{1,0:T(8,128)(2,1)}, bf16[256,768]{1,0:T(8,128)(2,1)}, bf16[256,768]{1,0:T(8,128)(2,1)}, bf16[768,512]{1,0:T(8,128)(2,1)}, ...) custom-call(bf16[256,768]{1,0:T(8,128)(2,1)} %bitcast.8, ...), custom_call_target="tpu_custom_call" | custom-call | tf_op jit(solution)/shard_map/forward_attention/pallas_call | solution.py:587
  60.7 13.7 %mlp.1 = (bf16[256,768]{1,0:T(8,128)(2,1)}, f32[256,768]{1,0:T(8,128)}, bf16[256,768]{1,0:T(8,128)(2,1)}, bf16[256,768]{1,0:T(8,128)(2,1)}, bf16[256,768]{1,0:T(...) custom-call(bf16[256,768]{1,0:T(8,128)(2,1)} %get-tuple-element.41.a, ...), custom_call_target="tpu_custom_call" | custom-call | tf_op jit(solution)/shard_map/mlp/pallas_call | solution.py:783
  74.4 118.3 %backward_attention.1 = (bf16[256,768]{1,0:T(8,128)(2,1)}, bf16[256,768]{1,0:T(8,128)(2,1)}, bf16[2,2,2,112,768]{4,3,2,1,0:T(8,128)(2,1)}, bf16[2,2,4,112,256]{4,3,2,1,0:T(8,128)(2,1)}, f32[2,16,128]{2,1,0:T(8,128)}) custom-call(bf16[256,768]{1,0:T(8,128)(2,1)} %get-tuple-element.44.datt_ref, s32[8,2048]{1,0:T(8,128)} %get-tuple-element.45.order_ref, ...), custom_call_target="tpu_custom_call" | custom-call | tf_op jit(solution)/shard_map/backward_attention/pallas_call | solution.py:1344
  192.8 0.0 copy-start
  192.8 1.3 copy-done
  194.1 0.0 copy-start.1
  194.1 1.2 copy-done.1
  195.3 0.0 copy-start.2
  195.3 1.0 copy-done.2
  196.3 0.0 copy-start.3
  196.3 1.0 copy-done.3
  197.3 0.0 copy-start.4
  197.3 0.7 copy-done.4
  198.0 2.3 %finish.1 = (bf16[1,256,768]{2,1,0:T(8,128)(2,1)}, bf16[1,256,768]{2,1,0:T(8,128)(2,1)}, f32[96,768]{1,0:T(8,128)}, f32[96]{0:T(128)}, f32[96,768]{1,0:T(8,128)}...) custom-call(bf16[896,768]{1,0:T(8,128)(2,1)S(1)} %bitcast.6, ...), custom_call_target="tpu_custom_call" | custom-call | tf_op jit(solution)/shard_map/finish/pallas_call | solution.py:1532
  200.3 0.7 copy.38
Async XLA Ops:
  192.8 1.3 copy-start
  194.1 1.2 copy-start.1
  195.3 1.0 copy-start.2
  196.3 1.0 copy-start.3
  197.3 0.7 copy-start.4
